TPU v7x, 32 devices: a whole 2x2x4 slice. The times are simulated.
32 devices in a mesh: groups: 2 (over x), comm: 16 (over z, y, core).
Axes of the slice: x: 2, y: 2, z: 4, core: 2. Of those that a mesh axis runs over, the one named last changes fastest.
Arguments:
- cost: float32 [512, 12, 256], P(('groups', 'comm')), parts along dimension 0, may hold values from 0.2 to 1.8
- demand: float32 [512, 12, 32], P(('groups', 'comm')), parts along dimension 0, may hold values from 0.2 to 3
- capacity: float32 [32, 12, 256], P(('groups', 'comm')), parts along dimension 0, may hold values from 4.8 to 24
- tiles: bfloat16 [1536, 256, 256], P(('groups', 'comm')), parts along dimension 0, may hold values from 0 to 1, as said below
- tile_row: int32 [1536], P(('groups', 'comm')), parts along dimension 0, may hold values from 0 to 15
- tile_col: int32 [1536], P(('groups', 'comm')), parts along dimension 0, may hold values from 0 to 15
- tile_count: int32 [32], P(('groups', 'comm')), parts along dimension 0, may hold values from 1 to 48, as said below
Outputs:
- flows: float32 [512, 12, 256], P(('groups', 'comm')), parts along dimension 0
- link_duals: float32 [32, 12, 256], P(('groups', 'comm')), parts along dimension 0
- demand_duals: float32 [512, 12, 32], P(('groups', 'comm')), parts along dimension 0
There are 2 independent parts, one for each index of `groups`. A program takes and returns all parts, laid end to end along the dimension named above; each array names one. Nothing has to cross between parts.
Inputs may be any that keep to these rules, and one draw needn't show every extreme that they name: Slots 0 to tile_count - 1 of a device hold its tiles, the rest are ignored; some device has all 48 slots live. `tiles`: every row of a tile has one or two ones.
All inputs are finite; a program needn't handle non-finite values.
Results may differ from a plain program's by a relative error of at most 0.0028.
Values may be sent and summed in bfloat16 or wider, within the bound.
No kernel may reach another device: no remote copies, remote signals or barrier semaphores. Data moves between devices by JAX's collectives and lax.ppermute only.
A program may use at most 64 MiB of HBM per device.

v0:
```python
import jax
import jax.numpy as jnp
from jax import lax
from jax.sharding import PartitionSpec as P

INTERVALS = 12
PATHS_PER = 8
TILE = 256
ITERS = 3


def per_device(cost, demand, capacity, tiles, tile_row, tile_col, tile_count):
    slots_dev = tiles.shape[0]
    path_blocks = cost.shape[0]
    owned_blocks = capacity.shape[0]
    link_blocks = owned_blocks * lax.axis_size("comm")
    live = (jnp.arange(slots_dev, dtype=jnp.int32) < tile_count[0]).astype(jnp.float32)
    link_onehot = (jnp.arange(link_blocks, dtype=jnp.int32)[:, None] == tile_col[None, :]).astype(
        jnp.float32
    )
    path_onehot = (jnp.arange(path_blocks, dtype=jnp.int32)[:, None] == tile_row[None, :]).astype(
        jnp.float32
    )
    flows = jnp.zeros(cost.shape, jnp.float32)
    demand_duals = jnp.zeros(demand.shape, jnp.float32)
    link_duals = jnp.zeros(capacity.shape, jnp.float32)
    for sweep in range(ITERS):
        gradient = cost - 1.0 + jnp.repeat(demand_duals, PATHS_PER, axis=2)
        if sweep > 0:
            rounded_full = lax.all_gather(
                link_duals.astype(jnp.bfloat16), "comm", axis=0, tiled=True
            )
            picked = jnp.take(rounded_full, tile_col, axis=0)
            back = jnp.einsum("ntj,nij->nti", picked, tiles, preferred_element_type=jnp.float32)
            back = back * live[:, None, None]
            gradient = gradient + jnp.einsum(
                "pn,nti->pti", path_onehot, back, precision=lax.Precision.HIGHEST
            )
        new_flows = jnp.maximum(0.0, flows - 0.5 * gradient)
        extrapolated = (2.0 * new_flows - flows).astype(jnp.bfloat16)
        contributions_picked = jnp.take(extrapolated, tile_row, axis=0)
        contrib = jnp.einsum(
            "nti,nij->ntj", contributions_picked, tiles, preferred_element_type=jnp.float32
        )
        contrib = contrib * live[:, None, None]
        partial_loads = jnp.einsum(
            "bn,ntj->btj", link_onehot, contrib, precision=lax.Precision.HIGHEST
        )
        loads = lax.psum_scatter(partial_loads, "comm", scatter_dimension=0, tiled=True)
        link_duals = jnp.maximum(0.0, link_duals + 0.08 * (loads - capacity))
        per_commodity = (
            extrapolated.astype(jnp.float32)
            .reshape(path_blocks, INTERVALS, TILE // PATHS_PER, PATHS_PER)
            .sum(axis=3)
        )
        demand_duals = jnp.maximum(0.0, demand_duals + 0.2 * (per_commodity - demand))
        flows = new_flows
    return (flows, link_duals, demand_duals)


def solution(mesh):
    in_specs = (
        P(("groups", "comm"), None, None),
        P(("groups", "comm"), None, None),
        P(("groups", "comm"), None, None),
        P(("groups", "comm"), None, None),
        P(("groups", "comm")),
        P(("groups", "comm")),
        P(("groups", "comm")),
    )
    out_specs = (
        P(("groups", "comm"), None, None),
        P(("groups", "comm"), None, None),
        P(("groups", "comm"), None, None),
    )
    return jax.shard_map(
        per_device, mesh=mesh, in_specs=in_specs, out_specs=out_specs, check_vma=False
    )
```

profile of v0, /device:TPU:0, one launch (start us, length us, event | category | flops | bytes accessed | tf_op | source)
XLA Modules:
  0.0 358.7 jit_solution(4825777198551664793)
XLA Ops:
  7.9 0.7 compare_select_fusion.1
  8.6 0.7 compare_and_fusion.1
  9.2 1.0 multiply_convert_fusion
  10.2 0.6 gather_fusion
  10.8 3.8 %convolution_multiply_fusion.4 = f32[48,12,256]{2,1,0:T(8,128)S(1)} fusion(bf16[48,256,256]{2,1,0:T(8,128)(2,1)} %param.12, bf16[48,12,256]{2,1,0:T(8,128)(2,1)S(1)} %gather_fusion, f32[48]{0:T(128)S(1)} %get-tuple-element.14, pred[48]{0:T(512)(128)(4,1)S(1)} %get-tuple-element.13), kind=kOutput, calls=%fused_computation.12 | convolution fusion | flops 75792384 | bytes 7176432 | tf_op jit(solution)/shard_map/nti,nij->ntj/dot_general | solution.py:42
  14.6 1.3 fusion.12
  16.5 0.5 bitcast_reduce_fusion.2
  17.1 0.4 copy.24
  17.6 0.7 dynamic-slice
  18.3 90.3 %all-reduce.7.cloned.1.call-done = f32[16,12,256]{2,0,1:T(8,128)} async-done(((f32[16,12,256]{2,0,1:T(8,128)}), f32[16,12,256]{2,0,1:T(8,128)}) %all-reduce.7.cloned.1.call-update) | async-done | bytes 196624
  108.5 1.6 fusion.54
  110.1 19.8 %all_gather.6 = bf16[16,12,256]{2,1,0:T(8,128)(2,1)S(1)} all-gather(bf16[1,12,256]{2,1,0:T(8,128)(2,1)S(1)} %copy.27), channel_id=1, replica_groups=mesh['groups'=2,'comm'=16] {'comm'}, dimensions={0}, use_global_device_ids=true | all-gather | bytes 104448 | tf_op jit(solution)/shard_map/all_gather | solution.py:30
  129.9 0.6 gather_fusion.1
  130.5 4.5 %convolution_multiply_fusion.3 = f32[48,12,256]{2,1,0:T(8,128)S(1)} fusion(bf16[48,256,256]{2,1,0:T(8,128)(2,1)} %param.12, bf16[48,12,256]{2,1,0:T(8,128)(2,1)S(1)} %gather_fusion.1, f32[48]{0:T(128)S(1)} %get-tuple-element.14, pred[48]{0:T(512)(128)(4,1)S(1)} %compare_and_fusion), kind=kOutput, calls=%fused_computation.11 | convolution fusion | flops 75792384 | bytes 7176432 | tf_op jit(solution)/shard_map/ntj,nij->nti/dot_general | solution.py:34
  135.1 0.7 subtract_convert_fusion.1
  136.0 0.6 gather_fusion.2
  136.6 3.8 %convolution_multiply_fusion.2 = f32[48,12,256]{2,1,0:T(8,128)S(1)} fusion(bf16[48,256,256]{2,1,0:T(8,128)(2,1)} %param.12, bf16[48,12,256]{2,1,0:T(8,128)(2,1)S(1)} %gather_fusion.2, f32[48]{0:T(128)S(1)} %get-tuple-element.14, pred[48]{0:T(512)(128)(4,1)S(1)} %get-tuple-element.13), kind=kOutput, calls=%fused_computation.10 | convolution fusion | flops 75792384 | bytes 7176432 | tf_op jit(solution)/shard_map/nti,nij->ntj/dot_general | solution.py:42
  140.4 1.3 fusion.9
  141.8 0.5 bitcast_reduce_fusion.1
  142.9 85.9 %all-reduce.9.cloned.1.call-done = f32[16,12,256]{2,0,1:T(8,128)} async-done(((f32[16,12,256]{2,0,1:T(8,128)}), f32[16,12,256]{2,0,1:T(8,128)}) %all-reduce.9.cloned.1.call-update) | async-done | bytes 196624
  228.8 1.7 fusion.55
  230.5 19.9 %all_gather.7 = bf16[16,12,256]{2,1,0:T(8,128)(2,1)S(1)} all-gather(bf16[1,12,256]{2,1,0:T(8,128)(2,1)S(1)} %copy.34), channel_id=1, replica_groups=mesh['groups'=2,'comm'=16] {'comm'}, dimensions={0}, use_global_device_ids=true | all-gather | bytes 104448 | tf_op jit(solution)/shard_map/all_gather | solution.py:30
  250.4 0.6 gather_fusion.3
  251.0 4.5 %convolution_multiply_fusion.1 = f32[48,12,256]{2,1,0:T(8,128)S(1)} fusion(bf16[48,256,256]{2,1,0:T(8,128)(2,1)} %param.12, bf16[48,12,256]{2,1,0:T(8,128)(2,1)S(1)} %gather_fusion.3, f32[48]{0:T(128)S(1)} %get-tuple-element.14, pred[48]{0:T(512)(128)(4,1)S(1)} %compare_and_fusion), kind=kOutput, calls=%fused_computation.9 | convolution fusion | flops 75792384 | bytes 7176432 | tf_op jit(solution)/shard_map/ntj,nij->nti/dot_general | solution.py:34
  255.6 1.4 subtract_convert_fusion
  257.2 0.6 gather_fusion.4
  257.8 3.8 %convolution_multiply_fusion = f32[48,12,256]{2,1,0:T(8,128)S(1)} fusion(bf16[48,256,256]{2,1,0:T(8,128)(2,1)} %param.12, bf16[48,12,256]{2,1,0:T(8,128)(2,1)S(1)} %gather_fusion.4, f32[48]{0:T(128)S(1)} %get-tuple-element.14, pred[48]{0:T(512)(128)(4,1)S(1)} %get-tuple-element.13), kind=kOutput, calls=%fused_computation.8 | convolution fusion | flops 75792384 | bytes 7176432 | tf_op jit(solution)/shard_map/nti,nij->ntj/dot_general | solution.py:42
  261.6 1.3 fusion.6
  262.9 0.5 bitcast_reduce_fusion
  263.5 0.8 copy.40
  264.3 85.7 %all-reduce.11.cloned.1.call-done = f32[16,12,256]{2,0,1:T(8,128)} async-done(((f32[16,12,256]{2,0,1:T(8,128)}), f32[16,12,256]{2,0,1:T(8,128)}) %all-reduce.11.cloned.1.call-update) | async-done | bytes 196624
  350.0 2.2 fusion.36
  (37 shorter events, 2.1 us)
Async XLA Ops:
  7.2 7.4 %copy-start.4 = (s32[48]{0:T(128)S(1)}, s32[48]{0:T(128)}, u32[]{:S(2)}) copy-start(s32[48]{0:T(128)} %param.14) | copy-start | bytes 580
  7.2 9.2 %copy-start.2 = (f32[16,12,32]{2,0,1:T(8,128)S(1)}, f32[16,12,32]{2,0,1:T(8,128)}, u32[]{:S(2)}) copy-start(f32[16,12,32]{2,0,1:T(8,128)} %param.10) | copy-start | bytes 73732
  7.2 101.3 %all-reduce.7.cloned.1.call-start = ((), (), s32[]{:S(2)}) async-start(), calls=%async_computation | async-start | bytes 393216
  14.6 3.0 copy-start.5
  14.6 93.9 %copy-start.1 = (f32[1,12,256]{2,0,1:T(1,128)S(1)}, f32[1,12,256]{2,0,1:T(1,128)}, u32[]{:S(2)}) copy-start(f32[1,12,256]{2,0,1:T(1,128)} %param.11) | copy-start | bytes 36868
  16.0 212.8 %all-reduce.9.cloned.1.call-start = ((), (), s32[]{:S(2)}) async-start(), calls=%async_computation.1 | async-start | bytes 393216
  17.0 118.1 %copy-start = (f32[16,12,256]{2,0,1:T(8,128)S(1)}, f32[16,12,256]{2,0,1:T(8,128)}, u32[]{:S(2)}) copy-start(f32[16,12,256]{2,0,1:T(8,128)} %param.9) | copy-start | bytes 589828
  17.0 118.1 %copy-start.3 = (s32[48]{0:T(128)S(1)}, s32[48]{0:T(128)}, u32[]{:S(2)}) copy-start(s32[48]{0:T(128)} %param.13) | copy-start | bytes 580
  141.8 208.2 %all-reduce.11.cloned.1.call-start = ((), (), s32[]{:S(2)}) async-start(), calls=%async_computation.2 | async-start | bytes 393216
Sparse Core Ops, SparseCore 0:
  16.1 92.3 all-reduce.6
  141.9 86.8 all-reduce.8
  263.1 86.8 all-reduce.10
where the time goes:
time: 359 us
  waiting for transfers between devices  262 us (73%)
  blocking collectives  39.7 us (11%)
  matrix products  26.4 us (7%)
  between operations  14.7 us (4%)
  other arithmetic  9.43 us (3%)
  local copies, waits for them, and re-layouts  6.49 us (2%)
    unnamed x6, waiting for transfers between devices  262 us
    all_gather x2, blocking collectives, per_device(): lax.all_gather(link_duals.astype(jnp.bfloat16), 'comm', axis=0, tiled=True)  39.7 us
    dot_general x3, matrix products, per_device(): jnp.einsum('nti,nij->ntj', contributions_picked, tiles, preferred_element...  11.3 us
    dot_general x2, matrix products, per_device(): jnp.einsum('ntj,nij->nti', picked, tiles, preferred_element_type=jnp.floa...  9.08 us
  transfers between devices with their start and end apart: 3, of which 3 were waited for; matrix products, arithmetic and copies ran while one was open for 1% of the time, Pallas kernels for 0%

commit v1 on v0

v1 whole, which is shorter than its diff:
```python
import functools

import jax
import jax.numpy as jnp
from jax import lax
from jax.experimental import pallas as pl
from jax.experimental.pallas import tpu as pltpu
from jax.sharding import PartitionSpec as P

PATHS_PER = 8
ITERS = 3
CHUNKS = 6
VMEM_LIMIT = 40 * 2**20
F32 = jnp.float32
BF16 = jnp.bfloat16


def spec(space):
    return pl.BlockSpec(memory_space=space)


def chunk_copies(tiles_hbm, tiles_v, sems):
    size = tiles_v.shape[0] // CHUNKS
    return [
        pltpu.make_async_copy(
            tiles_hbm.at[pl.ds(k * size, size)], tiles_v.at[pl.ds(k * size, size)], sems.at[k]
        )
        for k in range(CHUNKS)
    ]


def forward(row_ref, colpos_ref, tiles_v, ex, accs, copies=()):
    slots = tiles_v.shape[0]
    for acc in accs:
        acc[...] = jnp.zeros_like(acc)
    for n in range(slots):
        if copies and n % (slots // CHUNKS) == 0:
            copies[n // (slots // CHUNKS)].wait()
        acc = accs[n % len(accs)]
        acc[colpos_ref[n]] += jnp.dot(
            ex[row_ref[n]], tiles_v[n], preferred_element_type=F32
        )


def emit(me_ref, cap_ref, accs, keep_ref, send_ref):
    half = keep_ref.shape[0]
    me = me_ref[0]
    core = lax.rem(me, 2)
    own = core * half + me // 2
    accs[0][own] -= cap_ref[0]
    mine = pl.ds(core * half, half)
    theirs = pl.ds((1 - core) * half, half)
    keep_ref[...] = sum(acc[mine] for acc in accs)
    send_ref[...] = sum(acc[theirs] for acc in accs)


def first_kernel(
    me_ref, row_ref, colpos_ref, cost_ref, cap_ref, tiles_hbm, keep_ref, send_ref,
    tiles_v, ex, acc0, acc1, sems,
):
    copies = chunk_copies(tiles_hbm, tiles_v, sems)
    for copy in copies:
        copy.start()
    flows = jnp.maximum(0.0, -0.5 * (cost_ref[...] - 1.0))
    ex[...] = (2.0 * flows).astype(BF16)
    forward(row_ref, colpos_ref, tiles_v, ex, (acc0, acc1), copies)
    emit(me_ref, cap_ref, (acc0, acc1), keep_ref, send_ref)


def next_kernel(
    me_ref, row_ref, rowpos_ref, col_ref, colpos_ref, base_ref, flows_ref, own_ref, other_ref,
    cap_ref, tiles_hbm, keep_ref, send_ref, new_ref,
    tiles_v, ex, acc0, acc1, grad0, grad1, duals, sems,
):
    copies = chunk_copies(tiles_hbm, tiles_v, sems)
    for copy in copies:
        copy.start()
    half = own_ref.shape[0]
    core = lax.rem(me_ref[0], 2)
    duals[pl.ds(core * half, half)] = own_ref[...]
    duals[pl.ds((1 - core) * half, half)] = other_ref[...]
    grads = (grad0, grad1)
    for grad in grads:
        grad[...] = jnp.zeros_like(grad)
    slots = tiles_v.shape[0]
    for n in range(slots):
        if n % (slots // CHUNKS) == 0:
            copies[n // (slots // CHUNKS)].wait()
        grad = grads[n % 2]
        grad[rowpos_ref[n]] += lax.dot_general(
            duals[col_ref[n]], tiles_v[n], (((1,), (1,)), ((), ())), preferred_element_type=F32
        )
    blocks = base_ref.shape[0]
    new = jnp.maximum(
        0.0, base_ref[...] - 0.5 * (grad0[pl.ds(0, blocks)] + grad1[pl.ds(0, blocks)])
    )
    new_ref[...] = new
    ex[...] = (2.0 * new - flows_ref[...]).astype(BF16)
    forward(row_ref, colpos_ref, tiles_v, ex, (acc0, acc1))
    emit(me_ref, cap_ref, (acc0, acc1), keep_ref, send_ref)


def commodity_matrix(paths):
    path = lax.broadcasted_iota(jnp.int32, (paths, paths // PATHS_PER), 0)
    comm = lax.broadcasted_iota(jnp.int32, (paths, paths // PATHS_PER), 1)
    low = comm * PATHS_PER
    return ((path >= low) & (path < low + PATHS_PER)).astype(F32)


def demand_kernel(last, cost_ref, demand_ref, dd_ref, old_ref, new_ref, out_ref, *base):
    blocks, _, paths = cost_ref.shape
    which = commodity_matrix(paths)
    which16 = which.astype(BF16)
    for i in range(blocks):
        new = new_ref[i]
        ex = (2.0 * new - old_ref[i]).astype(BF16)
        per = jnp.dot(ex, which16, preferred_element_type=F32)
        dd = jnp.maximum(0.0, dd_ref[i] + 0.2 * (per - demand_ref[i]))
        out_ref[i] = dd
        if not last:
            spread = lax.dot_general(
                dd, which, (((1,), (1,)), ((), ())),
                precision=lax.Precision.HIGHEST, preferred_element_type=F32,
            )
            base[0][i] = new - 0.5 * (cost_ref[i] - 1.0 + spread)


def per_device(cost, demand, capacity, tiles, tile_row, tile_col, tile_count):
    slots, paths, links = tiles.shape
    blocks, intervals, _ = cost.shape
    n_dev = lax.axis_size("comm")
    link_blocks = n_dev * capacity.shape[0]
    half = link_blocks // 2
    me = lax.axis_index("comm")
    me_arr = me.astype(jnp.int32).reshape(1)
    live = jnp.arange(slots, dtype=jnp.int32) < tile_count[0]
    place = (tile_col % 2) * half + tile_col // 2
    colpos = jnp.where(live, place, link_blocks)
    rowpos = jnp.where(live, tile_row, blocks)

    V, S, A = pltpu.VMEM, pltpu.SMEM, pl.ANY
    params = pltpu.CompilerParams(vmem_limit_bytes=VMEM_LIMIT)
    halves = jax.ShapeDtypeStruct((half, intervals, links), F32)
    per_path = jax.ShapeDtypeStruct(cost.shape, F32)
    per_comm = jax.ShapeDtypeStruct(demand.shape, F32)
    passes = 2 * slots * 16 * paths * links
    tile_scratch = [V(tiles.shape, BF16), V(cost.shape, BF16)]
    acc_scratch = [V((link_blocks + 1, intervals, links), F32)] * 2
    grad_scratch = [V((blocks + 1, intervals, paths), F32)] * 2

    first = pl.pallas_call(
        first_kernel,
        out_shape=(halves, halves),
        in_specs=[spec(S)] * 3 + [spec(V)] * 2 + [spec(A)],
        out_specs=(spec(V), spec(V)),
        scratch_shapes=tile_scratch + acc_scratch + [pltpu.SemaphoreType.DMA((CHUNKS,))],
        compiler_params=params,
        cost_estimate=pl.CostEstimate(
            flops=passes, bytes_accessed=tiles.size * 2, transcendentals=0
        ),
        name="first_forward",
    )
    following = pl.pallas_call(
        next_kernel,
        out_shape=(halves, halves, per_path),
        in_specs=[spec(S)] * 5 + [spec(V)] * 5 + [spec(A)],
        out_specs=(spec(V),) * 3,
        scratch_shapes=tile_scratch
        + acc_scratch
        + grad_scratch
        + [V((link_blocks, intervals, links), BF16), pltpu.SemaphoreType.DMA((CHUNKS,))],
        compiler_params=params,
        cost_estimate=pl.CostEstimate(
            flops=2 * passes, bytes_accessed=tiles.size * 2, transcendentals=0
        ),
        name="adjoint_forward",
    )

    def demand_step(last, *args):
        return pl.pallas_call(
            functools.partial(demand_kernel, last),
            out_shape=(per_comm,) if last else (per_comm, per_path),
            in_specs=[spec(V)] * 5,
            out_specs=(spec(V),) if last else (spec(V),) * 2,
            compiler_params=params,
            cost_estimate=pl.CostEstimate(
                flops=10**6, bytes_accessed=4 * cost.size * 4, transcendentals=0
            ),
            name="demand_step",
        )(*args)

    def swap(x, bit):
        return lax.ppermute(x, "comm", [(i, i ^ bit) for i in range(n_dev)])

    scale = 1.0 / n_dev

    def sum_all(total):
        bit = 2
        while bit < n_dev:
            sent = (total * scale).astype(jnp.float16)
            total = total + swap(sent, bit).astype(F32) * n_dev
            bit *= 2
        return total

    zero_dd = jnp.zeros(demand.shape, F32)
    zero_flows = jnp.zeros(cost.shape, F32)
    old, flows = zero_flows, jnp.maximum(0.0, -0.5 * (cost - 1.0))
    dd = zero_dd
    link_duals = jnp.zeros((half, intervals, links), F32)
    keep, send = first(me_arr, tile_row, colpos, cost, capacity, tiles)
    for sweep in range(ITERS):
        last = sweep == ITERS - 1
        total = keep + swap(send, 1)
        dd, *base = demand_step(last, cost, demand, dd, old, flows)
        if last:
            break
        link_duals = jnp.maximum(0.0, link_duals + 0.08 * sum_all(total))
        rounded = link_duals.astype(BF16)
        other = swap(rounded, 1)
        keep, send, new = following(
            me_arr, tile_row, rowpos, place, colpos, base[0], flows, rounded, other, capacity, tiles
        )
        old, flows = flows, new
    groups = [[c + 2 * k for k in range(n_dev // 2)] for c in range(2)]
    parts = lax.all_to_all(total, "comm", 0, 0, axis_index_groups=groups, tiled=True)
    own_duals = lax.dynamic_index_in_dim(link_duals, me // 2, 0, keepdims=True)
    own_duals = jnp.maximum(0.0, own_duals + 0.08 * jnp.sum(parts, axis=0, keepdims=True))
    return (flows, own_duals, dd)


def solution(mesh):
    in_specs = (P(("groups", "comm"), None, None),) * 4 + (P(("groups", "comm")),) * 3
    out_specs = (P(("groups", "comm"), None, None),) * 3
    return jax.shard_map(
        per_device, mesh=mesh, in_specs=in_specs, out_specs=out_specs, check_vma=False
    )
```

time: 359 us -> 74.5 us (0.21)
  waiting for transfers between devices: 262 us -> 23.1 us
  blocking collectives: 39.7 us -> 0 us
  matrix products: 26.4 us -> 0 us
  starting transfers between devices: 0.12 us -> 23.3 us
  Pallas kernels: 0 us -> 17.2 us
  between operations: 14.7 us -> 1.46 us
  other arithmetic: 9.43 us -> 2.86 us
    unnamed x6 -> x0, waiting for transfers between devices: 262 us -> none
    all_gather x2 -> x0, blocking collectives: 39.7 us -> none  [per_device(): lax.all_gather(link_duals.astype(jnp.bfloat16), 'comm', axis=0, tiled=True)]
    dot_general x10 -> x0, matrix products: 26.4 us -> none  [the longest x3 11.3 us: per_device(): jnp.einsum('nti,nij->ntj', contributions_picked, tiles, preferred_element...]
    ppermute x0 -> x11, waiting for transfers between devices: none -> 17.3 us  [swap(): return lax.ppermute(x, 'comm', [(i, i ^ bit) for i in range(n_dev)])]
    pallas_call x0 -> x6, Pallas kernels: none -> 17.2 us  [the longest x2 9.02 us: per_device(): following(me_arr, tile_row, rowpos, place, colpos, base[0], flows, rounde...]
    ppermute x0 -> x11, starting transfers between devices: none -> 16.5 us  [swap(): return lax.ppermute(x, 'comm', [(i, i ^ bit) for i in range(n_dev)])]
    all_to_all x0 -> x1, starting transfers between devices: none -> 6.78 us  [per_device(): lax.all_to_all(total, 'comm', 0, 0, axis_index_groups=groups, tiled=True)]
    all_to_all x0 -> x1, waiting for transfers between devices: none -> 5.76 us  [per_device(): lax.all_to_all(total, 'comm', 0, 0, axis_index_groups=groups, tiled=True)]
  transfers between devices with their start and end apart: 3 -> 12, of which waited for: 3 -> 10; matrix products, arithmetic and copies ran while one was open for 1% -> 2% of each run, Pallas kernels for 0% -> 7%
where the time goes in v1:
time: 74.5 us; the launch traced here: 74.1 us
  starting transfers between devices  23.3 us (31%)
  waiting for transfers between devices  23.1 us (31%)
  Pallas kernels  17.2 us (23%)
  local copies, waits for them, and re-layouts  6.31 us (8%)
  other arithmetic  2.86 us (4%)
  between operations  1.46 us (2%)
    ppermute x11, waiting for transfers between devices, swap(): return lax.ppermute(x, 'comm', [(i, i ^ bit) for i in range(n_dev)])  17.3 us
    ppermute x11, starting transfers between devices, swap(): return lax.ppermute(x, 'comm', [(i, i ^ bit) for i in range(n_dev)])  16.5 us
    pallas_call x2, Pallas kernels, per_device(): following(me_arr, tile_row, rowpos, place, colpos, base[0], flows, rounde...  9.02 us
    all_to_all x1, starting transfers between devices, per_device(): lax.all_to_all(total, 'comm', 0, 0, axis_index_groups=groups, tiled=True)  6.78 us
    unnamed x13, local copies, waits for them, and re-layouts  6.28 us
    all_to_all x1, waiting for transfers between devices, per_device(): lax.all_to_all(total, 'comm', 0, 0, axis_index_groups=groups, tiled=True)  5.76 us
    pallas_call x3, Pallas kernels, demand_step(): pl.pallas_call(functools.partial(demand_kernel, last), out_shape=(per_com...  5.53 us
    pallas_call x1, Pallas kernels, per_device(): keep, send = first(me_arr, tile_row, colpos, cost, capacity, tiles)  2.64 us
  transfers between devices with their start and end apart: 12, of which 10 were waited for; matrix products, arithmetic and copies ran while one was open for 2% of the time, Pallas kernels for 7%

profile of v1, /device:TPU:0, one launch (start us, length us, event | category | flops | bytes accessed | tf_op | source)
XLA Modules:
  0.0 74.1 jit_solution(8531756822422907851)
XLA Ops:
  0.6 1.1 %multiply_maximum_fusion = (f32[16,12,256]{2,1,0:T(8,128)S(1)}, f32[16,12,256]{2,1,0:T(8,128)S(1)}) fusion(f32[16,12,256]{2,0,1:T(8,128)} %param.7), kind=kLoop, calls=%fused_computation | loop fusion | flops 147456 | bytes 589824 | tf_op jit(solution)/shard_map/max | solution.py:207
  2.4 0.7 copy.14.cap_ref
  3.1 0.7 compare_select_fusion.3
  3.8 2.8 %copy-done = bf16[48,256,256]{2,1,0:T(8,128)(2,1)S(1)} copy-done((bf16[48,256,256]{2,1,0:T(8,128)(2,1)S(1)}, bf16[48,256,256]{2,1,0:T(8,128)(2,1)}, u32[]{:S(2)}) %copy-start) | copy-done | bytes 6291480
  6.6 0.7 copy-done.2
  7.2 2.6 %first_forward.1 = (f32[8,12,256]{2,1,0:T(8,128)S(1)}, f32[8,12,256]{2,1,0:T(8,128)S(1)}) custom-call(s32[1]{0:T(128)} %bitcast.me_ref, s32[48]{0:T(128)S(1)} %copy-done.2, s32[48]{0:T(128)S(1)} %get-tuple-element.36.colpos_ref, f32[16,12,256]{2,1,0:T(8,128)S(1)} %get-tuple-element.39.cost_ref, f32[1,12,256]{2,1,0:T(8,128)S(1)} %copy.14.cap_ref, ...), custom_call_target="tpu_custom_call" | custom-call | flops 100663296 | bytes 6291456 | tf_op jit(solution)/shard_map/first_forward/pallas_call | solution.py:210
  10.4 1.0 %collective-permute-done = f32[8,12,256]{2,1,0:T(8,128)S(1)} collective-permute-done((f32[8,12,256]{2,1,0:T(8,128)S(1)}, f32[8,12,256]{2,1,0:T(8,128)S(1)}, u32[]{:S(2)}, u32[]{:S(2)}) %collective-permute-start) | collective-permute-done | bytes 98336 | tf_op jit(solution)/shard_map/ppermute | solution.py:193
  11.4 2.9 %collective-permute-start.1 = (f16[8,12,256]{2,1,0:T(8,128)(2,1)S(1)}, f16[8,12,256]{2,1,0:T(8,128)(2,1)S(1)}, u32[]{:S(2)}, u32[]{:S(2)}) collective-permute-start(f16[8,12,256]{2,1,0:T(8,128)(2,1)S(1)} %get-tuple-element.34), channel_id=1, source_target_pairs={{0,2},{1,3},{2,0},{3,1},{4,6},{5,7},{6,4},{7,5},{8,10},{9,11},{10,... | collective-permute-start | bytes 147464 | tf_op jit(solution)/shard_map/ppermute | solution.py:193
  14.4 2.4 %collective-permute-done.1 = f16[8,12,256]{2,1,0:T(8,128)(2,1)S(1)} collective-permute-done((f16[8,12,256]{2,1,0:T(8,128)(2,1)S(1)}, f16[8,12,256]{2,1,0:T(8,128)(2,1)S(1)}, u32[]{:S(2)}, u32[]{:S(2)}) %collective-permute-start.1) | collective-permute-done | bytes 49184 | tf_op jit(solution)/shard_map/ppermute | solution.py:193
  16.8 2.0 %collective-permute-start.2 = (f16[8,12,256]{2,1,0:T(8,128)(2,1)S(1)}, f16[8,12,256]{2,1,0:T(8,128)(2,1)S(1)}, u32[]{:S(2)}, u32[]{:S(2)}) collective-permute-start(f16[8,12,256]{2,1,0:T(8,128)(2,1)S(1)} %multiply_convert_fusion.4), channel_id=1, source_target_pairs={{0,4},{1,5},{2,6},{3,7},{4,0},{5,1},{6,2},{7,3},{8,12},{9,13},{10,... | collective-permute-start | bytes 147464 | tf_op jit(solution)/shard_map/ppermute | solution.py:193
  18.8 2.3 %collective-permute-done.2 = f16[8,12,256]{2,1,0:T(8,128)(2,1)S(1)} collective-permute-done((f16[8,12,256]{2,1,0:T(8,128)(2,1)S(1)}, f16[8,12,256]{2,1,0:T(8,128)(2,1)S(1)}, u32[]{:S(2)}, u32[]{:S(2)}) %collective-permute-start.2) | collective-permute-done | bytes 49184 | tf_op jit(solution)/shard_map/ppermute | solution.py:193
  21.2 3.0 %collective-permute-start.3 = (f16[8,12,256]{2,1,0:T(8,128)(2,1)S(1)}, f16[8,12,256]{2,1,0:T(8,128)(2,1)S(1)}, u32[]{:S(2)}, u32[]{:S(2)}) collective-permute-start(f16[8,12,256]{2,1,0:T(8,128)(2,1)S(1)} %multiply_convert_fusion.3), channel_id=1, source_target_pairs={{0,8},{1,9},{2,10},{3,11},{4,12},{5,13},{6,14},{7,15},{8,0},{9,1},... | collective-permute-start | bytes 147464 | tf_op jit(solution)/shard_map/ppermute | solution.py:193
  24.2 2.2 %collective-permute-done.3 = f16[8,12,256]{2,1,0:T(8,128)(2,1)S(1)} collective-permute-done((f16[8,12,256]{2,1,0:T(8,128)(2,1)S(1)}, f16[8,12,256]{2,1,0:T(8,128)(2,1)S(1)}, u32[]{:S(2)}, u32[]{:S(2)}) %collective-permute-start.3) | collective-permute-done | bytes 49184 | tf_op jit(solution)/shard_map/ppermute | solution.py:193
  26.7 2.6 %demand_step.3 = (f32[16,12,32]{2,1,0:T(8,128)S(1)}, f32[16,12,256]{2,1,0:T(8,128)S(1)}) custom-call(f32[16,12,256]{2,1,0:T(8,128)S(1)} %get-tuple-element.39.cost_ref, f32[16,12,32]{2,1,0:T(8,128)S(1)} %copy.17.demand_ref, f32[16,12,32]{2,1,0:T(8,128)S(1)} %broadcast_in_dim.10.dd_ref, f32[16,12,256]{2,1,0:T(8,128)S(1)} %broadcast_11_old_ref.2.old_ref, ...), custom_call_target="tpu_custom_call" | custom-call | flops 1000000 | bytes 786432 | tf_op jit(solution)/shard_map/demand_step/pallas_call | solution.py:180
  29.3 4.5 %adjoint_forward.2 = (f32[8,12,256]{2,1,0:T(8,128)S(1)}, f32[8,12,256]{2,1,0:T(8,128)S(1)}, f32[16,12,256]{2,1,0:T(8,128)S(1)}) custom-call(s32[1]{0:T(128)} %bitcast.me_ref, s32[48]{0:T(128)S(1)} %copy-done.2, s32[48]{0:T(128)S(1)} %compare_select_fusion.4.rowpos_ref, s32[48]{0:T(128)S(1)} %get-tuple-element.37.col_ref, ...), custom_call_target="tpu_custom_call" | custom-call | flops 201326592 | bytes 6291456 | tf_op jit(solution)/shard_map/adjoint_forward/pallas_call | solution.py:220
  34.4 1.0 %collective-permute-done.5 = f32[8,12,256]{2,1,0:T(8,128)S(1)} collective-permute-done((f32[8,12,256]{2,1,0:T(8,128)S(1)}, f32[8,12,256]{2,1,0:T(8,128)S(1)}, u32[]{:S(2)}, u32[]{:S(2)}) %collective-permute-start.5) | collective-permute-done | bytes 98336 | tf_op jit(solution)/shard_map/ppermute | solution.py:193
  35.4 1.9 %collective-permute-start.6 = (f16[8,12,256]{2,1,0:T(8,128)(2,1)S(1)}, f16[8,12,256]{2,1,0:T(8,128)(2,1)S(1)}, u32[]{:S(2)}, u32[]{:S(2)}) collective-permute-start(f16[8,12,256]{2,1,0:T(8,128)(2,1)S(1)} %get-tuple-element.32), channel_id=1, source_target_pairs={{0,2},{1,3},{2,0},{3,1},{4,6},{5,7},{6,4},{7,5},{8,10},{9,11},{10,... | collective-permute-start | bytes 147464 | tf_op jit(solution)/shard_map/ppermute | solution.py:193
  37.3 2.6 %collective-permute-done.6 = f16[8,12,256]{2,1,0:T(8,128)(2,1)S(1)} collective-permute-done((f16[8,12,256]{2,1,0:T(8,128)(2,1)S(1)}, f16[8,12,256]{2,1,0:T(8,128)(2,1)S(1)}, u32[]{:S(2)}, u32[]{:S(2)}) %collective-permute-start.6) | collective-permute-done | bytes 49184 | tf_op jit(solution)/shard_map/ppermute | solution.py:193
  40.0 1.9 %collective-permute-start.7 = (f16[8,12,256]{2,1,0:T(8,128)(2,1)S(1)}, f16[8,12,256]{2,1,0:T(8,128)(2,1)S(1)}, u32[]{:S(2)}, u32[]{:S(2)}) collective-permute-start(f16[8,12,256]{2,1,0:T(8,128)(2,1)S(1)} %multiply_convert_fusion.1), channel_id=1, source_target_pairs={{0,4},{1,5},{2,6},{3,7},{4,0},{5,1},{6,2},{7,3},{8,12},{9,13},{10,... | collective-permute-start | bytes 147464 | tf_op jit(solution)/shard_map/ppermute | solution.py:193
  41.8 2.5 %collective-permute-done.7 = f16[8,12,256]{2,1,0:T(8,128)(2,1)S(1)} collective-permute-done((f16[8,12,256]{2,1,0:T(8,128)(2,1)S(1)}, f16[8,12,256]{2,1,0:T(8,128)(2,1)S(1)}, u32[]{:S(2)}, u32[]{:S(2)}) %collective-permute-start.7) | collective-permute-done | bytes 49184 | tf_op jit(solution)/shard_map/ppermute | solution.py:193
  44.4 3.0 %collective-permute-start.8 = (f16[8,12,256]{2,1,0:T(8,128)(2,1)S(1)}, f16[8,12,256]{2,1,0:T(8,128)(2,1)S(1)}, u32[]{:S(2)}, u32[]{:S(2)}) collective-permute-start(f16[8,12,256]{2,1,0:T(8,128)(2,1)S(1)} %multiply_convert_fusion), channel_id=1, source_target_pairs={{0,8},{1,9},{2,10},{3,11},{4,12},{5,13},{6,14},{7,15},{8,0},{9,1},... | collective-permute-start | bytes 147464 | tf_op jit(solution)/shard_map/ppermute | solution.py:193
  47.4 2.2 %collective-permute-done.8 = f16[8,12,256]{2,1,0:T(8,128)(2,1)S(1)} collective-permute-done((f16[8,12,256]{2,1,0:T(8,128)(2,1)S(1)}, f16[8,12,256]{2,1,0:T(8,128)(2,1)S(1)}, u32[]{:S(2)}, u32[]{:S(2)}) %collective-permute-start.8) | collective-permute-done | bytes 49184 | tf_op jit(solution)/shard_map/ppermute | solution.py:193
  49.8 2.6 %demand_step.4 = (f32[16,12,32]{2,1,0:T(8,128)S(1)}, f32[16,12,256]{2,1,0:T(8,128)S(1)}) custom-call(f32[16,12,256]{2,1,0:T(8,128)S(1)} %get-tuple-element.39.cost_ref, f32[16,12,32]{2,1,0:T(8,128)S(1)} %copy.17.demand_ref, f32[16,12,32]{2,1,0:T(8,128)S(1)} %get-tuple-element.15.dd_ref, f32[16,12,256]{2,1,0:T(8,128)S(1)} %get-tuple-element.38.new_ref.flows_ref.old_ref, ...), custom_call_target="tpu_custom_call" | custom-call | flops 1000000 | bytes 786432 | tf_op jit(solution)/shard_map/demand_step/pallas_call | solution.py:180
  52.5 4.5 %adjoint_forward.3 = (f32[8,12,256]{2,1,0:T(8,128)S(1)}, f32[8,12,256]{2,1,0:T(8,128)S(1)}, f32[16,12,256]{2,1,0:T(8,128)S(1)}) custom-call(s32[1]{0:T(128)} %bitcast.me_ref, s32[48]{0:T(128)S(1)} %copy-done.2, s32[48]{0:T(128)S(1)} %compare_select_fusion.4.rowpos_ref, s32[48]{0:T(128)S(1)} %get-tuple-element.37.col_ref, ...), custom_call_target="tpu_custom_call" | custom-call | flops 201326592 | bytes 6291456 | tf_op jit(solution)/shard_map/adjoint_forward/pallas_call | solution.py:220
  57.0 0.6 collective-permute-start.10
  57.6 1.0 %collective-permute-done.10 = f32[8,12,256]{2,1,0:T(8,128)S(1)} collective-permute-done((f32[8,12,256]{2,1,0:T(8,128)S(1)}, f32[8,12,256]{2,1,0:T(8,128)S(1)}, u32[]{:S(2)}, u32[]{:S(2)}) %collective-permute-start.10) | collective-permute-done | bytes 98336 | tf_op jit(solution)/shard_map/ppermute | solution.py:193
  58.6 0.7 add.61
  59.2 6.8 %all-to-all-start = ((f32[8,12,256]{2,1,0:T(8,128)}), f32[8,12,256]{2,1,0:T(8,128)S(1)}, u32[]{:S(2)}, u32[]{:S(2)}) async-start(f32[8,12,256]{2,1,0:T(8,128)} %add.61), calls=%async_computation | async-start | bytes 262144 | tf_op jit(solution)/shard_map/all_to_all | solution.py:225
  66.0 0.8 %copy.21 = f32[16,12,256]{2,0,1:T(8,128)} copy(f32[16,12,256]{2,1,0:T(8,128)S(1)} %get-tuple-element.27.new_ref) | data formatting | bytes 393216
  67.0 0.7 copy.23
  67.7 5.8 %all-to-all-done = f32[8,12,256]{2,1,0:T(8,128)S(1)} async-done(((f32[8,12,256]{2,1,0:T(8,128)}), f32[8,12,256]{2,1,0:T(8,128)S(1)}, u32[]{:S(2)}, u32[]{:S(2)}) %all-to-all-start) | async-done | bytes 98336 | tf_op jit(solution)/shard_map/all_to_all | solution.py:225
  73.5 0.6 copy.22
  (27 shorter events, 2.0 us)
Async XLA Ops:
  0.6 25.9 %copy-start.3 = (f32[16,12,32]{2,0,1:T(8,128)S(1)}, f32[16,12,32]{2,0,1:T(8,128)}, u32[]{:S(2)}) copy-start(f32[16,12,32]{2,0,1:T(8,128)} %param.8) | copy-start | bytes 73732
  3.8 2.8 %copy-start = (bf16[48,256,256]{2,1,0:T(8,128)(2,1)S(1)}, bf16[48,256,256]{2,1,0:T(8,128)(2,1)}, u32[]{:S(2)}) copy-start(bf16[48,256,256]{2,1,0:T(8,128)(2,1)} %tiles_hbm.5) | copy-start | bytes 18874372
  6.6 0.7 copy-start.2
  7.2 22.1 %copy-start.1 = (bf16[48,256,256]{2,1,0:T(8,128)(2,1)S(1)}, bf16[48,256,256]{2,1,0:T(8,128)(2,1)}, u32[]{:S(2)}) copy-start(bf16[48,256,256]{2,1,0:T(8,128)(2,1)} %tiles_hbm.5) | copy-start | bytes 18874372
  9.9 1.5 %collective-permute-start = (f32[8,12,256]{2,1,0:T(8,128)S(1)}, f32[8,12,256]{2,1,0:T(8,128)S(1)}, u32[]{:S(2)}, u32[]{:S(2)}) collective-permute-start(f32[8,12,256]{2,1,0:T(8,128)S(1)} %get-tuple-element.18), channel_id=1, source_target_pairs={{0,1},{1,0},{2,3},{3,2},{4,5},{5,4},{6,7},{7,6},{8,9},{9,8},{10,11... | collective-permute-start | bytes 294920 | tf_op jit(solution)/shard_map/ppermute | solution.py:193
  11.4 5.3 %collective-permute-start.1 = (f16[8,12,256]{2,1,0:T(8,128)(2,1)S(1)}, f16[8,12,256]{2,1,0:T(8,128)(2,1)S(1)}, u32[]{:S(2)}, u32[]{:S(2)}) collective-permute-start(f16[8,12,256]{2,1,0:T(8,128)(2,1)S(1)} %get-tuple-element.34), channel_id=1, source_target_pairs={{0,2},{1,3},{2,0},{3,1},{4,6},{5,7},{6,4},{7,5},{8,10},{9,11},{10,... | collective-permute-start | bytes 147464 | tf_op jit(solution)/shard_map/ppermute | solution.py:193
  16.8 4.3 %collective-permute-start.2 = (f16[8,12,256]{2,1,0:T(8,128)(2,1)S(1)}, f16[8,12,256]{2,1,0:T(8,128)(2,1)S(1)}, u32[]{:S(2)}, u32[]{:S(2)}) collective-permute-start(f16[8,12,256]{2,1,0:T(8,128)(2,1)S(1)} %multiply_convert_fusion.4), channel_id=1, source_target_pairs={{0,4},{1,5},{2,6},{3,7},{4,0},{5,1},{6,2},{7,3},{8,12},{9,13},{10,... | collective-permute-start | bytes 147464 | tf_op jit(solution)/shard_map/ppermute | solution.py:193
  21.2 5.2 %collective-permute-start.3 = (f16[8,12,256]{2,1,0:T(8,128)(2,1)S(1)}, f16[8,12,256]{2,1,0:T(8,128)(2,1)S(1)}, u32[]{:S(2)}, u32[]{:S(2)}) collective-permute-start(f16[8,12,256]{2,1,0:T(8,128)(2,1)S(1)} %multiply_convert_fusion.3), channel_id=1, source_target_pairs={{0,8},{1,9},{2,10},{3,11},{4,12},{5,13},{6,14},{7,15},{8,0},{9,1},... | collective-permute-start | bytes 147464 | tf_op jit(solution)/shard_map/ppermute | solution.py:193
  26.5 2.8 %collective-permute-start.4 = (bf16[8,12,256]{2,1,0:T(8,128)(2,1)S(1)}, bf16[8,12,256]{2,1,0:T(8,128)(2,1)S(1)}, u32[]{:S(2)}, u32[]{:S(2)}) collective-permute-start(bf16[8,12,256]{2,1,0:T(8,128)(2,1)S(1)} %fusion.own_ref), channel_id=1, source_target_pairs={{0,1},{1,0},{2,3},{3,2},{4,5},{5,4},{6,7},{7,6},{8,9},{9,8},{10,11... | collective-permute-start | bytes 147464 | tf_op jit(solution)/shard_map/ppermute | solution.py:193
  33.9 1.5 %collective-permute-start.5 = (f32[8,12,256]{2,1,0:T(8,128)S(1)}, f32[8,12,256]{2,1,0:T(8,128)S(1)}, u32[]{:S(2)}, u32[]{:S(2)}) collective-permute-start(f32[8,12,256]{2,1,0:T(8,128)S(1)} %get-tuple-element.22), channel_id=1, source_target_pairs={{0,1},{1,0},{2,3},{3,2},{4,5},{5,4},{6,7},{7,6},{8,9},{9,8},{10,11... | collective-permute-start | bytes 294920 | tf_op jit(solution)/shard_map/ppermute | solution.py:193
  35.4 4.5 %collective-permute-start.6 = (f16[8,12,256]{2,1,0:T(8,128)(2,1)S(1)}, f16[8,12,256]{2,1,0:T(8,128)(2,1)S(1)}, u32[]{:S(2)}, u32[]{:S(2)}) collective-permute-start(f16[8,12,256]{2,1,0:T(8,128)(2,1)S(1)} %get-tuple-element.32), channel_id=1, source_target_pairs={{0,2},{1,3},{2,0},{3,1},{4,6},{5,7},{6,4},{7,5},{8,10},{9,11},{10,... | collective-permute-start | bytes 147464 | tf_op jit(solution)/shard_map/ppermute | solution.py:193
  40.0 4.3 %collective-permute-start.7 = (f16[8,12,256]{2,1,0:T(8,128)(2,1)S(1)}, f16[8,12,256]{2,1,0:T(8,128)(2,1)S(1)}, u32[]{:S(2)}, u32[]{:S(2)}) collective-permute-start(f16[8,12,256]{2,1,0:T(8,128)(2,1)S(1)} %multiply_convert_fusion.1), channel_id=1, source_target_pairs={{0,4},{1,5},{2,6},{3,7},{4,0},{5,1},{6,2},{7,3},{8,12},{9,13},{10,... | collective-permute-start | bytes 147464 | tf_op jit(solution)/shard_map/ppermute | solution.py:193
  44.4 5.3 %collective-permute-start.8 = (f16[8,12,256]{2,1,0:T(8,128)(2,1)S(1)}, f16[8,12,256]{2,1,0:T(8,128)(2,1)S(1)}, u32[]{:S(2)}, u32[]{:S(2)}) collective-permute-start(f16[8,12,256]{2,1,0:T(8,128)(2,1)S(1)} %multiply_convert_fusion), channel_id=1, source_target_pairs={{0,8},{1,9},{2,10},{3,11},{4,12},{5,13},{6,14},{7,15},{8,0},{9,1},... | collective-permute-start | bytes 147464 | tf_op jit(solution)/shard_map/ppermute | solution.py:193
  49.7 2.7 %collective-permute-start.9 = (bf16[8,12,256]{2,1,0:T(8,128)(2,1)S(1)}, bf16[8,12,256]{2,1,0:T(8,128)(2,1)S(1)}, u32[]{:S(2)}, u32[]{:S(2)}) collective-permute-start(bf16[8,12,256]{2,1,0:T(8,128)(2,1)S(1)} %get-tuple-element.30.own_ref), channel_id=1, source_target_pairs={{0,1},{1,0},{2,3},{3,2},{4,5},{5,4},{6,7},{7,6},{8,9},{9,8},{10,11... | collective-permute-start | bytes 147464 | tf_op jit(solution)/shard_map/ppermute | solution.py:193
  57.0 1.6 %collective-permute-start.10 = (f32[8,12,256]{2,1,0:T(8,128)S(1)}, f32[8,12,256]{2,1,0:T(8,128)S(1)}, u32[]{:S(2)}, u32[]{:S(2)}) collective-permute-start(f32[8,12,256]{2,1,0:T(8,128)S(1)} %get-tuple-element.25), channel_id=1, source_target_pairs={{0,1},{1,0},{2,3},{3,2},{4,5},{5,4},{6,7},{7,6},{8,9},{9,8},{10,11... | collective-permute-start | bytes 294920 | tf_op jit(solution)/shard_map/ppermute | solution.py:193
  59.2 14.3 %all-to-all-start = ((f32[8,12,256]{2,1,0:T(8,128)}), f32[8,12,256]{2,1,0:T(8,128)S(1)}, u32[]{:S(2)}, u32[]{:S(2)}) async-start(f32[8,12,256]{2,1,0:T(8,128)} %add.61), calls=%async_computation | async-start | bytes 262144 | tf_op jit(solution)/shard_map/all_to_all | solution.py:225

commit v2 on v1

v2 whole, which is shorter than its diff:
```python
import functools

import jax
import jax.numpy as jnp
from jax import lax
from jax.experimental import pallas as pl
from jax.experimental.pallas import tpu as pltpu
from jax.sharding import PartitionSpec as P

PATHS_PER = 8
ITERS = 3
CHUNKS = 8
VMEM_LIMIT = 40 * 2**20
F32 = jnp.float32
BF16 = jnp.bfloat16


def spec(space):
    return pl.BlockSpec(memory_space=space)


def forward(row_ref, col_ref, live, tiles_v, ex, accs, wait=None):
    slots = tiles_v.shape[0]
    half = (accs[0].shape[0] - 1) // 2
    for acc in accs:
        acc[...] = jnp.zeros_like(acc)
    for n in range(slots):
        if wait is not None:
            wait(n)
        acc = accs[n % 2]
        col = col_ref[n]
        place = jnp.where(n < live, (col & 1) * half + (col >> 1), 2 * half)
        acc[place] += jnp.dot(ex[row_ref[n]], tiles_v[n], preferred_element_type=F32)


def emit(me, cap_ref, accs, keep_ref, send_ref):
    half = keep_ref.shape[0]
    core = me & 1
    accs[0][core * half + (me >> 1)] -= cap_ref[0]
    mine = pl.ds(core * half, half)
    theirs = pl.ds((1 - core) * half, half)
    send_ref[...] = accs[0][theirs] + accs[1][theirs]
    keep_ref[...] = accs[0][mine] + accs[1][mine]


def first_kernel(
    row_ref, col_ref, count_ref, cap_ref, cost_hbm, tiles_hbm, keep_ref, send_ref, tiles_v,
    cost_v, ex, acc0, acc1, cost_sem, sems,
):
    me = lax.axis_index("comm")
    size = tiles_v.shape[0] // CHUNKS
    load = pltpu.make_async_copy(cost_hbm, cost_v, cost_sem)
    load.start()
    copies = []
    for k in range(CHUNKS):
        part = pl.ds(k * size, size)
        copies.append(pltpu.make_async_copy(tiles_hbm.at[part], tiles_v.at[part], sems.at[k]))
        copies[-1].start()
    load.wait()
    flows = jnp.maximum(0.0, -0.5 * (cost_v[...] - 1.0))
    ex[...] = (2.0 * flows).astype(BF16)

    def wait(n):
        if n % size == 0:
            copies[n // size].wait()

    accs = (acc0, acc1)
    forward(row_ref, col_ref, count_ref[0], tiles_v, ex, accs, wait)
    emit(me, cap_ref, accs, keep_ref, send_ref)


def next_kernel(
    row_ref, col_ref, count_ref, cap_ref, base_ref, flows_ref, own_ref, other_ref, tiles_v,
    keep_ref, send_ref, new_ref, ex, acc0, acc1, grad0, grad1, duals,
):
    me = lax.axis_index("comm")
    live = count_ref[0]
    half = own_ref.shape[0]
    core = me & 1
    duals[pl.ds(core * half, half)] = own_ref[...]
    duals[pl.ds((1 - core) * half, half)] = other_ref[...]
    grads = (grad0, grad1)
    for grad in grads:
        grad[...] = jnp.zeros_like(grad)
    blocks = base_ref.shape[0]
    for n in range(tiles_v.shape[0]):
        grad = grads[n % 2]
        col = col_ref[n]
        row = jnp.where(n < live, row_ref[n], blocks)
        grad[row] += lax.dot_general(
            duals[(col & 1) * half + (col >> 1)], tiles_v[n], (((1,), (1,)), ((), ())),
            preferred_element_type=F32,
        )
    new = jnp.maximum(
        0.0, base_ref[...] - 0.5 * (grad0[pl.ds(0, blocks)] + grad1[pl.ds(0, blocks)])
    )
    new_ref[...] = new
    ex[...] = (2.0 * new - flows_ref[...]).astype(BF16)
    accs = (acc0, acc1)
    forward(row_ref, col_ref, live, tiles_v, ex, accs)
    emit(me, cap_ref, accs, keep_ref, send_ref)


def commodity_matrix(paths):
    path = lax.broadcasted_iota(jnp.int32, (paths, paths // PATHS_PER), 0)
    low = lax.broadcasted_iota(jnp.int32, (paths, paths // PATHS_PER), 1) * PATHS_PER
    return ((path >= low) & (path < low + PATHS_PER)).astype(F32)


def demand_kernel(sweep, *refs):
    refs = list(refs)
    cost_ref, demand_ref = refs[:2]
    blocks, intervals, paths = cost_ref.shape
    if sweep == 0:
        dd_ref, base_ref, flows_ref, rows, spread = refs[2:]
        flows_ref[...] = jnp.maximum(0.0, -0.5 * (cost_ref[...] - 1.0))
    elif sweep < ITERS - 1:
        old_dd_ref, old_ref, flows_ref, dd_ref, base_ref, rows, spread = refs[2:]
    else:
        old_dd_ref, old_ref, flows_ref, dd_ref, rows, spread = refs[2:]
    which = commodity_matrix(paths)
    ex = 2.0 * flows_ref[...]
    if sweep > 0:
        ex = ex - old_ref[...]
    rows[...] = jnp.zeros_like(rows)
    spread[...] = jnp.zeros_like(spread)
    rows[:, :intervals] = ex.astype(BF16).astype(F32)
    per = jnp.dot(
        rows[...].reshape(-1, paths).astype(BF16), which.astype(BF16), preferred_element_type=F32
    ).reshape(blocks, -1, paths // PATHS_PER)[:, :intervals]
    dd = 0.2 * (per - demand_ref[...])
    if sweep > 0:
        dd = old_dd_ref[...] + dd
    dd = jnp.maximum(0.0, dd)
    dd_ref[...] = dd
    if sweep < ITERS - 1:
        spread[:, :intervals] = dd
        wide = lax.dot_general(
            spread[...].reshape(-1, paths // PATHS_PER), which, (((1,), (1,)), ((), ())),
            precision=lax.Precision.HIGHEST, preferred_element_type=F32,
        ).reshape(blocks, -1, paths)[:, :intervals]
        base_ref[...] = flows_ref[...] - 0.5 * (cost_ref[...] - 1.0 + wide)


def per_device(cost, demand, capacity, tiles, tile_row, tile_col, tile_count):
    slots, paths, links = tiles.shape
    blocks, intervals, _ = cost.shape
    n_dev = lax.axis_size("comm")
    link_blocks = n_dev * capacity.shape[0]
    half = link_blocks // 2
    me = lax.axis_index("comm")

    V, S, A = pltpu.VMEM, pltpu.SMEM, pl.ANY
    params = pltpu.CompilerParams(vmem_limit_bytes=VMEM_LIMIT)
    halves = jax.ShapeDtypeStruct((half, intervals, links), F32)
    per_path = jax.ShapeDtypeStruct(cost.shape, F32)
    per_comm = jax.ShapeDtypeStruct(demand.shape, F32)
    passes = 2 * slots * 16 * paths * links
    padded = -(-intervals // 16) * 16
    acc_scratch = [V((link_blocks + 1, intervals, links), F32)] * 2
    grad_scratch = [V((blocks + 1, intervals, paths), F32)] * 2

    keep, send, tiles_v = pl.pallas_call(
        first_kernel,
        out_shape=(halves, halves, V(tiles.shape, BF16)),
        in_specs=[spec(S)] * 3 + [spec(V)] + [spec(pltpu.HBM)] * 2,
        out_specs=(spec(V),) * 3,
        scratch_shapes=[V(cost.shape, F32), V(cost.shape, BF16)]
        + acc_scratch
        + [pltpu.SemaphoreType.DMA, pltpu.SemaphoreType.DMA((CHUNKS,))],
        compiler_params=params,
        cost_estimate=pl.CostEstimate(
            flops=passes, bytes_accessed=tiles.size * 2, transcendentals=0
        ),
        name="first_forward",
    )(tile_row, tile_col, tile_count, capacity, cost, tiles)

    following = pl.pallas_call(
        next_kernel,
        out_shape=(halves, halves, per_path),
        in_specs=[spec(S)] * 3 + [spec(V)] * 6,
        out_specs=(spec(V),) * 3,
        scratch_shapes=[V(cost.shape, BF16)]
        + acc_scratch
        + grad_scratch
        + [V((link_blocks, intervals, links), BF16)],
        compiler_params=params,
        cost_estimate=pl.CostEstimate(
            flops=2 * passes, bytes_accessed=tiles.size * 2, transcendentals=0
        ),
        name="adjoint_forward",
    )

    def demand_step(sweep, *args):
        outs = ((per_comm, per_path, per_path), (per_comm, per_path), (per_comm,))
        outs = outs[0 if sweep == 0 else 2 if sweep == ITERS - 1 else 1]
        return pl.pallas_call(
            functools.partial(demand_kernel, sweep),
            out_shape=outs,
            in_specs=[spec(V)] * len(args),
            out_specs=(spec(V),) * len(outs),
            scratch_shapes=[
                V((blocks, padded, paths), F32),
                V((blocks, padded, paths // PATHS_PER), F32),
            ],
            compiler_params=params,
            cost_estimate=pl.CostEstimate(
                flops=10**6, bytes_accessed=4 * cost.size * 4, transcendentals=0
            ),
            name="demand_step",
        )(*args)

    def swap(x, bit):
        return lax.ppermute(x, "comm", [(i, i ^ bit) for i in range(n_dev)])

    stages = []
    bit = 2
    while bit < n_dev:
        stages.append((bit, min(4, n_dev // bit)))
        bit *= 4

    def sum_all(total):
        for bit, size in stages:
            sent = (total * (1.0 / n_dev)).astype(jnp.float16)
            parts = [swap(sent, bit * d) for d in range(1, size)]
            for part in parts:
                total = total + part.astype(F32) * n_dev
        return total

    def scatter(total):
        for bit, size in stages:
            here = (me // bit) % size
            total = total.reshape((-1, size) + total.shape[1:])
            pick = lambda i: lax.dynamic_index_in_dim(total, i, 1, keepdims=False)
            parts = [swap(pick(here ^ d), bit * d) for d in range(1, size)]
            total = pick(here)
            for part in parts:
                total = total + part
        return total

    dd = flows = old = None
    link_duals = jnp.zeros((half, intervals, links), F32)
    for sweep in range(ITERS):
        total = keep + swap(send, 1)
        if sweep == 0:
            dd, base, flows = demand_step(0, cost, demand)
        elif sweep < ITERS - 1:
            dd, base = demand_step(sweep, cost, demand, dd, old, flows)
        else:
            (dd,) = demand_step(sweep, cost, demand, dd, old, flows)
            break
        link_duals = jnp.maximum(0.0, link_duals + 0.08 * sum_all(total))
        rounded = link_duals.astype(BF16)
        keep, send, new = following(
            tile_row, tile_col, tile_count, capacity, base, flows, rounded, swap(rounded, 1), tiles_v
        )
        old, flows = flows, new
    own_duals = lax.dynamic_index_in_dim(link_duals, me // 2, 0, keepdims=True)
    own_duals = jnp.maximum(0.0, own_duals + 0.08 * scatter(total))
    return (flows, own_duals, dd)


def solution(mesh):
    in_specs = (P(("groups", "comm"), None, None),) * 4 + (P(("groups", "comm")),) * 3
    out_specs = (P(("groups", "comm"), None, None),) * 3
    return jax.shard_map(
        per_device, mesh=mesh, in_specs=in_specs, out_specs=out_specs, check_vma=False
    )
```

time: 74.5 us -> 64.7 us (0.87)
  Pallas kernels: 17.2 us -> 11 us
  other arithmetic: 2.86 us -> 0.33 us
  starting transfers between devices: 23.3 us -> 20.9 us
  local copies, waits for them, and re-layouts: 6.31 us -> 8.03 us
    all_to_all x1 -> x0, starting transfers between devices: 6.78 us -> none  [per_device(): lax.all_to_all(total, 'comm', 0, 0, axis_index_groups=groups, tiled=True)]
    pallas_call x6, Pallas kernels: 17.2 us -> 11 us  [the longest x2 6.72 us: per_device(): following(tile_row, tile_col, tile_count, capacity, base, flows, rounded,...]
    all_to_all x1 -> x0, waiting for transfers between devices: 5.76 us -> none  [per_device(): lax.all_to_all(total, 'comm', 0, 0, axis_index_groups=groups, tiled=True)]
    ppermute x11 -> x17, waiting for transfers between devices: 17.3 us -> 22.8 us  [swap(): return lax.ppermute(x, 'comm', [(i, i ^ bit) for i in range(n_dev)])]
    ppermute x11 -> x17, starting transfers between devices: 16.5 us -> 20.9 us  [swap(): return lax.ppermute(x, 'comm', [(i, i ^ bit) for i in range(n_dev)])]
    unnamed x13 -> x14, local copies, waits for them, and re-layouts: 6.28 us -> 8 us
    max x2 -> x1, other arithmetic: 1.13 us -> 0.01 us  [per_device(): own_duals = jnp.maximum(0.0, own_duals + 0.08 * scatter(total))]
  transfers between devices with their start and end apart: 12 -> 17, of which waited for: 10 -> 17; matrix products, arithmetic and copies ran while one was open for 2% -> 2% of each run, Pallas kernels for 7% -> 2%
where the time goes in v2:
time: 64.7 us; the launch traced here: 64.4 us
  waiting for transfers between devices  22.8 us (35%)
  starting transfers between devices  20.9 us (32%)
  Pallas kernels  11 us (17%)
  local copies, waits for them, and re-layouts  8.03 us (12%)
  between operations  1.44 us (2%)
    ppermute x17, waiting for transfers between devices, swap(): return lax.ppermute(x, 'comm', [(i, i ^ bit) for i in range(n_dev)])  22.8 us
    ppermute x17, starting transfers between devices, swap(): return lax.ppermute(x, 'comm', [(i, i ^ bit) for i in range(n_dev)])  20.9 us
    unnamed x14, local copies, waits for them, and re-layouts  8 us
    pallas_call x2, Pallas kernels, per_device(): following(tile_row, tile_col, tile_count, capacity, base, flows, rounded,...  6.72 us
    pallas_call x1, Pallas kernels, per_device(): pl.pallas_call(first_kernel, out_shape=(halves, halves, V(tiles.shape, BF...  2.93 us
    pallas_call x3, Pallas kernels, demand_step(): pl.pallas_call(functools.partial(demand_kernel, sweep), out_shape=outs, i...  1.31 us
  transfers between devices with their start and end apart: 17, of which 17 were waited for; matrix products, arithmetic and copies ran while one was open for 2% of the time, Pallas kernels for 2%

profile of v2, /device:TPU:0, one launch (start us, length us, event | category | flops | bytes accessed | tf_op | source)
XLA Modules:
  0.0 64.4 jit_solution(17113122729262669694)
XLA Ops:
  0.6 1.1 %copy.15.refs_0_.cost_hbm = f32[16,12,256]{2,1,0:T(8,128)S(1)} copy(f32[16,12,256]{2,0,1:T(8,128)} %param.7) | data formatting | bytes 393216 | tf_op args[0]
  1.7 0.7 %copy.17.cap_ref = f32[1,12,256]{2,1,0:T(8,128)S(1)} copy(f32[1,12,256]{2,0,1:T(1,128)} %param.9) | data formatting | bytes 24576 | tf_op args[2]
  3.1 2.8 %copy-done = bf16[48,256,256]{2,1,0:T(8,128)(2,1)S(1)} copy-done((bf16[48,256,256]{2,1,0:T(8,128)(2,1)S(1)}, bf16[48,256,256]{2,1,0:T(8,128)(2,1)}, u32[]{:S(2)}) %copy-start) | copy-done | bytes 6291480
  5.9 0.7 %copy-done.1 = s32[48]{0:T(128)S(1)} copy-done((s32[48]{0:T(128)S(1)}, s32[48]{0:T(128)}, u32[]{:S(2)}) %copy-start.1) | copy-done | bytes 216
  6.5 0.7 %copy-done.2 = s32[48]{0:T(128)S(1)} copy-done((s32[48]{0:T(128)S(1)}, s32[48]{0:T(128)}, u32[]{:S(2)}) %copy-start.2) | copy-done | bytes 216
  7.2 2.9 %first_forward.1 = (f32[8,12,256]{2,1,0:T(8,128)S(1)}, f32[8,12,256]{2,1,0:T(8,128)S(1)}, bf16[48,256,256]{2,1,0:T(8,128)(2,1)S(1)}) custom-call(s32[48]{0:T(128)S(1)} %copy-done.1, s32[48]{0:T(128)S(1)} %copy-done.2, s32[1]{0:T(128)S(6)} %copy.31.count_ref, f32[1,12,256]{2,1,0:T(8,128)S(1)} %copy.17.cap_ref, f32[16,12,256]{2,1,0:T(8,128)S(1)} %copy.15.refs_0_.cost_hbm, ...), custom_call_target="tpu_custom_call" | custom-call | flops 100663296 | bytes 6291456 | tf_op jit(solution)/shard_map/first_forward/pallas_call | solution.py:163
  10.6 1.0 %collective-permute-done = f32[8,12,256]{2,1,0:T(8,128)S(1)} collective-permute-done((f32[8,12,256]{2,1,0:T(8,128)S(1)}, f32[8,12,256]{2,1,0:T(8,128)S(1)}, u32[]{:S(2)}, u32[]{:S(2)}) %collective-permute-start) | collective-permute-done | bytes 98336 | tf_op jit(solution)/shard_map/ppermute | solution.py:214
  11.7 2.9 %collective-permute-start.1 = (f16[8,12,256]{2,1,0:T(8,128)(2,1)S(1)}, f16[8,12,256]{2,1,0:T(8,128)(2,1)S(1)}, u32[]{:S(2)}, u32[]{:S(2)}) collective-permute-start(f16[8,12,256]{2,1,0:T(8,128)(2,1)S(1)} %get-tuple-element.40), channel_id=1, source_target_pairs={{0,2},{1,3},{2,0},{3,1},{4,6},{5,7},{6,4},{7,5},{8,10},{9,11},{10,... | collective-permute-start | bytes 147464 | tf_op jit(solution)/shard_map/ppermute | solution.py:214
  14.6 1.6 %collective-permute-start.2 = (f16[8,12,256]{2,1,0:T(8,128)(2,1)S(1)}, f16[8,12,256]{2,1,0:T(8,128)(2,1)S(1)}, u32[]{:S(2)}, u32[]{:S(2)}) collective-permute-start(f16[8,12,256]{2,1,0:T(8,128)(2,1)S(1)} %get-tuple-element.40), channel_id=1, source_target_pairs={{0,4},{1,5},{2,6},{3,7},{4,0},{5,1},{6,2},{7,3},{8,12},{9,13},{10,... | collective-permute-start | bytes 147464 | tf_op jit(solution)/shard_map/ppermute | solution.py:214
  16.2 0.8 %collective-permute-done.1 = f16[8,12,256]{2,1,0:T(8,128)(2,1)S(1)} collective-permute-done((f16[8,12,256]{2,1,0:T(8,128)(2,1)S(1)}, f16[8,12,256]{2,1,0:T(8,128)(2,1)S(1)}, u32[]{:S(2)}, u32[]{:S(2)}) %collective-permute-start.1) | collective-permute-done | bytes 49184 | tf_op jit(solution)/shard_map/ppermute | solution.py:214
  17.0 2.4 %collective-permute-done.2 = f16[8,12,256]{2,1,0:T(8,128)(2,1)S(1)} collective-permute-done((f16[8,12,256]{2,1,0:T(8,128)(2,1)S(1)}, f16[8,12,256]{2,1,0:T(8,128)(2,1)S(1)}, u32[]{:S(2)}, u32[]{:S(2)}) %collective-permute-start.2) | collective-permute-done | bytes 49184 | tf_op jit(solution)/shard_map/ppermute | solution.py:214
  19.4 1.9 %collective-permute-done.3 = f16[8,12,256]{2,1,0:T(8,128)(2,1)S(1)} collective-permute-done((f16[8,12,256]{2,1,0:T(8,128)(2,1)S(1)}, f16[8,12,256]{2,1,0:T(8,128)(2,1)S(1)}, u32[]{:S(2)}, u32[]{:S(2)}) %collective-permute-start.3) | collective-permute-done | bytes 49184 | tf_op jit(solution)/shard_map/ppermute | solution.py:214
  21.4 2.7 %collective-permute-start.4 = (f16[8,12,256]{2,1,0:T(8,128)(2,1)S(1)}, f16[8,12,256]{2,1,0:T(8,128)(2,1)S(1)}, u32[]{:S(2)}, u32[]{:S(2)}) collective-permute-start(f16[8,12,256]{2,1,0:T(8,128)(2,1)S(1)} %get-tuple-element.38), channel_id=1, source_target_pairs={{0,8},{1,9},{2,10},{3,11},{4,12},{5,13},{6,14},{7,15},{8,0},{9,1},... | collective-permute-start | bytes 147464 | tf_op jit(solution)/shard_map/ppermute | solution.py:214
  24.0 3.2 %collective-permute-done.4 = f16[8,12,256]{2,1,0:T(8,128)(2,1)S(1)} collective-permute-done((f16[8,12,256]{2,1,0:T(8,128)(2,1)S(1)}, f16[8,12,256]{2,1,0:T(8,128)(2,1)S(1)}, u32[]{:S(2)}, u32[]{:S(2)}) %collective-permute-start.4) | collective-permute-done | bytes 49184 | tf_op jit(solution)/shard_map/ppermute | solution.py:214
  28.6 3.4 %adjoint_forward.2 = (f32[8,12,256]{2,1,0:T(8,128)S(1)}, f32[8,12,256]{2,1,0:T(8,128)S(1)}, f32[16,12,256]{2,1,0:T(8,128)S(1)}) custom-call(s32[48]{0:T(128)S(1)} %copy-done.1, s32[48]{0:T(128)S(1)} %copy-done.2, s32[1]{0:T(128)S(6)} %copy.31.count_ref, f32[1,12,256]{2,1,0:T(8,128)S(1)} %copy.17.cap_ref, f32[16,12,256]{2,1,0:T(8,128)S(1)} %get-tuple-element.19.base_ref, ...), custom_call_target="tpu_custom_call" | custom-call | flops 201326592 | bytes 6291456 | tf_op jit(solution)/shard_map/adjoint_forward/pallas_call | solution.py:254
  32.2 1.2 %collective-permute-done.6 = f32[8,12,256]{2,1,0:T(8,128)S(1)} collective-permute-done((f32[8,12,256]{2,1,0:T(8,128)S(1)}, f32[8,12,256]{2,1,0:T(8,128)S(1)}, u32[]{:S(2)}, u32[]{:S(2)}) %collective-permute-start.6) | collective-permute-done | bytes 98336 | tf_op jit(solution)/shard_map/ppermute | solution.py:214
  33.4 0.7 %collective-permute-start.7 = (f16[8,12,256]{2,1,0:T(8,128)(2,1)S(1)}, f16[8,12,256]{2,1,0:T(8,128)(2,1)S(1)}, u32[]{:S(2)}, u32[]{:S(2)}) collective-permute-start(f16[8,12,256]{2,1,0:T(8,128)(2,1)S(1)} %get-tuple-element.36), channel_id=1, source_target_pairs={{0,2},{1,3},{2,0},{3,1},{4,6},{5,7},{6,4},{7,5},{8,10},{9,11},{10,... | collective-permute-start | bytes 147464 | tf_op jit(solution)/shard_map/ppermute | solution.py:214
  34.5 2.4 %collective-permute-start.9 = (f16[8,12,256]{2,1,0:T(8,128)(2,1)S(1)}, f16[8,12,256]{2,1,0:T(8,128)(2,1)S(1)}, u32[]{:S(2)}, u32[]{:S(2)}) collective-permute-start(f16[8,12,256]{2,1,0:T(8,128)(2,1)S(1)} %get-tuple-element.36), channel_id=1, source_target_pairs={{0,6},{1,7},{2,4},{3,5},{4,2},{5,3},{6,0},{7,1},{8,14},{9,15},{10,... | collective-permute-start | bytes 147464 | tf_op jit(solution)/shard_map/ppermute | solution.py:214
  36.9 0.8 %collective-permute-done.7 = f16[8,12,256]{2,1,0:T(8,128)(2,1)S(1)} collective-permute-done((f16[8,12,256]{2,1,0:T(8,128)(2,1)S(1)}, f16[8,12,256]{2,1,0:T(8,128)(2,1)S(1)}, u32[]{:S(2)}, u32[]{:S(2)}) %collective-permute-start.7) | collective-permute-done | bytes 49184 | tf_op jit(solution)/shard_map/ppermute | solution.py:214
  37.7 1.1 %collective-permute-done.8 = f16[8,12,256]{2,1,0:T(8,128)(2,1)S(1)} collective-permute-done((f16[8,12,256]{2,1,0:T(8,128)(2,1)S(1)}, f16[8,12,256]{2,1,0:T(8,128)(2,1)S(1)}, u32[]{:S(2)}, u32[]{:S(2)}) %collective-permute-start.8) | collective-permute-done | bytes 49184 | tf_op jit(solution)/shard_map/ppermute | solution.py:214
  38.8 1.4 %collective-permute-done.9 = f16[8,12,256]{2,1,0:T(8,128)(2,1)S(1)} collective-permute-done((f16[8,12,256]{2,1,0:T(8,128)(2,1)S(1)}, f16[8,12,256]{2,1,0:T(8,128)(2,1)S(1)}, u32[]{:S(2)}, u32[]{:S(2)}) %collective-permute-start.9) | collective-permute-done | bytes 49184 | tf_op jit(solution)/shard_map/ppermute | solution.py:214
  40.2 2.8 %collective-permute-start.10 = (f16[8,12,256]{2,1,0:T(8,128)(2,1)S(1)}, f16[8,12,256]{2,1,0:T(8,128)(2,1)S(1)}, u32[]{:S(2)}, u32[]{:S(2)}) collective-permute-start(f16[8,12,256]{2,1,0:T(8,128)(2,1)S(1)} %multiply_convert_fusion), channel_id=1, source_target_pairs={{0,8},{1,9},{2,10},{3,11},{4,12},{5,13},{6,14},{7,15},{8,0},{9,1},... | collective-permute-start | bytes 147464 | tf_op jit(solution)/shard_map/ppermute | solution.py:214
  43.0 3.2 %collective-permute-done.10 = f16[8,12,256]{2,1,0:T(8,128)(2,1)S(1)} collective-permute-done((f16[8,12,256]{2,1,0:T(8,128)(2,1)S(1)}, f16[8,12,256]{2,1,0:T(8,128)(2,1)S(1)}, u32[]{:S(2)}, u32[]{:S(2)}) %collective-permute-start.10) | collective-permute-done | bytes 49184 | tf_op jit(solution)/shard_map/ppermute | solution.py:214
  46.9 0.7 %collective-permute-done.11.other_ref = bf16[8,12,256]{2,1,0:T(8,128)(2,1)S(1)} collective-permute-done((bf16[8,12,256]{2,1,0:T(8,128)(2,1)S(1)}, bf16[8,12,256]{2,1,0:T(8,128)(2,1)S(1)}, u32[]{:S(2)}, u32[]{:S(2)}) %collective-permute-start.11) | collective-permute-done | bytes 49184 | tf_op jit(solution)/shard_map/ppermute | solution.py:214
  47.6 3.4 %adjoint_forward.3 = (f32[8,12,256]{2,1,0:T(8,128)S(1)}, f32[8,12,256]{2,1,0:T(8,128)S(1)}, f32[16,12,256]{2,1,0:T(8,128)S(1)}) custom-call(s32[48]{0:T(128)S(1)} %copy-done.1, s32[48]{0:T(128)S(1)} %copy-done.2, s32[1]{0:T(128)S(6)} %copy.31.count_ref, f32[1,12,256]{2,1,0:T(8,128)S(1)} %copy.17.cap_ref, f32[16,12,256]{2,1,0:T(8,128)S(1)} %get-tuple-element.24.base_ref, ...), custom_call_target="tpu_custom_call" | custom-call | flops 201326592 | bytes 6291456 | tf_op jit(solution)/shard_map/adjoint_forward/pallas_call | solution.py:254
  51.2 1.2 %collective-permute-done.12 = f32[8,12,256]{2,1,0:T(8,128)S(1)} collective-permute-done((f32[8,12,256]{2,1,0:T(8,128)S(1)}, f32[8,12,256]{2,1,0:T(8,128)S(1)}, u32[]{:S(2)}, u32[]{:S(2)}) %collective-permute-start.12) | collective-permute-done | bytes 98336 | tf_op jit(solution)/shard_map/ppermute | solution.py:214
  52.6 1.7 %collective-permute-start.14 = (f32[2,12,256]{2,1,0:T(8,128)S(1)}, f32[2,12,256]{2,1,0:T(8,128)S(1)}, u32[]{:S(2)}, u32[]{:S(2)}) collective-permute-start(f32[2,12,256]{2,1,0:T(8,128)S(1)} %get-tuple-element.43), channel_id=1, source_target_pairs={{0,4},{1,5},{2,6},{3,7},{4,0},{5,1},{6,2},{7,3},{8,12},{9,13},{10,... | collective-permute-start | bytes 73736 | tf_op jit(solution)/shard_map/ppermute | solution.py:214
  54.3 1.7 %collective-permute-start.15 = (f32[2,12,256]{2,1,0:T(8,128)S(1)}, f32[2,12,256]{2,1,0:T(8,128)S(1)}, u32[]{:S(2)}, u32[]{:S(2)}) collective-permute-start(f32[2,12,256]{2,1,0:T(8,128)S(1)} %get-tuple-element.44), channel_id=1, source_target_pairs={{0,6},{1,7},{2,4},{3,5},{4,2},{5,3},{6,0},{7,1},{8,14},{9,15},{10,... | collective-permute-start | bytes 73736 | tf_op jit(solution)/shard_map/ppermute | solution.py:214
  56.5 2.6 %collective-permute-done.15 = f32[2,12,256]{2,1,0:T(8,128)S(1)} collective-permute-done((f32[2,12,256]{2,1,0:T(8,128)S(1)}, f32[2,12,256]{2,1,0:T(8,128)S(1)}, u32[]{:S(2)}, u32[]{:S(2)}) %collective-permute-start.15) | collective-permute-done | bytes 24608 | tf_op jit(solution)/shard_map/ppermute | solution.py:214
  59.1 2.7 %collective-permute-start.16 = (f32[1,12,256]{2,1,0:T(8,128)S(1)}, f32[1,12,256]{2,1,0:T(8,128)S(1)}, u32[]{:S(2)}, u32[]{:S(2)}) collective-permute-start(f32[1,12,256]{2,1,0:T(8,128)S(1)} %constant_dynamic-slice_fusion), channel_id=1, source_target_pairs={{0,8},{1,9},{2,10},{3,11},{4,12},{5,13},{6,14},{7,15},{8,0},{9,1},... | collective-permute-start | bytes 36872 | tf_op jit(solution)/shard_map/ppermute | solution.py:214
  61.9 0.8 %copy.24 = f32[16,12,256]{2,0,1:T(8,128)} copy(f32[16,12,256]{2,1,0:T(8,128)S(1)} %get-tuple-element.31.refs_4_) | data formatting | bytes 393216
  62.9 0.7 %copy.26 = f32[16,12,32]{2,0,1:T(8,128)} copy(f32[16,12,32]{2,1,0:T(8,128)S(1)} %demand_step.5) | data formatting | bytes 49152
  (33 shorter events, 5.4 us)
Async XLA Ops:
  0.6 26.7 %copy-start.3 = (f32[16,12,32]{2,0,1:T(8,128)S(1)}, f32[16,12,32]{2,0,1:T(8,128)}, u32[]{:S(2)}) copy-start(f32[16,12,32]{2,0,1:T(8,128)} %param.8) | copy-start | bytes 73732
  3.1 2.8 %copy-start = (bf16[48,256,256]{2,1,0:T(8,128)(2,1)S(1)}, bf16[48,256,256]{2,1,0:T(8,128)(2,1)}, u32[]{:S(2)}) copy-start(bf16[48,256,256]{2,1,0:T(8,128)(2,1)} %tiles_hbm.1) | copy-start | bytes 18874372
  5.9 0.7 %copy-start.1 = (s32[48]{0:T(128)S(1)}, s32[48]{0:T(128)}, u32[]{:S(2)}) copy-start(s32[48]{0:T(128)} %row_ref.5) | copy-start | bytes 580
  6.5 0.7 %copy-start.2 = (s32[48]{0:T(128)S(1)}, s32[48]{0:T(128)}, u32[]{:S(2)}) copy-start(s32[48]{0:T(128)} %col_ref.5) | copy-start | bytes 580
  10.1 1.5 %collective-permute-start = (f32[8,12,256]{2,1,0:T(8,128)S(1)}, f32[8,12,256]{2,1,0:T(8,128)S(1)}, u32[]{:S(2)}, u32[]{:S(2)}) collective-permute-start(f32[8,12,256]{2,1,0:T(8,128)S(1)} %get-tuple-element.21), channel_id=1, source_target_pairs={{0,1},{1,0},{2,3},{3,2},{4,5},{5,4},{6,7},{7,6},{8,9},{9,8},{10,11... | collective-permute-start | bytes 294920 | tf_op jit(solution)/shard_map/ppermute | solution.py:214
  11.7 5.3 %collective-permute-start.1 = (f16[8,12,256]{2,1,0:T(8,128)(2,1)S(1)}, f16[8,12,256]{2,1,0:T(8,128)(2,1)S(1)}, u32[]{:S(2)}, u32[]{:S(2)}) collective-permute-start(f16[8,12,256]{2,1,0:T(8,128)(2,1)S(1)} %get-tuple-element.40), channel_id=1, source_target_pairs={{0,2},{1,3},{2,0},{3,1},{4,6},{5,7},{6,4},{7,5},{8,10},{9,11},{10,... | collective-permute-start | bytes 147464 | tf_op jit(solution)/shard_map/ppermute | solution.py:214
  14.6 4.8 %collective-permute-start.2 = (f16[8,12,256]{2,1,0:T(8,128)(2,1)S(1)}, f16[8,12,256]{2,1,0:T(8,128)(2,1)S(1)}, u32[]{:S(2)}, u32[]{:S(2)}) collective-permute-start(f16[8,12,256]{2,1,0:T(8,128)(2,1)S(1)} %get-tuple-element.40), channel_id=1, source_target_pairs={{0,4},{1,5},{2,6},{3,7},{4,0},{5,1},{6,2},{7,3},{8,12},{9,13},{10,... | collective-permute-start | bytes 147464 | tf_op jit(solution)/shard_map/ppermute | solution.py:214
  16.2 5.2 %collective-permute-start.3 = (f16[8,12,256]{2,1,0:T(8,128)(2,1)S(1)}, f16[8,12,256]{2,1,0:T(8,128)(2,1)S(1)}, u32[]{:S(2)}, u32[]{:S(2)}) collective-permute-start(f16[8,12,256]{2,1,0:T(8,128)(2,1)S(1)} %get-tuple-element.40), channel_id=1, source_target_pairs={{0,6},{1,7},{2,4},{3,5},{4,2},{5,3},{6,0},{7,1},{8,14},{9,15},{10,... | collective-permute-start | bytes 147464 | tf_op jit(solution)/shard_map/ppermute | solution.py:214
  21.4 5.8 %collective-permute-start.4 = (f16[8,12,256]{2,1,0:T(8,128)(2,1)S(1)}, f16[8,12,256]{2,1,0:T(8,128)(2,1)S(1)}, u32[]{:S(2)}, u32[]{:S(2)}) collective-permute-start(f16[8,12,256]{2,1,0:T(8,128)(2,1)S(1)} %get-tuple-element.38), channel_id=1, source_target_pairs={{0,8},{1,9},{2,10},{3,11},{4,12},{5,13},{6,14},{7,15},{8,0},{9,1},... | collective-permute-start | bytes 147464 | tf_op jit(solution)/shard_map/ppermute | solution.py:214
  27.2 1.3 %collective-permute-start.5 = (bf16[8,12,256]{2,1,0:T(8,128)(2,1)S(1)}, bf16[8,12,256]{2,1,0:T(8,128)(2,1)S(1)}, u32[]{:S(2)}, u32[]{:S(2)}) collective-permute-start(bf16[8,12,256]{2,1,0:T(8,128)(2,1)S(1)} %fusion.own_ref), channel_id=1, source_target_pairs={{0,1},{1,0},{2,3},{3,2},{4,5},{5,4},{6,7},{7,6},{8,9},{9,8},{10,11... | collective-permute-start | bytes 147464 | tf_op jit(solution)/shard_map/ppermute | solution.py:214
  31.9 1.4 %collective-permute-start.6 = (f32[8,12,256]{2,1,0:T(8,128)S(1)}, f32[8,12,256]{2,1,0:T(8,128)S(1)}, u32[]{:S(2)}, u32[]{:S(2)}) collective-permute-start(f32[8,12,256]{2,1,0:T(8,128)S(1)} %get-tuple-element.26), channel_id=1, source_target_pairs={{0,1},{1,0},{2,3},{3,2},{4,5},{5,4},{6,7},{7,6},{8,9},{9,8},{10,11... | collective-permute-start | bytes 294920 | tf_op jit(solution)/shard_map/ppermute | solution.py:214
  33.4 4.3 %collective-permute-start.7 = (f16[8,12,256]{2,1,0:T(8,128)(2,1)S(1)}, f16[8,12,256]{2,1,0:T(8,128)(2,1)S(1)}, u32[]{:S(2)}, u32[]{:S(2)}) collective-permute-start(f16[8,12,256]{2,1,0:T(8,128)(2,1)S(1)} %get-tuple-element.36), channel_id=1, source_target_pairs={{0,2},{1,3},{2,0},{3,1},{4,6},{5,7},{6,4},{7,5},{8,10},{9,11},{10,... | collective-permute-start | bytes 147464 | tf_op jit(solution)/shard_map/ppermute | solution.py:214
  34.1 4.7 %collective-permute-start.8 = (f16[8,12,256]{2,1,0:T(8,128)(2,1)S(1)}, f16[8,12,256]{2,1,0:T(8,128)(2,1)S(1)}, u32[]{:S(2)}, u32[]{:S(2)}) collective-permute-start(f16[8,12,256]{2,1,0:T(8,128)(2,1)S(1)} %get-tuple-element.36), channel_id=1, source_target_pairs={{0,4},{1,5},{2,6},{3,7},{4,0},{5,1},{6,2},{7,3},{8,12},{9,13},{10,... | collective-permute-start | bytes 147464 | tf_op jit(solution)/shard_map/ppermute | solution.py:214
  34.5 5.7 %collective-permute-start.9 = (f16[8,12,256]{2,1,0:T(8,128)(2,1)S(1)}, f16[8,12,256]{2,1,0:T(8,128)(2,1)S(1)}, u32[]{:S(2)}, u32[]{:S(2)}) collective-permute-start(f16[8,12,256]{2,1,0:T(8,128)(2,1)S(1)} %get-tuple-element.36), channel_id=1, source_target_pairs={{0,6},{1,7},{2,4},{3,5},{4,2},{5,3},{6,0},{7,1},{8,14},{9,15},{10,... | collective-permute-start | bytes 147464 | tf_op jit(solution)/shard_map/ppermute | solution.py:214
  40.2 5.9 %collective-permute-start.10 = (f16[8,12,256]{2,1,0:T(8,128)(2,1)S(1)}, f16[8,12,256]{2,1,0:T(8,128)(2,1)S(1)}, u32[]{:S(2)}, u32[]{:S(2)}) collective-permute-start(f16[8,12,256]{2,1,0:T(8,128)(2,1)S(1)} %multiply_convert_fusion), channel_id=1, source_target_pairs={{0,8},{1,9},{2,10},{3,11},{4,12},{5,13},{6,14},{7,15},{8,0},{9,1},... | collective-permute-start | bytes 147464 | tf_op jit(solution)/shard_map/ppermute | solution.py:214
  46.3 1.3 %collective-permute-start.11 = (bf16[8,12,256]{2,1,0:T(8,128)(2,1)S(1)}, bf16[8,12,256]{2,1,0:T(8,128)(2,1)S(1)}, u32[]{:S(2)}, u32[]{:S(2)}) collective-permute-start(bf16[8,12,256]{2,1,0:T(8,128)(2,1)S(1)} %get-tuple-element.34.own_ref), channel_id=1, source_target_pairs={{0,1},{1,0},{2,3},{3,2},{4,5},{5,4},{6,7},{7,6},{8,9},{9,8},{10,11... | collective-permute-start | bytes 147464 | tf_op jit(solution)/shard_map/ppermute | solution.py:214
  51.0 1.4 %collective-permute-start.12 = (f32[8,12,256]{2,1,0:T(8,128)S(1)}, f32[8,12,256]{2,1,0:T(8,128)S(1)}, u32[]{:S(2)}, u32[]{:S(2)}) collective-permute-start(f32[8,12,256]{2,1,0:T(8,128)S(1)} %get-tuple-element.29), channel_id=1, source_target_pairs={{0,1},{1,0},{2,3},{3,2},{4,5},{5,4},{6,7},{7,6},{8,9},{9,8},{10,11... | collective-permute-start | bytes 294920 | tf_op jit(solution)/shard_map/ppermute | solution.py:214
  52.4 4.0 %collective-permute-start.13 = (f32[2,12,256]{2,1,0:T(8,128)S(1)}, f32[2,12,256]{2,1,0:T(8,128)S(1)}, u32[]{:S(2)}, u32[]{:S(2)}) collective-permute-start(f32[2,12,256]{2,1,0:T(8,128)S(1)} %get-tuple-element.42), channel_id=1, source_target_pairs={{0,2},{1,3},{2,0},{3,1},{4,6},{5,7},{6,4},{7,5},{8,10},{9,11},{10,... | collective-permute-start | bytes 73736 | tf_op jit(solution)/shard_map/ppermute | solution.py:214
  52.6 3.9 %collective-permute-start.14 = (f32[2,12,256]{2,1,0:T(8,128)S(1)}, f32[2,12,256]{2,1,0:T(8,128)S(1)}, u32[]{:S(2)}, u32[]{:S(2)}) collective-permute-start(f32[2,12,256]{2,1,0:T(8,128)S(1)} %get-tuple-element.43), channel_id=1, source_target_pairs={{0,4},{1,5},{2,6},{3,7},{4,0},{5,1},{6,2},{7,3},{8,12},{9,13},{10,... | collective-permute-start | bytes 73736 | tf_op jit(solution)/shard_map/ppermute | solution.py:214
  54.3 4.8 %collective-permute-start.15 = (f32[2,12,256]{2,1,0:T(8,128)S(1)}, f32[2,12,256]{2,1,0:T(8,128)S(1)}, u32[]{:S(2)}, u32[]{:S(2)}) collective-permute-start(f32[2,12,256]{2,1,0:T(8,128)S(1)} %get-tuple-element.44), channel_id=1, source_target_pairs={{0,6},{1,7},{2,4},{3,5},{4,2},{5,3},{6,0},{7,1},{8,14},{9,15},{10,... | collective-permute-start | bytes 73736 | tf_op jit(solution)/shard_map/ppermute | solution.py:214
  59.1 4.7 %collective-permute-start.16 = (f32[1,12,256]{2,1,0:T(8,128)S(1)}, f32[1,12,256]{2,1,0:T(8,128)S(1)}, u32[]{:S(2)}, u32[]{:S(2)}) collective-permute-start(f32[1,12,256]{2,1,0:T(8,128)S(1)} %constant_dynamic-slice_fusion), channel_id=1, source_target_pairs={{0,8},{1,9},{2,10},{3,11},{4,12},{5,13},{6,14},{7,15},{8,0},{9,1},... | collective-permute-start | bytes 36872 | tf_op jit(solution)/shard_map/ppermute | solution.py:214

commit v3 on v2

v3 whole, which is shorter than its diff:
```python
import functools

import jax
import jax.numpy as jnp
from jax import lax
from jax.experimental import pallas as pl
from jax.experimental.pallas import tpu as pltpu
from jax.sharding import PartitionSpec as P

PATHS_PER = 8
ITERS = 3
CHUNKS = 8
VMEM_LIMIT = 40 * 2**20
F32 = jnp.float32
BF16 = jnp.bfloat16


def spec(space):
    return pl.BlockSpec(memory_space=space)


def forward(row_ref, col_ref, live, tiles_v, ex, accs, wait=None):
    slots = tiles_v.shape[0]
    half = (accs[0].shape[0] - 1) // 2
    for acc in accs:
        acc[...] = jnp.zeros_like(acc)
    for n in range(slots):
        if wait is not None:
            wait(n)
        acc = accs[n % 2]
        col = col_ref[n]
        place = jnp.where(n < live, (col & 1) * half + (col >> 1), 2 * half)
        acc[place] += jnp.dot(ex[row_ref[n]], tiles_v[n], preferred_element_type=F32)


def emit(me, cap, accs, keep_ref, send_ref):
    half = keep_ref.shape[1]
    core = me & 1
    mine = pl.ds(core * half, half)
    theirs = pl.ds((1 - core) * half, half)
    send_ref[...] = jnp.swapaxes(accs[0][theirs] + accs[1][theirs], 0, 1)
    keep = jnp.swapaxes(accs[0][mine] + accs[1][mine], 0, 1)
    place = lax.broadcasted_iota(jnp.int32, keep.shape, 1)
    keep_ref[...] = keep - jnp.where(place == (me >> 1), cap, 0.0)


def first_kernel(
    count_ref, row_hbm, col_hbm, cap_hbm, cost_hbm, tiles_hbm, keep_ref, send_ref, tiles_v,
    row_s, col_s, cap_v, cost_v, ex, acc0, acc1, small_sems, sems,
):
    me = lax.axis_index("comm")
    size = tiles_v.shape[0] // CHUNKS
    pairs = ((cost_hbm, cost_v), (row_hbm, row_s), (col_hbm, col_s), (cap_hbm, cap_v))
    small = [pltpu.make_async_copy(src, dst, small_sems.at[k]) for k, (src, dst) in enumerate(pairs)]
    for copy in small:
        copy.start()
    copies = []
    for k in range(CHUNKS):
        part = pl.ds(k * size, size)
        copies.append(pltpu.make_async_copy(tiles_hbm.at[part], tiles_v.at[part], sems.at[k]))
        copies[-1].start()
    for copy in small:
        copy.wait()
    flows = jnp.maximum(0.0, -0.5 * (cost_v[...] - 1.0))
    ex[...] = jnp.swapaxes(2.0 * flows, 0, 1).astype(BF16)

    def wait(n):
        if n % size == 0:
            copies[n // size].wait()

    accs = (acc0, acc1)
    forward(row_s, col_s, count_ref[0], tiles_v, ex, accs, wait)
    emit(me, cap_v[...], accs, keep_ref, send_ref)


def next_kernel(
    row_ref, col_ref, count_ref, cap_ref, base_ref, flows_ref, own_ref, other_ref, tiles_v,
    keep_ref, send_ref, new_ref, ex, acc0, acc1, grad0, grad1, duals,
):
    me = lax.axis_index("comm")
    live = count_ref[0]
    half = own_ref.shape[1]
    core = me & 1
    own = jnp.swapaxes(own_ref[...].astype(F32), 0, 1)
    other = jnp.swapaxes(other_ref[...].astype(F32), 0, 1)
    duals[pl.ds(core * half, half)] = own.astype(BF16)
    duals[pl.ds((1 - core) * half, half)] = other.astype(BF16)
    grads = (grad0, grad1)
    for grad in grads:
        grad[...] = jnp.zeros_like(grad)
    blocks = base_ref.shape[1]
    for n in range(tiles_v.shape[0]):
        grad = grads[n % 2]
        col = col_ref[n]
        row = jnp.where(n < live, row_ref[n], blocks)
        grad[row] += lax.dot_general(
            duals[(col & 1) * half + (col >> 1)], tiles_v[n], (((1,), (1,)), ((), ())),
            preferred_element_type=F32,
        )
    back = jnp.swapaxes(grad0[pl.ds(0, blocks)] + grad1[pl.ds(0, blocks)], 0, 1)
    new = jnp.maximum(0.0, base_ref[...] - 0.5 * back)
    new_ref[...] = new
    ex[...] = jnp.swapaxes(2.0 * new - flows_ref[...], 0, 1).astype(BF16)
    accs = (acc0, acc1)
    forward(row_ref, col_ref, live, tiles_v, ex, accs)
    emit(me, cap_ref[...], accs, keep_ref, send_ref)


def commodity_matrix(paths):
    path = lax.broadcasted_iota(jnp.int32, (paths, paths // PATHS_PER), 0)
    low = lax.broadcasted_iota(jnp.int32, (paths, paths // PATHS_PER), 1) * PATHS_PER
    return ((path >= low) & (path < low + PATHS_PER)).astype(F32)


def demand_kernel(sweep, *refs):
    refs = list(refs)
    cost_ref, demand_ref = refs[:2]
    shape = cost_ref.shape
    paths = shape[2]
    if sweep == 0:
        dd_ref, base_ref, flows_ref = refs[2:]
        flows_ref[...] = jnp.maximum(0.0, -0.5 * (cost_ref[...] - 1.0))
    elif sweep < ITERS - 1:
        old_dd_ref, old_ref, flows_ref, dd_ref, base_ref = refs[2:]
    else:
        old_dd_ref, old_ref, flows_ref, dd_ref = refs[2:]
    which = commodity_matrix(paths)
    ex = 2.0 * flows_ref[...]
    if sweep > 0:
        ex = ex - old_ref[...]
    per = jnp.dot(
        ex.reshape(-1, paths).astype(BF16), which.astype(BF16), preferred_element_type=F32
    )
    dd = 0.2 * (per.reshape(demand_ref.shape) - demand_ref[...])
    if sweep > 0:
        dd = old_dd_ref[...] + dd
    dd = jnp.maximum(0.0, dd)
    dd_ref[...] = dd
    if sweep < ITERS - 1:
        wide = lax.dot_general(
            dd.reshape(-1, paths // PATHS_PER), which, (((1,), (1,)), ((), ())),
            precision=lax.Precision.HIGHEST, preferred_element_type=F32,
        )
        base_ref[...] = flows_ref[...] - 0.5 * (cost_ref[...] - 1.0 + wide.reshape(shape))


def per_device(cost, demand, capacity, tiles, tile_row, tile_col, tile_count):
    slots, paths, links = tiles.shape
    blocks, intervals, _ = cost.shape
    cost, demand, capacity = (jnp.swapaxes(x, 0, 1) for x in (cost, demand, capacity))
    n_dev = lax.axis_size("comm")
    link_blocks = n_dev * capacity.shape[1]
    half = link_blocks // 2
    me = lax.axis_index("comm")

    V, S, A = pltpu.VMEM, pltpu.SMEM, pl.ANY
    params = pltpu.CompilerParams(vmem_limit_bytes=VMEM_LIMIT)
    halves = jax.ShapeDtypeStruct((intervals, half, links), F32)
    by_block = (blocks, intervals, paths)
    per_path = jax.ShapeDtypeStruct(cost.shape, F32)
    per_comm = jax.ShapeDtypeStruct(demand.shape, F32)
    passes = 2 * slots * 16 * paths * links
    acc_scratch = [V((link_blocks + 1, intervals, links), F32)] * 2
    grad_scratch = [V((blocks + 1, intervals, paths), F32)] * 2

    in_hbm = functools.partial(pltpu.with_memory_space_constraint, memory_space=pltpu.HBM)
    index = (tile_row, tile_col)
    keep, send, tiles_v, *index = pl.pallas_call(
        first_kernel,
        out_shape=(halves, halves, V(tiles.shape, BF16)) + tuple(S(x.shape, x.dtype) for x in index),
        in_specs=[spec(S)] + [spec(pltpu.HBM)] * 5,
        out_specs=(spec(V),) * 3 + (spec(S),) * 2,
        scratch_shapes=[V(capacity.shape, F32), V(cost.shape, F32), V(by_block, BF16)]
        + acc_scratch
        + [pltpu.SemaphoreType.DMA((4,)), pltpu.SemaphoreType.DMA((CHUNKS,))],
        compiler_params=params,
        cost_estimate=pl.CostEstimate(
            flops=passes, bytes_accessed=tiles.size * 2, transcendentals=0
        ),
        name="first_forward",
    )(tile_count, *(in_hbm(x) for x in (*index, capacity, cost, tiles)))

    following = pl.pallas_call(
        next_kernel,
        out_shape=(halves, halves, per_path),
        in_specs=[spec(S)] * 3 + [spec(V)] * 6,
        out_specs=(spec(V),) * 3,
        scratch_shapes=[V(by_block, BF16)]
        + acc_scratch
        + grad_scratch
        + [V((link_blocks, intervals, links), BF16)],
        compiler_params=params,
        cost_estimate=pl.CostEstimate(
            flops=2 * passes, bytes_accessed=tiles.size * 2, transcendentals=0
        ),
        name="adjoint_forward",
    )

    def demand_step(sweep, *args):
        outs = ((per_comm, per_path, per_path), (per_comm, per_path), (per_comm,))
        outs = outs[0 if sweep == 0 else 2 if sweep == ITERS - 1 else 1]
        return pl.pallas_call(
            functools.partial(demand_kernel, sweep),
            out_shape=outs,
            in_specs=[spec(V)] * len(args),
            out_specs=(spec(V),) * len(outs),
            compiler_params=params,
            cost_estimate=pl.CostEstimate(
                flops=10**6, bytes_accessed=4 * cost.size * 4, transcendentals=0
            ),
            name="demand_step",
        )(*args)

    def swap(x, bit):
        return lax.ppermute(x, "comm", [(i, i ^ bit) for i in range(n_dev)])

    stages = []
    bit = 2
    while bit < n_dev:
        stages.append((bit, min(4, n_dev // bit)))
        bit *= 4

    def sum_all(total):
        for bit, size in stages:
            sent = (total * (1.0 / n_dev)).astype(jnp.float16)
            parts = [swap(sent, bit * d) for d in range(1, size)]
            for part in parts:
                total = total + part.astype(F32) * n_dev
        return total

    def scatter(total):
        for bit, size in stages:
            here = (me // bit) % size
            split = total.reshape(total.shape[0], -1, size, total.shape[2])
            pick = lambda x, i: lax.dynamic_index_in_dim(x, i, 2, keepdims=False)
            sent = (split * (1.0 / n_dev)).astype(jnp.float16)
            parts = [swap(pick(sent, here ^ d), bit * d) for d in range(1, size)]
            total = pick(split, here)
            for part in parts:
                total = total + part.astype(F32) * n_dev
        return total

    dd = flows = old = None
    link_duals = jnp.zeros(halves.shape, F32)
    for sweep in range(ITERS):
        total = keep + swap(send, 1)
        if sweep == 0:
            dd, base, flows = demand_step(0, cost, demand)
        elif sweep < ITERS - 1:
            dd, base = demand_step(sweep, cost, demand, dd, old, flows)
        else:
            (dd,) = demand_step(sweep, cost, demand, dd, old, flows)
            break
        link_duals = jnp.maximum(0.0, link_duals + 0.08 * sum_all(total))
        rounded = link_duals.astype(BF16)
        keep, send, new = following(
            *index, tile_count, capacity, base, flows, rounded, swap(rounded, 1), tiles_v
        )
        old, flows = flows, new
    own_duals = lax.dynamic_index_in_dim(link_duals, me // 2, 1, keepdims=True)
    own_duals = jnp.maximum(0.0, own_duals + 0.08 * scatter(total))
    return tuple(jnp.swapaxes(x, 0, 1) for x in (flows, own_duals, dd))


def solution(mesh):
    in_specs = (P(("groups", "comm"), None, None),) * 4 + (P(("groups", "comm")),) * 3
    out_specs = (P(("groups", "comm"), None, None),) * 3
    return jax.shard_map(
        per_device, mesh=mesh, in_specs=in_specs, out_specs=out_specs, check_vma=False
    )
```

time: 64.7 us -> 58.9 us (0.910)
  local copies, waits for them, and re-layouts: 8.03 us -> 1.01 us
  Pallas kernels: 11 us -> 12.8 us
  starting transfers between devices: 20.9 us -> 20.2 us
  other arithmetic: 0.33 us -> 1.02 us
    unnamed x14 -> x8, local copies, waits for them, and re-layouts: 8 us -> 0.94 us
    pallas_call x1, Pallas kernels: 2.93 us -> 4.7 us  [per_device(): pl.pallas_call(first_kernel, out_shape=(halves, halves, V(tiles.shape, BF...]
    ppermute x17, starting transfers between devices: 20.9 us -> 20.2 us  [swap(): return lax.ppermute(x, 'comm', [(i, i ^ bit) for i in range(n_dev)])]
  transfers between devices with their start and end apart: 17 -> 17, of which waited for: 17 -> 17; matrix products, arithmetic and copies ran while one was open for 2% -> 0% of each run, Pallas kernels for 2% -> 3%
where the time goes in v3:
time: 58.9 us; the launch traced here: 58.7 us
  waiting for transfers between devices  22.2 us (38%)
  starting transfers between devices  20.2 us (34%)
  Pallas kernels  12.8 us (22%)
  between operations  1.48 us (3%)
  other arithmetic  1.02 us (2%)
  local copies, waits for them, and re-layouts  1.01 us (2%)
    ppermute x17, waiting for transfers between devices, swap(): return lax.ppermute(x, 'comm', [(i, i ^ bit) for i in range(n_dev)])  22.2 us
    ppermute x17, starting transfers between devices, swap(): return lax.ppermute(x, 'comm', [(i, i ^ bit) for i in range(n_dev)])  20.2 us
    pallas_call x2, Pallas kernels, per_device(): following(*index, tile_count, capacity, base, flows, rounded, swap(rounde...  6.35 us
    pallas_call x1, Pallas kernels, per_device(): pl.pallas_call(first_kernel, out_shape=(halves, halves, V(tiles.shape, BF...  4.7 us
    pallas_call x3, Pallas kernels, demand_step(): pl.pallas_call(functools.partial(demand_kernel, sweep), out_shape=outs, i...  1.73 us
  transfers between devices with their start and end apart: 17, of which 17 were waited for; matrix products, arithmetic and copies ran while one was open for 0% of the time, Pallas kernels for 3%

profile of v3, /device:TPU:0, one launch (start us, length us, event | category | flops | bytes accessed | tf_op | source)
XLA Modules:
  0.0 58.7 jit_solution(18009121741699563598)
XLA Ops:
  1.4 4.7 %first_forward.1 = (f32[12,8,256]{2,1,0:T(8,128)S(1)}, f32[12,8,256]{2,1,0:T(8,128)S(1)}, bf16[48,256,256]{2,1,0:T(8,128)(2,1)S(1)}, s32[48]{0:T(128)S(4)}, s32[48]{0:T(128)S(4)}) custom-call(s32[1]{0:T(128)S(6)} %copy.14.count_ref, s32[48]{0:T(128)} %row_hbm.1, s32[48]{0:T(128)} %col_hbm.1, f32[12,1,256]{2,1,0:T(1,128)} %bitcast.27, ...), custom_call_target="tpu_custom_call" | custom-call | flops 100663296 | bytes 6291456 | tf_op jit(solution)/shard_map/first_forward/pallas_call | solution.py:168
  6.1 0.5 collective-permute-start
  6.6 0.9 %collective-permute-done = f32[12,8,256]{2,1,0:T(8,128)S(1)} collective-permute-done((f32[12,8,256]{2,1,0:T(8,128)S(1)}, f32[12,8,256]{2,1,0:T(8,128)S(1)}, u32[]{:S(2)}, u32[]{:S(2)}) %collective-permute-start) | collective-permute-done | bytes 98336 | tf_op jit(solution)/shard_map/ppermute | solution.py:215
  7.5 2.9 %collective-permute-start.1 = (f16[12,8,256]{2,1,0:T(8,128)(2,1)S(1)}, f16[12,8,256]{2,1,0:T(8,128)(2,1)S(1)}, u32[]{:S(2)}, u32[]{:S(2)}) collective-permute-start(f16[12,8,256]{2,1,0:T(8,128)(2,1)S(1)} %get-tuple-element.41), channel_id=1, source_target_pairs={{0,2},{1,3},{2,0},{3,1},{4,6},{5,7},{6,4},{7,5},{8,10},{9,11},{10,... | collective-permute-start | bytes 147464 | tf_op jit(solution)/shard_map/ppermute | solution.py:215
  10.5 1.6 %collective-permute-start.2 = (f16[12,8,256]{2,1,0:T(8,128)(2,1)S(1)}, f16[12,8,256]{2,1,0:T(8,128)(2,1)S(1)}, u32[]{:S(2)}, u32[]{:S(2)}) collective-permute-start(f16[12,8,256]{2,1,0:T(8,128)(2,1)S(1)} %get-tuple-element.41), channel_id=1, source_target_pairs={{0,4},{1,5},{2,6},{3,7},{4,0},{5,1},{6,2},{7,3},{8,12},{9,13},{10,... | collective-permute-start | bytes 147464 | tf_op jit(solution)/shard_map/ppermute | solution.py:215
  12.1 0.5 collective-permute-done.1
  12.5 2.4 %collective-permute-done.2 = f16[12,8,256]{2,1,0:T(8,128)(2,1)S(1)} collective-permute-done((f16[12,8,256]{2,1,0:T(8,128)(2,1)S(1)}, f16[12,8,256]{2,1,0:T(8,128)(2,1)S(1)}, u32[]{:S(2)}, u32[]{:S(2)}) %collective-permute-start.2) | collective-permute-done | bytes 49184 | tf_op jit(solution)/shard_map/ppermute | solution.py:215
  14.9 2.1 %collective-permute-done.3 = f16[12,8,256]{2,1,0:T(8,128)(2,1)S(1)} collective-permute-done((f16[12,8,256]{2,1,0:T(8,128)(2,1)S(1)}, f16[12,8,256]{2,1,0:T(8,128)(2,1)S(1)}, u32[]{:S(2)}, u32[]{:S(2)}) %collective-permute-start.3) | collective-permute-done | bytes 49184 | tf_op jit(solution)/shard_map/ppermute | solution.py:215
  17.1 2.7 %collective-permute-start.4 = (f16[12,8,256]{2,1,0:T(8,128)(2,1)S(1)}, f16[12,8,256]{2,1,0:T(8,128)(2,1)S(1)}, u32[]{:S(2)}, u32[]{:S(2)}) collective-permute-start(f16[12,8,256]{2,1,0:T(8,128)(2,1)S(1)} %get-tuple-element.39), channel_id=1, source_target_pairs={{0,8},{1,9},{2,10},{3,11},{4,12},{5,13},{6,14},{7,15},{8,0},{9,1},... | collective-permute-start | bytes 147464 | tf_op jit(solution)/shard_map/ppermute | solution.py:215
  19.7 2.8 %collective-permute-done.4 = f16[12,8,256]{2,1,0:T(8,128)(2,1)S(1)} collective-permute-done((f16[12,8,256]{2,1,0:T(8,128)(2,1)S(1)}, f16[12,8,256]{2,1,0:T(8,128)(2,1)S(1)}, u32[]{:S(2)}, u32[]{:S(2)}) %collective-permute-start.4) | collective-permute-done | bytes 49184 | tf_op jit(solution)/shard_map/ppermute | solution.py:215
  23.1 0.7 %collective-permute-done.5.other_ref = bf16[12,8,256]{2,1,0:T(8,128)(2,1)S(1)} collective-permute-done((bf16[12,8,256]{2,1,0:T(8,128)(2,1)S(1)}, bf16[12,8,256]{2,1,0:T(8,128)(2,1)S(1)}, u32[]{:S(2)}, u32[]{:S(2)}) %collective-permute-start.5) | collective-permute-done | bytes 49184 | tf_op jit(solution)/shard_map/ppermute | solution.py:215
  23.9 2.9 %adjoint_forward.2 = (f32[12,8,256]{2,1,0:T(8,128)S(1)}, f32[12,8,256]{2,1,0:T(8,128)S(1)}, f32[12,16,256]{2,1,0:T(8,128)S(1)}) custom-call(s32[48]{0:T(128)S(4)} %get-tuple-element.19.row_ref, s32[48]{0:T(128)S(4)} %get-tuple-element.20.col_ref, s32[1]{0:T(128)S(6)} %copy.14.count_ref, f32[12,1,256]{2,1,0:T(1,128)S(1)} %bitcast.28, ...), custom_call_target="tpu_custom_call" | custom-call | flops 201326592 | bytes 6291456 | tf_op jit(solution)/shard_map/adjoint_forward/pallas_call | solution.py:256
  27.0 1.1 %collective-permute-done.6 = f32[12,8,256]{2,1,0:T(8,128)S(1)} collective-permute-done((f32[12,8,256]{2,1,0:T(8,128)S(1)}, f32[12,8,256]{2,1,0:T(8,128)S(1)}, u32[]{:S(2)}, u32[]{:S(2)}) %collective-permute-start.6) | collective-permute-done | bytes 98336 | tf_op jit(solution)/shard_map/ppermute | solution.py:215
  28.2 0.7 %collective-permute-start.7 = (f16[12,8,256]{2,1,0:T(8,128)(2,1)S(1)}, f16[12,8,256]{2,1,0:T(8,128)(2,1)S(1)}, u32[]{:S(2)}, u32[]{:S(2)}) collective-permute-start(f16[12,8,256]{2,1,0:T(8,128)(2,1)S(1)} %get-tuple-element.37), channel_id=1, source_target_pairs={{0,2},{1,3},{2,0},{3,1},{4,6},{5,7},{6,4},{7,5},{8,10},{9,11},{10,... | collective-permute-start | bytes 147464 | tf_op jit(solution)/shard_map/ppermute | solution.py:215
  29.1 2.7 %collective-permute-start.9 = (f16[12,8,256]{2,1,0:T(8,128)(2,1)S(1)}, f16[12,8,256]{2,1,0:T(8,128)(2,1)S(1)}, u32[]{:S(2)}, u32[]{:S(2)}) collective-permute-start(f16[12,8,256]{2,1,0:T(8,128)(2,1)S(1)} %get-tuple-element.37), channel_id=1, source_target_pairs={{0,6},{1,7},{2,4},{3,5},{4,2},{5,3},{6,0},{7,1},{8,14},{9,15},{10,... | collective-permute-start | bytes 147464 | tf_op jit(solution)/shard_map/ppermute | solution.py:215
  31.8 0.6 %collective-permute-done.7 = f16[12,8,256]{2,1,0:T(8,128)(2,1)S(1)} collective-permute-done((f16[12,8,256]{2,1,0:T(8,128)(2,1)S(1)}, f16[12,8,256]{2,1,0:T(8,128)(2,1)S(1)}, u32[]{:S(2)}, u32[]{:S(2)}) %collective-permute-start.7) | collective-permute-done | bytes 49184 | tf_op jit(solution)/shard_map/ppermute | solution.py:215
  32.4 0.9 %collective-permute-done.8 = f16[12,8,256]{2,1,0:T(8,128)(2,1)S(1)} collective-permute-done((f16[12,8,256]{2,1,0:T(8,128)(2,1)S(1)}, f16[12,8,256]{2,1,0:T(8,128)(2,1)S(1)}, u32[]{:S(2)}, u32[]{:S(2)}) %collective-permute-start.8) | collective-permute-done | bytes 49184 | tf_op jit(solution)/shard_map/ppermute | solution.py:215
  33.3 1.1 %collective-permute-done.9 = f16[12,8,256]{2,1,0:T(8,128)(2,1)S(1)} collective-permute-done((f16[12,8,256]{2,1,0:T(8,128)(2,1)S(1)}, f16[12,8,256]{2,1,0:T(8,128)(2,1)S(1)}, u32[]{:S(2)}, u32[]{:S(2)}) %collective-permute-start.9) | collective-permute-done | bytes 49184 | tf_op jit(solution)/shard_map/ppermute | solution.py:215
  34.4 2.2 %collective-permute-start.10 = (f16[12,8,256]{2,1,0:T(8,128)(2,1)S(1)}, f16[12,8,256]{2,1,0:T(8,128)(2,1)S(1)}, u32[]{:S(2)}, u32[]{:S(2)}) collective-permute-start(f16[12,8,256]{2,1,0:T(8,128)(2,1)S(1)} %multiply_convert_fusion.1), channel_id=1, source_target_pairs={{0,8},{1,9},{2,10},{3,11},{4,12},{5,13},{6,14},{7,15},{8,0},{9,1},... | collective-permute-start | bytes 147464 | tf_op jit(solution)/shard_map/ppermute | solution.py:215
  36.6 2.8 %collective-permute-done.10 = f16[12,8,256]{2,1,0:T(8,128)(2,1)S(1)} collective-permute-done((f16[12,8,256]{2,1,0:T(8,128)(2,1)S(1)}, f16[12,8,256]{2,1,0:T(8,128)(2,1)S(1)}, u32[]{:S(2)}, u32[]{:S(2)}) %collective-permute-start.10) | collective-permute-done | bytes 49184 | tf_op jit(solution)/shard_map/ppermute | solution.py:215
  40.1 0.8 %collective-permute-done.11.other_ref = bf16[12,8,256]{2,1,0:T(8,128)(2,1)S(1)} collective-permute-done((bf16[12,8,256]{2,1,0:T(8,128)(2,1)S(1)}, bf16[12,8,256]{2,1,0:T(8,128)(2,1)S(1)}, u32[]{:S(2)}, u32[]{:S(2)}) %collective-permute-start.11) | collective-permute-done | bytes 49184 | tf_op jit(solution)/shard_map/ppermute | solution.py:215
  40.8 3.4 %adjoint_forward.3 = (f32[12,8,256]{2,1,0:T(8,128)S(1)}, f32[12,8,256]{2,1,0:T(8,128)S(1)}, f32[12,16,256]{2,1,0:T(8,128)}) custom-call(s32[48]{0:T(128)S(4)} %get-tuple-element.19.row_ref, s32[48]{0:T(128)S(4)} %get-tuple-element.20.col_ref, s32[1]{0:T(128)S(6)} %copy.14.count_ref, f32[12,1,256]{2,1,0:T(1,128)S(1)} %bitcast.29, ...), custom_call_target="tpu_custom_call" | custom-call | flops 201326592 | bytes 6291456 | tf_op jit(solution)/shard_map/adjoint_forward/pallas_call | solution.py:256
  44.4 1.1 %collective-permute-done.12 = f32[12,8,256]{2,1,0:T(8,128)S(1)} collective-permute-done((f32[12,8,256]{2,1,0:T(8,128)S(1)}, f32[12,8,256]{2,1,0:T(8,128)S(1)}, u32[]{:S(2)}, u32[]{:S(2)}) %collective-permute-start.12) | collective-permute-done | bytes 98336 | tf_op jit(solution)/shard_map/ppermute | solution.py:215
  45.7 1.1 %collective-permute-start.13 = (f16[12,2,256]{2,1,0:T(2,128)(2,1)S(1)}, f16[12,2,256]{2,1,0:T(2,128)(2,1)S(1)}, u32[]{:S(2)}, u32[]{:S(2)}) collective-permute-start(f16[12,2,256]{2,1,0:T(2,128)(2,1)S(1)} %get-tuple-element.45), channel_id=1, source_target_pairs={{0,2},{1,3},{2,0},{3,1},{4,6},{5,7},{6,4},{7,5},{8,10},{9,11},{10,... | collective-permute-start | bytes 36872 | tf_op jit(solution)/shard_map/ppermute | solution.py:215
  46.8 1.9 %collective-permute-start.14 = (f16[12,2,256]{2,1,0:T(2,128)(2,1)S(1)}, f16[12,2,256]{2,1,0:T(2,128)(2,1)S(1)}, u32[]{:S(2)}, u32[]{:S(2)}) collective-permute-start(f16[12,2,256]{2,1,0:T(2,128)(2,1)S(1)} %get-tuple-element.47), channel_id=1, source_target_pairs={{0,4},{1,5},{2,6},{3,7},{4,0},{5,1},{6,2},{7,3},{8,12},{9,13},{10,... | collective-permute-start | bytes 36872 | tf_op jit(solution)/shard_map/ppermute | solution.py:215
  48.8 0.5 collective-permute-start.15
  49.5 1.0 %collective-permute-done.14 = f16[12,2,256]{2,1,0:T(2,128)(2,1)S(1)} collective-permute-done((f16[12,2,256]{2,1,0:T(2,128)(2,1)S(1)}, f16[12,2,256]{2,1,0:T(2,128)(2,1)S(1)}, u32[]{:S(2)}, u32[]{:S(2)}) %collective-permute-start.14) | collective-permute-done | bytes 12320 | tf_op jit(solution)/shard_map/ppermute | solution.py:215
  50.5 2.8 %collective-permute-done.15 = f16[12,2,256]{2,1,0:T(2,128)(2,1)S(1)} collective-permute-done((f16[12,2,256]{2,1,0:T(2,128)(2,1)S(1)}, f16[12,2,256]{2,1,0:T(2,128)(2,1)S(1)}, u32[]{:S(2)}, u32[]{:S(2)}) %collective-permute-start.15) | collective-permute-done | bytes 12320 | tf_op jit(solution)/shard_map/ppermute | solution.py:215
  53.4 2.7 %collective-permute-start.16 = (f16[12,1,256]{2,1,0:T(2,128)(2,1)S(1)}, f16[12,1,256]{2,1,0:T(2,128)(2,1)S(1)}, u32[]{:S(2)}, u32[]{:S(2)}) collective-permute-start(f16[12,1,256]{2,1,0:T(2,128)(2,1)S(1)} %fusion.3), channel_id=1, source_target_pairs={{0,8},{1,9},{2,10},{3,11},{4,12},{5,13},{6,14},{7,15},{8,0},{9,1},... | collective-permute-start | bytes 18440 | tf_op jit(solution)/shard_map/ppermute | solution.py:215
  56.1 0.9 %copy-done.2 = f32[12,16,256]{2,1,0:T(8,128)S(1)} copy-done((f32[12,16,256]{2,1,0:T(8,128)S(1)}, f32[12,16,256]{2,1,0:T(8,128)}, u32[]{:S(2)}) %copy-start.2) | copy-done | bytes 196632
  57.0 0.8 %demand_step.5 = f32[12,16,32]{2,1,0:T(8,128)} custom-call(f32[12,16,256]{2,1,0:T(8,128)S(1)} %bitcast.22, f32[12,16,32]{2,1,0:T(8,128)S(1)} %bitcast.25, f32[12,16,32]{2,1,0:T(8,128)S(1)} %get-tuple-element.34.refs_2_, f32[12,16,256]{2,1,0:T(8,128)S(1)} %get-tuple-element.27.refs_4_.flows_ref.refs_3_, f32[12,16,256]{2,1,0:T(8,128)S(1)} %copy-done.2), custom_call_target="tpu_custom_call" | custom-call | flops 1000000 | bytes 786432 | tf_op jit(solution)/shard_map/demand_step/pallas_call | solution.py:202
  58.1 0.6 %maximum_bitcast_fusion = f32[1,12,256]{2,0,1:T(1,128)} fusion(f16[12,1,256]{2,1,0:T(2,128)(2,1)S(1)} %collective-permute-done.16, f32[12,2,256]{2,1,0:T(2,128)S(1)} %fusion.2, s32[]{:T(128)S(6)} %select_n.54, f32[12,8,256]{2,1,0:T(8,128)S(1)} %get-tuple-element.36, s32[]{:T(128)S(6)} %select_n.46), kind=kLoop, calls=%fused_computation.15 | loop fusion | flops 18432 | bytes 43016 | tf_op jit(solution)/shard_map/transpose | solution.py:262
  (29 shorter events, 2.5 us)
Async XLA Ops:
  0.6 22.0 %copy-start = (f32[16,12,256]{2,0,1:T(8,128)S(1)}, f32[16,12,256]{2,0,1:T(8,128)}, u32[]{:S(2)}) copy-start(f32[16,12,256]{2,0,1:T(8,128)} %param.7) | copy-start | bytes 589828
  0.6 23.2 %copy-start.3 = (f32[1,12,256]{2,0,1:T(1,128)S(1)}, f32[1,12,256]{2,0,1:T(1,128)}, u32[]{:S(2)}) copy-start(f32[1,12,256]{2,0,1:T(1,128)} %param.9) | copy-start | bytes 36868
  0.7 22.0 %copy-start.1 = (f32[16,12,32]{2,0,1:T(8,128)S(1)}, f32[16,12,32]{2,0,1:T(8,128)}, u32[]{:S(2)}) copy-start(f32[16,12,32]{2,0,1:T(8,128)} %param.8) | copy-start | bytes 73732
  6.1 1.5 %collective-permute-start = (f32[12,8,256]{2,1,0:T(8,128)S(1)}, f32[12,8,256]{2,1,0:T(8,128)S(1)}, u32[]{:S(2)}, u32[]{:S(2)}) collective-permute-start(f32[12,8,256]{2,1,0:T(8,128)S(1)} %get-tuple-element.25), channel_id=1, source_target_pairs={{0,1},{1,0},{2,3},{3,2},{4,5},{5,4},{6,7},{7,6},{8,9},{9,8},{10,11... | collective-permute-start | bytes 294920 | tf_op jit(solution)/shard_map/ppermute | solution.py:215
  7.5 5.0 %collective-permute-start.1 = (f16[12,8,256]{2,1,0:T(8,128)(2,1)S(1)}, f16[12,8,256]{2,1,0:T(8,128)(2,1)S(1)}, u32[]{:S(2)}, u32[]{:S(2)}) collective-permute-start(f16[12,8,256]{2,1,0:T(8,128)(2,1)S(1)} %get-tuple-element.41), channel_id=1, source_target_pairs={{0,2},{1,3},{2,0},{3,1},{4,6},{5,7},{6,4},{7,5},{8,10},{9,11},{10,... | collective-permute-start | bytes 147464 | tf_op jit(solution)/shard_map/ppermute | solution.py:215
  10.5 4.5 %collective-permute-start.2 = (f16[12,8,256]{2,1,0:T(8,128)(2,1)S(1)}, f16[12,8,256]{2,1,0:T(8,128)(2,1)S(1)}, u32[]{:S(2)}, u32[]{:S(2)}) collective-permute-start(f16[12,8,256]{2,1,0:T(8,128)(2,1)S(1)} %get-tuple-element.41), channel_id=1, source_target_pairs={{0,4},{1,5},{2,6},{3,7},{4,0},{5,1},{6,2},{7,3},{8,12},{9,13},{10,... | collective-permute-start | bytes 147464 | tf_op jit(solution)/shard_map/ppermute | solution.py:215
  12.1 5.0 %collective-permute-start.3 = (f16[12,8,256]{2,1,0:T(8,128)(2,1)S(1)}, f16[12,8,256]{2,1,0:T(8,128)(2,1)S(1)}, u32[]{:S(2)}, u32[]{:S(2)}) collective-permute-start(f16[12,8,256]{2,1,0:T(8,128)(2,1)S(1)} %get-tuple-element.41), channel_id=1, source_target_pairs={{0,6},{1,7},{2,4},{3,5},{4,2},{5,3},{6,0},{7,1},{8,14},{9,15},{10,... | collective-permute-start | bytes 147464 | tf_op jit(solution)/shard_map/ppermute | solution.py:215
  17.1 5.5 %collective-permute-start.4 = (f16[12,8,256]{2,1,0:T(8,128)(2,1)S(1)}, f16[12,8,256]{2,1,0:T(8,128)(2,1)S(1)}, u32[]{:S(2)}, u32[]{:S(2)}) collective-permute-start(f16[12,8,256]{2,1,0:T(8,128)(2,1)S(1)} %get-tuple-element.39), channel_id=1, source_target_pairs={{0,8},{1,9},{2,10},{3,11},{4,12},{5,13},{6,14},{7,15},{8,0},{9,1},... | collective-permute-start | bytes 147464 | tf_op jit(solution)/shard_map/ppermute | solution.py:215
  22.6 1.3 %collective-permute-start.5 = (bf16[12,8,256]{2,1,0:T(8,128)(2,1)S(1)}, bf16[12,8,256]{2,1,0:T(8,128)(2,1)S(1)}, u32[]{:S(2)}, u32[]{:S(2)}) collective-permute-start(bf16[12,8,256]{2,1,0:T(8,128)(2,1)S(1)} %fusion.own_ref), channel_id=1, source_target_pairs={{0,1},{1,0},{2,3},{3,2},{4,5},{5,4},{6,7},{7,6},{8,9},{9,8},{10,11... | collective-permute-start | bytes 147464 | tf_op jit(solution)/shard_map/ppermute | solution.py:215
  26.8 1.4 %collective-permute-start.6 = (f32[12,8,256]{2,1,0:T(8,128)S(1)}, f32[12,8,256]{2,1,0:T(8,128)S(1)}, u32[]{:S(2)}, u32[]{:S(2)}) collective-permute-start(f32[12,8,256]{2,1,0:T(8,128)S(1)} %get-tuple-element.30), channel_id=1, source_target_pairs={{0,1},{1,0},{2,3},{3,2},{4,5},{5,4},{6,7},{7,6},{8,9},{9,8},{10,11... | collective-permute-start | bytes 294920 | tf_op jit(solution)/shard_map/ppermute | solution.py:215
  28.2 4.2 %collective-permute-start.7 = (f16[12,8,256]{2,1,0:T(8,128)(2,1)S(1)}, f16[12,8,256]{2,1,0:T(8,128)(2,1)S(1)}, u32[]{:S(2)}, u32[]{:S(2)}) collective-permute-start(f16[12,8,256]{2,1,0:T(8,128)(2,1)S(1)} %get-tuple-element.37), channel_id=1, source_target_pairs={{0,2},{1,3},{2,0},{3,1},{4,6},{5,7},{6,4},{7,5},{8,10},{9,11},{10,... | collective-permute-start | bytes 147464 | tf_op jit(solution)/shard_map/ppermute | solution.py:215
  28.9 4.4 %collective-permute-start.8 = (f16[12,8,256]{2,1,0:T(8,128)(2,1)S(1)}, f16[12,8,256]{2,1,0:T(8,128)(2,1)S(1)}, u32[]{:S(2)}, u32[]{:S(2)}) collective-permute-start(f16[12,8,256]{2,1,0:T(8,128)(2,1)S(1)} %get-tuple-element.37), channel_id=1, source_target_pairs={{0,4},{1,5},{2,6},{3,7},{4,0},{5,1},{6,2},{7,3},{8,12},{9,13},{10,... | collective-permute-start | bytes 147464 | tf_op jit(solution)/shard_map/ppermute | solution.py:215
  29.1 5.3 %collective-permute-start.9 = (f16[12,8,256]{2,1,0:T(8,128)(2,1)S(1)}, f16[12,8,256]{2,1,0:T(8,128)(2,1)S(1)}, u32[]{:S(2)}, u32[]{:S(2)}) collective-permute-start(f16[12,8,256]{2,1,0:T(8,128)(2,1)S(1)} %get-tuple-element.37), channel_id=1, source_target_pairs={{0,6},{1,7},{2,4},{3,5},{4,2},{5,3},{6,0},{7,1},{8,14},{9,15},{10,... | collective-permute-start | bytes 147464 | tf_op jit(solution)/shard_map/ppermute | solution.py:215
  34.4 5.1 %collective-permute-start.10 = (f16[12,8,256]{2,1,0:T(8,128)(2,1)S(1)}, f16[12,8,256]{2,1,0:T(8,128)(2,1)S(1)}, u32[]{:S(2)}, u32[]{:S(2)}) collective-permute-start(f16[12,8,256]{2,1,0:T(8,128)(2,1)S(1)} %multiply_convert_fusion.1), channel_id=1, source_target_pairs={{0,8},{1,9},{2,10},{3,11},{4,12},{5,13},{6,14},{7,15},{8,0},{9,1},... | collective-permute-start | bytes 147464 | tf_op jit(solution)/shard_map/ppermute | solution.py:215
  39.5 1.3 %collective-permute-start.11 = (bf16[12,8,256]{2,1,0:T(8,128)(2,1)S(1)}, bf16[12,8,256]{2,1,0:T(8,128)(2,1)S(1)}, u32[]{:S(2)}, u32[]{:S(2)}) collective-permute-start(bf16[12,8,256]{2,1,0:T(8,128)(2,1)S(1)} %get-tuple-element.35.own_ref), channel_id=1, source_target_pairs={{0,1},{1,0},{2,3},{3,2},{4,5},{5,4},{6,7},{7,6},{8,9},{9,8},{10,11... | collective-permute-start | bytes 147464 | tf_op jit(solution)/shard_map/ppermute | solution.py:215
  44.3 1.3 %collective-permute-start.12 = (f32[12,8,256]{2,1,0:T(8,128)S(1)}, f32[12,8,256]{2,1,0:T(8,128)S(1)}, u32[]{:S(2)}, u32[]{:S(2)}) collective-permute-start(f32[12,8,256]{2,1,0:T(8,128)S(1)} %get-tuple-element.33), channel_id=1, source_target_pairs={{0,1},{1,0},{2,3},{3,2},{4,5},{5,4},{6,7},{7,6},{8,9},{9,8},{10,11... | collective-permute-start | bytes 294920 | tf_op jit(solution)/shard_map/ppermute | solution.py:215
  45.7 3.8 %collective-permute-start.13 = (f16[12,2,256]{2,1,0:T(2,128)(2,1)S(1)}, f16[12,2,256]{2,1,0:T(2,128)(2,1)S(1)}, u32[]{:S(2)}, u32[]{:S(2)}) collective-permute-start(f16[12,2,256]{2,1,0:T(2,128)(2,1)S(1)} %get-tuple-element.45), channel_id=1, source_target_pairs={{0,2},{1,3},{2,0},{3,1},{4,6},{5,7},{6,4},{7,5},{8,10},{9,11},{10,... | collective-permute-start | bytes 36872 | tf_op jit(solution)/shard_map/ppermute | solution.py:215
  46.8 3.7 %collective-permute-start.14 = (f16[12,2,256]{2,1,0:T(2,128)(2,1)S(1)}, f16[12,2,256]{2,1,0:T(2,128)(2,1)S(1)}, u32[]{:S(2)}, u32[]{:S(2)}) collective-permute-start(f16[12,2,256]{2,1,0:T(2,128)(2,1)S(1)} %get-tuple-element.47), channel_id=1, source_target_pairs={{0,4},{1,5},{2,6},{3,7},{4,0},{5,1},{6,2},{7,3},{8,12},{9,13},{10,... | collective-permute-start | bytes 36872 | tf_op jit(solution)/shard_map/ppermute | solution.py:215
  48.8 4.6 %collective-permute-start.15 = (f16[12,2,256]{2,1,0:T(2,128)(2,1)S(1)}, f16[12,2,256]{2,1,0:T(2,128)(2,1)S(1)}, u32[]{:S(2)}, u32[]{:S(2)}) collective-permute-start(f16[12,2,256]{2,1,0:T(2,128)(2,1)S(1)} %get-tuple-element.46), channel_id=1, source_target_pairs={{0,6},{1,7},{2,4},{3,5},{4,2},{5,3},{6,0},{7,1},{8,14},{9,15},{10,... | collective-permute-start | bytes 36872 | tf_op jit(solution)/shard_map/ppermute | solution.py:215
  53.4 4.7 %collective-permute-start.16 = (f16[12,1,256]{2,1,0:T(2,128)(2,1)S(1)}, f16[12,1,256]{2,1,0:T(2,128)(2,1)S(1)}, u32[]{:S(2)}, u32[]{:S(2)}) collective-permute-start(f16[12,1,256]{2,1,0:T(2,128)(2,1)S(1)} %fusion.3), channel_id=1, source_target_pairs={{0,8},{1,9},{2,10},{3,11},{4,12},{5,13},{6,14},{7,15},{8,0},{9,1},... | collective-permute-start | bytes 18440 | tf_op jit(solution)/shard_map/ppermute | solution.py:215
  56.1 0.9 %copy-start.2 = (f32[12,16,256]{2,1,0:T(8,128)S(1)}, f32[12,16,256]{2,1,0:T(8,128)}, u32[]{:S(2)}) copy-start(f32[12,16,256]{2,1,0:T(8,128)} %get-tuple-element.31.refs_4_) | copy-start | bytes 589828

commit v4 on v3

--- a/solution.py
+++ b/solution.py
@@ -9,7 +9,7 @@
 
 PATHS_PER = 8
 ITERS = 3
-CHUNKS = 8
+CHUNKS = 4
 VMEM_LIMIT = 40 * 2**20
 F32 = jnp.float32
 BF16 = jnp.bfloat16
@@ -223,7 +223,7 @@
     def sum_all(total):
         for bit, size in stages:
             sent = (total * (1.0 / n_dev)).astype(jnp.float16)
-            parts = [swap(sent, bit * d) for d in range(1, size)]
+            parts = [swap(sent, bit * d) for d in reversed(range(1, size))]
             for part in parts:
                 total = total + part.astype(F32) * n_dev
         return total
@@ -234,7 +234,7 @@
             split = total.reshape(total.shape[0], -1, size, total.shape[2])
             pick = lambda x, i: lax.dynamic_index_in_dim(x, i, 2, keepdims=False)
             sent = (split * (1.0 / n_dev)).astype(jnp.float16)
-            parts = [swap(pick(sent, here ^ d), bit * d) for d in range(1, size)]
+            parts = [swap(pick(sent, here ^ d), bit * d) for d in reversed(range(1, size))]
             total = pick(split, here)
             for part in parts:
                 total = total + part.astype(F32) * n_dev

time: 58.9 us -> 56 us (0.951)
  waiting for transfers between devices: 22.2 us -> 19 us
  starting transfers between devices: 20.2 us -> 21.2 us
  Pallas kernels: 12.8 us -> 12.2 us
    ppermute x17, waiting for transfers between devices: 22.2 us -> 19 us  [swap(): return lax.ppermute(x, 'comm', [(i, i ^ bit) for i in range(n_dev)])]
    ppermute x17, starting transfers between devices: 20.2 us -> 21.2 us  [swap(): return lax.ppermute(x, 'comm', [(i, i ^ bit) for i in range(n_dev)])]
where the time goes in v4:
time: 56 us; the launch traced here: 55.8 us
  starting transfers between devices  21.2 us (38%)
  waiting for transfers between devices  19 us (34%)
  Pallas kernels  12.2 us (22%)
  between operations  1.48 us (3%)
  other arithmetic  1.02 us (2%)
  local copies, waits for them, and re-layouts  1.01 us (2%)
    ppermute x17, starting transfers between devices, swap(): return lax.ppermute(x, 'comm', [(i, i ^ bit) for i in range(n_dev)])  21.2 us
    ppermute x17, waiting for transfers between devices, swap(): return lax.ppermute(x, 'comm', [(i, i ^ bit) for i in range(n_dev)])  19 us
    pallas_call x2, Pallas kernels, per_device(): following(*index, tile_count, capacity, base, flows, rounded, swap(rounde...  6.34 us
    pallas_call x1, Pallas kernels, per_device(): pl.pallas_call(first_kernel, out_shape=(halves, halves, V(tiles.shape, BF...  4.13 us
    pallas_call x3, Pallas kernels, demand_step(): pl.pallas_call(functools.partial(demand_kernel, sweep), out_shape=outs, i...  1.74 us
  transfers between devices with their start and end apart: 17, of which 17 were waited for; matrix products, arithmetic and copies ran while one was open for 0% of the time, Pallas kernels for 3%

profile of v4, /device:TPU:0, one launch (start us, length us, event | category | flops | bytes accessed | tf_op | source)
XLA Modules:
  0.0 55.8 jit_solution(11687047604178493546)
XLA Ops:
  1.4 4.1 %first_forward.1 = (f32[12,8,256]{2,1,0:T(8,128)S(1)}, f32[12,8,256]{2,1,0:T(8,128)S(1)}, bf16[48,256,256]{2,1,0:T(8,128)(2,1)S(1)}, s32[48]{0:T(128)S(4)}, s32[48]{0:T(128)S(4)}) custom-call(s32[1]{0:T(128)S(6)} %copy.14.count_ref, s32[48]{0:T(128)} %row_hbm.1, s32[48]{0:T(128)} %col_hbm.1, f32[12,1,256]{2,1,0:T(1,128)} %bitcast.27, ...), custom_call_target="tpu_custom_call" | custom-call | flops 100663296 | bytes 6291456 | tf_op jit(solution)/shard_map/first_forward/pallas_call | solution.py:168
  5.5 0.5 collective-permute-start
  6.0 0.9 %collective-permute-done = f32[12,8,256]{2,1,0:T(8,128)S(1)} collective-permute-done((f32[12,8,256]{2,1,0:T(8,128)S(1)}, f32[12,8,256]{2,1,0:T(8,128)S(1)}, u32[]{:S(2)}, u32[]{:S(2)}) %collective-permute-start) | collective-permute-done | bytes 98336 | tf_op jit(solution)/shard_map/ppermute | solution.py:215
  7.0 4.0 %collective-permute-start.1 = (f16[12,8,256]{2,1,0:T(8,128)(2,1)S(1)}, f16[12,8,256]{2,1,0:T(8,128)(2,1)S(1)}, u32[]{:S(2)}, u32[]{:S(2)}) collective-permute-start(f16[12,8,256]{2,1,0:T(8,128)(2,1)S(1)} %get-tuple-element.41), channel_id=1, source_target_pairs={{0,6},{1,7},{2,4},{3,5},{4,2},{5,3},{6,0},{7,1},{8,14},{9,15},{10,... | collective-permute-start | bytes 147464 | tf_op jit(solution)/shard_map/ppermute | solution.py:215
  10.9 0.4 collective-permute-start.2
  11.6 1.4 %collective-permute-done.1 = f16[12,8,256]{2,1,0:T(8,128)(2,1)S(1)} collective-permute-done((f16[12,8,256]{2,1,0:T(8,128)(2,1)S(1)}, f16[12,8,256]{2,1,0:T(8,128)(2,1)S(1)}, u32[]{:S(2)}, u32[]{:S(2)}) %collective-permute-start.1) | collective-permute-done | bytes 49184 | tf_op jit(solution)/shard_map/ppermute | solution.py:215
  13.0 2.0 %collective-permute-done.2 = f16[12,8,256]{2,1,0:T(8,128)(2,1)S(1)} collective-permute-done((f16[12,8,256]{2,1,0:T(8,128)(2,1)S(1)}, f16[12,8,256]{2,1,0:T(8,128)(2,1)S(1)}, u32[]{:S(2)}, u32[]{:S(2)}) %collective-permute-start.2) | collective-permute-done | bytes 49184 | tf_op jit(solution)/shard_map/ppermute | solution.py:215
  15.0 0.4 collective-permute-done.3
  15.5 2.7 %collective-permute-start.4 = (f16[12,8,256]{2,1,0:T(8,128)(2,1)S(1)}, f16[12,8,256]{2,1,0:T(8,128)(2,1)S(1)}, u32[]{:S(2)}, u32[]{:S(2)}) collective-permute-start(f16[12,8,256]{2,1,0:T(8,128)(2,1)S(1)} %get-tuple-element.39), channel_id=1, source_target_pairs={{0,8},{1,9},{2,10},{3,11},{4,12},{5,13},{6,14},{7,15},{8,0},{9,1},... | collective-permute-start | bytes 147464 | tf_op jit(solution)/shard_map/ppermute | solution.py:215
  18.2 2.4 %collective-permute-done.4 = f16[12,8,256]{2,1,0:T(8,128)(2,1)S(1)} collective-permute-done((f16[12,8,256]{2,1,0:T(8,128)(2,1)S(1)}, f16[12,8,256]{2,1,0:T(8,128)(2,1)S(1)}, u32[]{:S(2)}, u32[]{:S(2)}) %collective-permute-start.4) | collective-permute-done | bytes 49184 | tf_op jit(solution)/shard_map/ppermute | solution.py:215
  20.7 0.5 demand_step.3
  21.2 0.7 %collective-permute-done.5.other_ref = bf16[12,8,256]{2,1,0:T(8,128)(2,1)S(1)} collective-permute-done((bf16[12,8,256]{2,1,0:T(8,128)(2,1)S(1)}, bf16[12,8,256]{2,1,0:T(8,128)(2,1)S(1)}, u32[]{:S(2)}, u32[]{:S(2)}) %collective-permute-start.5) | collective-permute-done | bytes 49184 | tf_op jit(solution)/shard_map/ppermute | solution.py:215
  21.9 2.9 %adjoint_forward.2 = (f32[12,8,256]{2,1,0:T(8,128)S(1)}, f32[12,8,256]{2,1,0:T(8,128)S(1)}, f32[12,16,256]{2,1,0:T(8,128)S(1)}) custom-call(s32[48]{0:T(128)S(4)} %get-tuple-element.19.row_ref, s32[48]{0:T(128)S(4)} %get-tuple-element.20.col_ref, s32[1]{0:T(128)S(6)} %copy.14.count_ref, f32[12,1,256]{2,1,0:T(1,128)S(1)} %bitcast.28, ...), custom_call_target="tpu_custom_call" | custom-call | flops 201326592 | bytes 6291456 | tf_op jit(solution)/shard_map/adjoint_forward/pallas_call | solution.py:256
  25.1 1.1 %collective-permute-done.6 = f32[12,8,256]{2,1,0:T(8,128)S(1)} collective-permute-done((f32[12,8,256]{2,1,0:T(8,128)S(1)}, f32[12,8,256]{2,1,0:T(8,128)S(1)}, u32[]{:S(2)}, u32[]{:S(2)}) %collective-permute-start.6) | collective-permute-done | bytes 98336 | tf_op jit(solution)/shard_map/ppermute | solution.py:215
  26.2 1.6 %collective-permute-start.7 = (f16[12,8,256]{2,1,0:T(8,128)(2,1)S(1)}, f16[12,8,256]{2,1,0:T(8,128)(2,1)S(1)}, u32[]{:S(2)}, u32[]{:S(2)}) collective-permute-start(f16[12,8,256]{2,1,0:T(8,128)(2,1)S(1)} %get-tuple-element.37), channel_id=1, source_target_pairs={{0,6},{1,7},{2,4},{3,5},{4,2},{5,3},{6,0},{7,1},{8,14},{9,15},{10,... | collective-permute-start | bytes 147464 | tf_op jit(solution)/shard_map/ppermute | solution.py:215
  27.9 1.8 %collective-permute-start.9 = (f16[12,8,256]{2,1,0:T(8,128)(2,1)S(1)}, f16[12,8,256]{2,1,0:T(8,128)(2,1)S(1)}, u32[]{:S(2)}, u32[]{:S(2)}) collective-permute-start(f16[12,8,256]{2,1,0:T(8,128)(2,1)S(1)} %get-tuple-element.37), channel_id=1, source_target_pairs={{0,2},{1,3},{2,0},{3,1},{4,6},{5,7},{6,4},{7,5},{8,10},{9,11},{10,... | collective-permute-start | bytes 147464 | tf_op jit(solution)/shard_map/ppermute | solution.py:215
  29.8 1.6 %collective-permute-done.7 = f16[12,8,256]{2,1,0:T(8,128)(2,1)S(1)} collective-permute-done((f16[12,8,256]{2,1,0:T(8,128)(2,1)S(1)}, f16[12,8,256]{2,1,0:T(8,128)(2,1)S(1)}, u32[]{:S(2)}, u32[]{:S(2)}) %collective-permute-start.7) | collective-permute-done | bytes 49184 | tf_op jit(solution)/shard_map/ppermute | solution.py:215
  31.4 0.5 collective-permute-done.8
  32.1 3.0 %collective-permute-start.10 = (f16[12,8,256]{2,1,0:T(8,128)(2,1)S(1)}, f16[12,8,256]{2,1,0:T(8,128)(2,1)S(1)}, u32[]{:S(2)}, u32[]{:S(2)}) collective-permute-start(f16[12,8,256]{2,1,0:T(8,128)(2,1)S(1)} %multiply_convert_fusion.1), channel_id=1, source_target_pairs={{0,8},{1,9},{2,10},{3,11},{4,12},{5,13},{6,14},{7,15},{8,0},{9,1},... | collective-permute-start | bytes 147464 | tf_op jit(solution)/shard_map/ppermute | solution.py:215
  35.1 2.3 %collective-permute-done.10 = f16[12,8,256]{2,1,0:T(8,128)(2,1)S(1)} collective-permute-done((f16[12,8,256]{2,1,0:T(8,128)(2,1)S(1)}, f16[12,8,256]{2,1,0:T(8,128)(2,1)S(1)}, u32[]{:S(2)}, u32[]{:S(2)}) %collective-permute-start.10) | collective-permute-done | bytes 49184 | tf_op jit(solution)/shard_map/ppermute | solution.py:215
  37.6 0.5 demand_step.4
  38.0 0.7 %collective-permute-done.11.other_ref = bf16[12,8,256]{2,1,0:T(8,128)(2,1)S(1)} collective-permute-done((bf16[12,8,256]{2,1,0:T(8,128)(2,1)S(1)}, bf16[12,8,256]{2,1,0:T(8,128)(2,1)S(1)}, u32[]{:S(2)}, u32[]{:S(2)}) %collective-permute-start.11) | collective-permute-done | bytes 49184 | tf_op jit(solution)/shard_map/ppermute | solution.py:215
  38.8 3.4 %adjoint_forward.3 = (f32[12,8,256]{2,1,0:T(8,128)S(1)}, f32[12,8,256]{2,1,0:T(8,128)S(1)}, f32[12,16,256]{2,1,0:T(8,128)}) custom-call(s32[48]{0:T(128)S(4)} %get-tuple-element.19.row_ref, s32[48]{0:T(128)S(4)} %get-tuple-element.20.col_ref, s32[1]{0:T(128)S(6)} %copy.14.count_ref, f32[12,1,256]{2,1,0:T(1,128)S(1)} %bitcast.29, ...), custom_call_target="tpu_custom_call" | custom-call | flops 201326592 | bytes 6291456 | tf_op jit(solution)/shard_map/adjoint_forward/pallas_call | solution.py:256
  42.4 1.1 %collective-permute-done.12 = f32[12,8,256]{2,1,0:T(8,128)S(1)} collective-permute-done((f32[12,8,256]{2,1,0:T(8,128)S(1)}, f32[12,8,256]{2,1,0:T(8,128)S(1)}, u32[]{:S(2)}, u32[]{:S(2)}) %collective-permute-start.12) | collective-permute-done | bytes 98336 | tf_op jit(solution)/shard_map/ppermute | solution.py:215
  43.7 2.7 %collective-permute-start.13 = (f16[12,2,256]{2,1,0:T(2,128)(2,1)S(1)}, f16[12,2,256]{2,1,0:T(2,128)(2,1)S(1)}, u32[]{:S(2)}, u32[]{:S(2)}) collective-permute-start(f16[12,2,256]{2,1,0:T(2,128)(2,1)S(1)} %get-tuple-element.45), channel_id=1, source_target_pairs={{0,6},{1,7},{2,4},{3,5},{4,2},{5,3},{6,0},{7,1},{8,14},{9,15},{10,... | collective-permute-start | bytes 36872 | tf_op jit(solution)/shard_map/ppermute | solution.py:215
  46.8 0.5 collective-permute-start.15
  47.2 1.1 %collective-permute-done.13 = f16[12,2,256]{2,1,0:T(2,128)(2,1)S(1)} collective-permute-done((f16[12,2,256]{2,1,0:T(2,128)(2,1)S(1)}, f16[12,2,256]{2,1,0:T(2,128)(2,1)S(1)}, u32[]{:S(2)}, u32[]{:S(2)}) %collective-permute-start.13) | collective-permute-done | bytes 12320 | tf_op jit(solution)/shard_map/ppermute | solution.py:215
  48.4 1.8 %collective-permute-done.14 = f16[12,2,256]{2,1,0:T(2,128)(2,1)S(1)} collective-permute-done((f16[12,2,256]{2,1,0:T(2,128)(2,1)S(1)}, f16[12,2,256]{2,1,0:T(2,128)(2,1)S(1)}, u32[]{:S(2)}, u32[]{:S(2)}) %collective-permute-start.14) | collective-permute-done | bytes 12320 | tf_op jit(solution)/shard_map/ppermute | solution.py:215
  50.5 2.7 %collective-permute-start.16 = (f16[12,1,256]{2,1,0:T(2,128)(2,1)S(1)}, f16[12,1,256]{2,1,0:T(2,128)(2,1)S(1)}, u32[]{:S(2)}, u32[]{:S(2)}) collective-permute-start(f16[12,1,256]{2,1,0:T(2,128)(2,1)S(1)} %fusion.3), channel_id=1, source_target_pairs={{0,8},{1,9},{2,10},{3,11},{4,12},{5,13},{6,14},{7,15},{8,0},{9,1},... | collective-permute-start | bytes 18440 | tf_op jit(solution)/shard_map/ppermute | solution.py:215
  53.2 0.9 %copy-done.2 = f32[12,16,256]{2,1,0:T(8,128)S(1)} copy-done((f32[12,16,256]{2,1,0:T(8,128)S(1)}, f32[12,16,256]{2,1,0:T(8,128)}, u32[]{:S(2)}) %copy-start.2) | copy-done | bytes 196632
  54.2 0.8 %demand_step.5 = f32[12,16,32]{2,1,0:T(8,128)} custom-call(f32[12,16,256]{2,1,0:T(8,128)S(1)} %bitcast.22, f32[12,16,32]{2,1,0:T(8,128)S(1)} %bitcast.25, f32[12,16,32]{2,1,0:T(8,128)S(1)} %get-tuple-element.34.refs_2_, f32[12,16,256]{2,1,0:T(8,128)S(1)} %get-tuple-element.27.refs_4_.flows_ref.refs_3_, f32[12,16,256]{2,1,0:T(8,128)S(1)} %copy-done.2), custom_call_target="tpu_custom_call" | custom-call | flops 1000000 | bytes 786432 | tf_op jit(solution)/shard_map/demand_step/pallas_call | solution.py:202
  55.2 0.6 %maximum_bitcast_fusion = f32[1,12,256]{2,0,1:T(1,128)} fusion(f16[12,1,256]{2,1,0:T(2,128)(2,1)S(1)} %collective-permute-done.16, f32[12,2,256]{2,1,0:T(2,128)S(1)} %fusion.2, s32[]{:T(128)S(6)} %select_n.54, f32[12,8,256]{2,1,0:T(8,128)S(1)} %get-tuple-element.36, s32[]{:T(128)S(6)} %select_n.46), kind=kLoop, calls=%fused_computation.15 | loop fusion | flops 18432 | bytes 43016 | tf_op jit(solution)/shard_map/transpose | solution.py:262
  (29 shorter events, 2.4 us)
Async XLA Ops:
  0.6 20.0 %copy-start = (f32[16,12,256]{2,0,1:T(8,128)S(1)}, f32[16,12,256]{2,0,1:T(8,128)}, u32[]{:S(2)}) copy-start(f32[16,12,256]{2,0,1:T(8,128)} %param.7) | copy-start | bytes 589828
  0.6 21.2 %copy-start.3 = (f32[1,12,256]{2,0,1:T(1,128)S(1)}, f32[1,12,256]{2,0,1:T(1,128)}, u32[]{:S(2)}) copy-start(f32[1,12,256]{2,0,1:T(1,128)} %param.9) | copy-start | bytes 36868
  0.7 20.0 %copy-start.1 = (f32[16,12,32]{2,0,1:T(8,128)S(1)}, f32[16,12,32]{2,0,1:T(8,128)}, u32[]{:S(2)}) copy-start(f32[16,12,32]{2,0,1:T(8,128)} %param.8) | copy-start | bytes 73732
  5.5 1.5 %collective-permute-start = (f32[12,8,256]{2,1,0:T(8,128)S(1)}, f32[12,8,256]{2,1,0:T(8,128)S(1)}, u32[]{:S(2)}, u32[]{:S(2)}) collective-permute-start(f32[12,8,256]{2,1,0:T(8,128)S(1)} %get-tuple-element.25), channel_id=1, source_target_pairs={{0,1},{1,0},{2,3},{3,2},{4,5},{5,4},{6,7},{7,6},{8,9},{9,8},{10,11... | collective-permute-start | bytes 294920 | tf_op jit(solution)/shard_map/ppermute | solution.py:215
  7.0 6.0 %collective-permute-start.1 = (f16[12,8,256]{2,1,0:T(8,128)(2,1)S(1)}, f16[12,8,256]{2,1,0:T(8,128)(2,1)S(1)}, u32[]{:S(2)}, u32[]{:S(2)}) collective-permute-start(f16[12,8,256]{2,1,0:T(8,128)(2,1)S(1)} %get-tuple-element.41), channel_id=1, source_target_pairs={{0,6},{1,7},{2,4},{3,5},{4,2},{5,3},{6,0},{7,1},{8,14},{9,15},{10,... | collective-permute-start | bytes 147464 | tf_op jit(solution)/shard_map/ppermute | solution.py:215
  10.9 4.1 %collective-permute-start.2 = (f16[12,8,256]{2,1,0:T(8,128)(2,1)S(1)}, f16[12,8,256]{2,1,0:T(8,128)(2,1)S(1)}, u32[]{:S(2)}, u32[]{:S(2)}) collective-permute-start(f16[12,8,256]{2,1,0:T(8,128)(2,1)S(1)} %get-tuple-element.41), channel_id=1, source_target_pairs={{0,4},{1,5},{2,6},{3,7},{4,0},{5,1},{6,2},{7,3},{8,12},{9,13},{10,... | collective-permute-start | bytes 147464 | tf_op jit(solution)/shard_map/ppermute | solution.py:215
  11.4 4.1 %collective-permute-start.3 = (f16[12,8,256]{2,1,0:T(8,128)(2,1)S(1)}, f16[12,8,256]{2,1,0:T(8,128)(2,1)S(1)}, u32[]{:S(2)}, u32[]{:S(2)}) collective-permute-start(f16[12,8,256]{2,1,0:T(8,128)(2,1)S(1)} %get-tuple-element.41), channel_id=1, source_target_pairs={{0,2},{1,3},{2,0},{3,1},{4,6},{5,7},{6,4},{7,5},{8,10},{9,11},{10,... | collective-permute-start | bytes 147464 | tf_op jit(solution)/shard_map/ppermute | solution.py:215
  15.5 5.1 %collective-permute-start.4 = (f16[12,8,256]{2,1,0:T(8,128)(2,1)S(1)}, f16[12,8,256]{2,1,0:T(8,128)(2,1)S(1)}, u32[]{:S(2)}, u32[]{:S(2)}) collective-permute-start(f16[12,8,256]{2,1,0:T(8,128)(2,1)S(1)} %get-tuple-element.39), channel_id=1, source_target_pairs={{0,8},{1,9},{2,10},{3,11},{4,12},{5,13},{6,14},{7,15},{8,0},{9,1},... | collective-permute-start | bytes 147464 | tf_op jit(solution)/shard_map/ppermute | solution.py:215
  20.6 1.3 %collective-permute-start.5 = (bf16[12,8,256]{2,1,0:T(8,128)(2,1)S(1)}, bf16[12,8,256]{2,1,0:T(8,128)(2,1)S(1)}, u32[]{:S(2)}, u32[]{:S(2)}) collective-permute-start(bf16[12,8,256]{2,1,0:T(8,128)(2,1)S(1)} %fusion.own_ref), channel_id=1, source_target_pairs={{0,1},{1,0},{2,3},{3,2},{4,5},{5,4},{6,7},{7,6},{8,9},{9,8},{10,11... | collective-permute-start | bytes 147464 | tf_op jit(solution)/shard_map/ppermute | solution.py:215
  24.8 1.4 %collective-permute-start.6 = (f32[12,8,256]{2,1,0:T(8,128)S(1)}, f32[12,8,256]{2,1,0:T(8,128)S(1)}, u32[]{:S(2)}, u32[]{:S(2)}) collective-permute-start(f32[12,8,256]{2,1,0:T(8,128)S(1)} %get-tuple-element.30), channel_id=1, source_target_pairs={{0,1},{1,0},{2,3},{3,2},{4,5},{5,4},{6,7},{7,6},{8,9},{9,8},{10,11... | collective-permute-start | bytes 294920 | tf_op jit(solution)/shard_map/ppermute | solution.py:215
  26.2 5.2 %collective-permute-start.7 = (f16[12,8,256]{2,1,0:T(8,128)(2,1)S(1)}, f16[12,8,256]{2,1,0:T(8,128)(2,1)S(1)}, u32[]{:S(2)}, u32[]{:S(2)}) collective-permute-start(f16[12,8,256]{2,1,0:T(8,128)(2,1)S(1)} %get-tuple-element.37), channel_id=1, source_target_pairs={{0,6},{1,7},{2,4},{3,5},{4,2},{5,3},{6,0},{7,1},{8,14},{9,15},{10,... | collective-permute-start | bytes 147464 | tf_op jit(solution)/shard_map/ppermute | solution.py:215
  27.8 4.1 %collective-permute-start.8 = (f16[12,8,256]{2,1,0:T(8,128)(2,1)S(1)}, f16[12,8,256]{2,1,0:T(8,128)(2,1)S(1)}, u32[]{:S(2)}, u32[]{:S(2)}) collective-permute-start(f16[12,8,256]{2,1,0:T(8,128)(2,1)S(1)} %get-tuple-element.37), channel_id=1, source_target_pairs={{0,4},{1,5},{2,6},{3,7},{4,0},{5,1},{6,2},{7,3},{8,12},{9,13},{10,... | collective-permute-start | bytes 147464 | tf_op jit(solution)/shard_map/ppermute | solution.py:215
  27.9 4.1 %collective-permute-start.9 = (f16[12,8,256]{2,1,0:T(8,128)(2,1)S(1)}, f16[12,8,256]{2,1,0:T(8,128)(2,1)S(1)}, u32[]{:S(2)}, u32[]{:S(2)}) collective-permute-start(f16[12,8,256]{2,1,0:T(8,128)(2,1)S(1)} %get-tuple-element.37), channel_id=1, source_target_pairs={{0,2},{1,3},{2,0},{3,1},{4,6},{5,7},{6,4},{7,5},{8,10},{9,11},{10,... | collective-permute-start | bytes 147464 | tf_op jit(solution)/shard_map/ppermute | solution.py:215
  32.1 5.3 %collective-permute-start.10 = (f16[12,8,256]{2,1,0:T(8,128)(2,1)S(1)}, f16[12,8,256]{2,1,0:T(8,128)(2,1)S(1)}, u32[]{:S(2)}, u32[]{:S(2)}) collective-permute-start(f16[12,8,256]{2,1,0:T(8,128)(2,1)S(1)} %multiply_convert_fusion.1), channel_id=1, source_target_pairs={{0,8},{1,9},{2,10},{3,11},{4,12},{5,13},{6,14},{7,15},{8,0},{9,1},... | collective-permute-start | bytes 147464 | tf_op jit(solution)/shard_map/ppermute | solution.py:215
  37.5 1.3 %collective-permute-start.11 = (bf16[12,8,256]{2,1,0:T(8,128)(2,1)S(1)}, bf16[12,8,256]{2,1,0:T(8,128)(2,1)S(1)}, u32[]{:S(2)}, u32[]{:S(2)}) collective-permute-start(bf16[12,8,256]{2,1,0:T(8,128)(2,1)S(1)} %get-tuple-element.35.own_ref), channel_id=1, source_target_pairs={{0,1},{1,0},{2,3},{3,2},{4,5},{5,4},{6,7},{7,6},{8,9},{9,8},{10,11... | collective-permute-start | bytes 147464 | tf_op jit(solution)/shard_map/ppermute | solution.py:215
  42.2 1.3 %collective-permute-start.12 = (f32[12,8,256]{2,1,0:T(8,128)S(1)}, f32[12,8,256]{2,1,0:T(8,128)S(1)}, u32[]{:S(2)}, u32[]{:S(2)}) collective-permute-start(f32[12,8,256]{2,1,0:T(8,128)S(1)} %get-tuple-element.33), channel_id=1, source_target_pairs={{0,1},{1,0},{2,3},{3,2},{4,5},{5,4},{6,7},{7,6},{8,9},{9,8},{10,11... | collective-permute-start | bytes 294920 | tf_op jit(solution)/shard_map/ppermute | solution.py:215
  43.7 4.7 %collective-permute-start.13 = (f16[12,2,256]{2,1,0:T(2,128)(2,1)S(1)}, f16[12,2,256]{2,1,0:T(2,128)(2,1)S(1)}, u32[]{:S(2)}, u32[]{:S(2)}) collective-permute-start(f16[12,2,256]{2,1,0:T(2,128)(2,1)S(1)} %get-tuple-element.45), channel_id=1, source_target_pairs={{0,6},{1,7},{2,4},{3,5},{4,2},{5,3},{6,0},{7,1},{8,14},{9,15},{10,... | collective-permute-start | bytes 36872 | tf_op jit(solution)/shard_map/ppermute | solution.py:215
  46.4 3.7 %collective-permute-start.14 = (f16[12,2,256]{2,1,0:T(2,128)(2,1)S(1)}, f16[12,2,256]{2,1,0:T(2,128)(2,1)S(1)}, u32[]{:S(2)}, u32[]{:S(2)}) collective-permute-start(f16[12,2,256]{2,1,0:T(2,128)(2,1)S(1)} %get-tuple-element.47), channel_id=1, source_target_pairs={{0,4},{1,5},{2,6},{3,7},{4,0},{5,1},{6,2},{7,3},{8,12},{9,13},{10,... | collective-permute-start | bytes 36872 | tf_op jit(solution)/shard_map/ppermute | solution.py:215
  46.8 3.7 %collective-permute-start.15 = (f16[12,2,256]{2,1,0:T(2,128)(2,1)S(1)}, f16[12,2,256]{2,1,0:T(2,128)(2,1)S(1)}, u32[]{:S(2)}, u32[]{:S(2)}) collective-permute-start(f16[12,2,256]{2,1,0:T(2,128)(2,1)S(1)} %get-tuple-element.46), channel_id=1, source_target_pairs={{0,2},{1,3},{2,0},{3,1},{4,6},{5,7},{6,4},{7,5},{8,10},{9,11},{10,... | collective-permute-start | bytes 36872 | tf_op jit(solution)/shard_map/ppermute | solution.py:215
  50.5 4.7 %collective-permute-start.16 = (f16[12,1,256]{2,1,0:T(2,128)(2,1)S(1)}, f16[12,1,256]{2,1,0:T(2,128)(2,1)S(1)}, u32[]{:S(2)}, u32[]{:S(2)}) collective-permute-start(f16[12,1,256]{2,1,0:T(2,128)(2,1)S(1)} %fusion.3), channel_id=1, source_target_pairs={{0,8},{1,9},{2,10},{3,11},{4,12},{5,13},{6,14},{7,15},{8,0},{9,1},... | collective-permute-start | bytes 18440 | tf_op jit(solution)/shard_map/ppermute | solution.py:215
  53.2 0.9 %copy-start.2 = (f32[12,16,256]{2,1,0:T(8,128)S(1)}, f32[12,16,256]{2,1,0:T(8,128)}, u32[]{:S(2)}) copy-start(f32[12,16,256]{2,1,0:T(8,128)} %get-tuple-element.31.refs_4_) | copy-start | bytes 589828

commit v5 on v4

--- a/solution.py
+++ b/solution.py
@@ -10,7 +10,7 @@
 PATHS_PER = 8
 ITERS = 3
 CHUNKS = 4
-VMEM_LIMIT = 40 * 2**20
+VMEM_LIMIT = 20 * 2**20
 F32 = jnp.float32
 BF16 = jnp.bfloat16
 
@@ -74,7 +74,7 @@
 
 
 def next_kernel(
-    row_ref, col_ref, count_ref, cap_ref, base_ref, flows_ref, own_ref, other_ref, tiles_v,
+    row_ref, col_ref, count_ref, cap_ref, base_ref, flows_ref, own_ref, other_ref, tiles_v, turned_v,
     keep_ref, send_ref, new_ref, ex, acc0, acc1, grad0, grad1, duals,
 ):
     me = lax.axis_index("comm")
@@ -93,9 +93,8 @@
         grad = grads[n % 2]
         col = col_ref[n]
         row = jnp.where(n < live, row_ref[n], blocks)
-        grad[row] += lax.dot_general(
-            duals[(col & 1) * half + (col >> 1)], tiles_v[n], (((1,), (1,)), ((), ())),
-            preferred_element_type=F32,
+        grad[row] += jnp.dot(
+            duals[(col & 1) * half + (col >> 1)], turned_v[n], preferred_element_type=F32
         )
     back = jnp.swapaxes(grad0[pl.ds(0, blocks)] + grad1[pl.ds(0, blocks)], 0, 1)
     new = jnp.maximum(0.0, base_ref[...] - 0.5 * back)
@@ -104,6 +103,12 @@
     accs = (acc0, acc1)
     forward(row_ref, col_ref, live, tiles_v, ex, accs)
     emit(me, cap_ref[...], accs, keep_ref, send_ref)
+
+
+def transpose_kernel(tiles_v, total_ref, turned_ref, same_ref):
+    same_ref[...] = total_ref[...]
+    for n in range(tiles_v.shape[0]):
+        turned_ref[n] = tiles_v[n].T
 
 
 def commodity_matrix(paths):
@@ -182,8 +187,8 @@
 
     following = pl.pallas_call(
         next_kernel,
-        out_shape=(halves, halves, per_path),
-        in_specs=[spec(S)] * 3 + [spec(V)] * 6,
+        out_shape=(halves, halves, V(cost.shape, F32)),
+        in_specs=[spec(S)] * 3 + [spec(V)] * 7,
         out_specs=(spec(V),) * 3,
         scratch_shapes=[V(by_block, BF16)]
         + acc_scratch
@@ -194,6 +199,18 @@
             flops=2 * passes, bytes_accessed=tiles.size * 2, transcendentals=0
         ),
         name="adjoint_forward",
+    )
+
+    turn = pl.pallas_call(
+        transpose_kernel,
+        out_shape=(V(tiles.shape, BF16), halves),
+        in_specs=[spec(V)] * 2,
+        out_specs=(spec(V),) * 2,
+        compiler_params=params,
+        cost_estimate=pl.CostEstimate(
+            flops=0, bytes_accessed=4 * tiles.size, transcendentals=0
+        ),
+        name="transpose_tiles",
     )
 
     def demand_step(sweep, *args):
@@ -220,13 +237,15 @@
         stages.append((bit, min(4, n_dev // bit)))
         bit *= 4
 
-    def sum_all(total):
-        for bit, size in stages:
+    def sum_all(total, beside):
+        for k, (bit, size) in enumerate(stages):
             sent = (total * (1.0 / n_dev)).astype(jnp.float16)
             parts = [swap(sent, bit * d) for d in reversed(range(1, size))]
+            if k == 0 and beside is not None:
+                beside, total = turn(beside, total)
             for part in parts:
                 total = total + part.astype(F32) * n_dev
-        return total
+        return total, beside
 
     def scatter(total):
         for bit, size in stages:
@@ -251,10 +270,12 @@
         else:
             (dd,) = demand_step(sweep, cost, demand, dd, old, flows)
             break
-        link_duals = jnp.maximum(0.0, link_duals + 0.08 * sum_all(total))
+        total, turned = sum_all(total, tiles_v if sweep == 0 else None)
+        turned_v = turned if sweep == 0 else turned_v
+        link_duals = jnp.maximum(0.0, link_duals + 0.08 * total)
         rounded = link_duals.astype(BF16)
         keep, send, new = following(
-            *index, tile_count, capacity, base, flows, rounded, swap(rounded, 1), tiles_v
+            *index, tile_count, capacity, base, flows, rounded, swap(rounded, 1), tiles_v, turned_v
         )
         old, flows = flows, new
     own_duals = lax.dynamic_index_in_dim(link_duals, me // 2, 1, keepdims=True)

time: 56 us -> 53.7 us (0.959)
  waiting for transfers between devices: 19 us -> 17.5 us
  Pallas kernels: 12.2 us -> 11.5 us
    pallas_call x2, Pallas kernels: 6.34 us -> 4.31 us  [per_device(): following(*index, tile_count, capacity, base, flows, rounded, swap(rounde...]
    pallas_call x0 -> x1, Pallas kernels: none -> 1.67 us  [sum_all(): beside, total = turn(beside, total)]
    ppermute x17, waiting for transfers between devices: 19 us -> 17.5 us  [swap(): return lax.ppermute(x, 'comm', [(i, i ^ bit) for i in range(n_dev)])]
  transfers between devices with their start and end apart: 17 -> 17, of which waited for: 17 -> 16; matrix products, arithmetic and copies ran while one was open for 0% -> 1% of each run, Pallas kernels for 3% -> 6%
where the time goes in v5:
time: 53.7 us; the launch traced here: 53.5 us
  starting transfers between devices  21.2 us (39%)
  waiting for transfers between devices  17.5 us (33%)
  Pallas kernels  11.5 us (21%)
  between operations  1.46 us (3%)
  other arithmetic  1.03 us (2%)
  local copies, waits for them, and re-layouts  0.76 us (1%)
    ppermute x17, starting transfers between devices, swap(): return lax.ppermute(x, 'comm', [(i, i ^ bit) for i in range(n_dev)])  21.2 us
    ppermute x17, waiting for transfers between devices, swap(): return lax.ppermute(x, 'comm', [(i, i ^ bit) for i in range(n_dev)])  17.5 us
    pallas_call x2, Pallas kernels, per_device(): following(*index, tile_count, capacity, base, flows, rounded, swap(rounde...  4.31 us
    pallas_call x1, Pallas kernels, per_device(): pl.pallas_call(first_kernel, out_shape=(halves, halves, V(tiles.shape, BF...  3.78 us
    pallas_call x3, Pallas kernels, demand_step(): pl.pallas_call(functools.partial(demand_kernel, sweep), out_shape=outs, i...  1.74 us
    pallas_call x1, Pallas kernels, sum_all(): beside, total = turn(beside, total)  1.67 us
  transfers between devices with their start and end apart: 17, of which 16 were waited for; matrix products, arithmetic and copies ran while one was open for 1% of the time, Pallas kernels for 6%

profile of v5, /device:TPU:0, one launch (start us, length us, event | category | flops | bytes accessed | tf_op | source)
XLA Modules:
  0.0 53.5 jit_solution(10857499989157092020)
XLA Ops:
  1.3 3.8 %first_forward.1 = (f32[12,8,256]{2,1,0:T(8,128)S(1)}, f32[12,8,256]{2,1,0:T(8,128)S(1)}, bf16[48,256,256]{2,1,0:T(8,128)(2,1)S(1)}, s32[48]{0:T(128)S(4)}, s32[48]{0:T(128)S(4)}) custom-call(s32[1]{0:T(128)S(6)} %copy.15.count_ref, s32[48]{0:T(128)} %row_hbm.1, s32[48]{0:T(128)} %col_hbm.1, f32[12,1,256]{2,1,0:T(1,128)} %bitcast.27, ...), custom_call_target="tpu_custom_call" | custom-call | flops 100663296 | bytes 6291456 | tf_op jit(solution)/shard_map/first_forward/pallas_call | solution.py:173
  5.1 0.5 collective-permute-start
  5.6 0.9 %collective-permute-done = f32[12,8,256]{2,1,0:T(8,128)S(1)} collective-permute-done((f32[12,8,256]{2,1,0:T(8,128)S(1)}, f32[12,8,256]{2,1,0:T(8,128)S(1)}, u32[]{:S(2)}, u32[]{:S(2)}) %collective-permute-start) | collective-permute-done | bytes 98336 | tf_op jit(solution)/shard_map/ppermute | solution.py:232
  6.6 4.0 %collective-permute-start.1 = (f16[12,8,256]{2,1,0:T(8,128)(2,1)S(1)}, f16[12,8,256]{2,1,0:T(8,128)(2,1)S(1)}, u32[]{:S(2)}, u32[]{:S(2)}) collective-permute-start(f16[12,8,256]{2,1,0:T(8,128)(2,1)S(1)} %get-tuple-element.45), channel_id=1, source_target_pairs={{0,6},{1,7},{2,4},{3,5},{4,2},{5,3},{6,0},{7,1},{8,14},{9,15},{10,... | collective-permute-start | bytes 147464 | tf_op jit(solution)/shard_map/ppermute | solution.py:232
  10.5 0.4 collective-permute-start.2
  11.2 1.7 %transpose_tiles.1 = (bf16[48,256,256]{2,1,0:T(8,128)(2,1)S(1)}, f32[12,8,256]{2,1,0:T(8,128)S(1)}) custom-call(bf16[48,256,256]{2,1,0:T(8,128)(2,1)S(1)} %get-tuple-element.26.tiles_v, f32[12,8,256]{2,1,0:T(8,128)S(1)} %get-tuple-element.46.total_ref), custom_call_target="tpu_custom_call" | custom-call | bytes 12582912 | tf_op jit(solution)/shard_map/transpose_tiles/pallas_call | solution.py:245
  12.9 1.8 %collective-permute-done.2 = f16[12,8,256]{2,1,0:T(8,128)(2,1)S(1)} collective-permute-done((f16[12,8,256]{2,1,0:T(8,128)(2,1)S(1)}, f16[12,8,256]{2,1,0:T(8,128)(2,1)S(1)}, u32[]{:S(2)}, u32[]{:S(2)}) %collective-permute-start.2) | collective-permute-done | bytes 49184 | tf_op jit(solution)/shard_map/ppermute | solution.py:232
  15.1 2.7 %collective-permute-start.4 = (f16[12,8,256]{2,1,0:T(8,128)(2,1)S(1)}, f16[12,8,256]{2,1,0:T(8,128)(2,1)S(1)}, u32[]{:S(2)}, u32[]{:S(2)}) collective-permute-start(f16[12,8,256]{2,1,0:T(8,128)(2,1)S(1)} %get-tuple-element.43), channel_id=1, source_target_pairs={{0,8},{1,9},{2,10},{3,11},{4,12},{5,13},{6,14},{7,15},{8,0},{9,1},... | collective-permute-start | bytes 147464 | tf_op jit(solution)/shard_map/ppermute | solution.py:232
  17.8 2.4 %collective-permute-done.4 = f16[12,8,256]{2,1,0:T(8,128)(2,1)S(1)} collective-permute-done((f16[12,8,256]{2,1,0:T(8,128)(2,1)S(1)}, f16[12,8,256]{2,1,0:T(8,128)(2,1)S(1)}, u32[]{:S(2)}, u32[]{:S(2)}) %collective-permute-start.4) | collective-permute-done | bytes 49184 | tf_op jit(solution)/shard_map/ppermute | solution.py:232
  20.3 0.5 demand_step.3
  20.8 0.7 %collective-permute-done.5.other_ref = bf16[12,8,256]{2,1,0:T(8,128)(2,1)S(1)} collective-permute-done((bf16[12,8,256]{2,1,0:T(8,128)(2,1)S(1)}, bf16[12,8,256]{2,1,0:T(8,128)(2,1)S(1)}, u32[]{:S(2)}, u32[]{:S(2)}) %collective-permute-start.5) | collective-permute-done | bytes 49184 | tf_op jit(solution)/shard_map/ppermute | solution.py:232
  21.5 2.2 %adjoint_forward.2 = (f32[12,8,256]{2,1,0:T(8,128)S(1)}, f32[12,8,256]{2,1,0:T(8,128)S(1)}, f32[12,16,256]{2,1,0:T(8,128)S(1)}) custom-call(s32[48]{0:T(128)S(4)} %get-tuple-element.21.row_ref, s32[48]{0:T(128)S(4)} %get-tuple-element.22.col_ref, s32[1]{0:T(128)S(6)} %copy.15.count_ref, f32[12,1,256]{2,1,0:T(1,128)S(1)} %bitcast.28, ...), custom_call_target="tpu_custom_call" | custom-call | flops 201326592 | bytes 6291456 | tf_op jit(solution)/shard_map/adjoint_forward/pallas_call | solution.py:277
  23.9 1.1 %collective-permute-done.6 = f32[12,8,256]{2,1,0:T(8,128)S(1)} collective-permute-done((f32[12,8,256]{2,1,0:T(8,128)S(1)}, f32[12,8,256]{2,1,0:T(8,128)S(1)}, u32[]{:S(2)}, u32[]{:S(2)}) %collective-permute-start.6) | collective-permute-done | bytes 98336 | tf_op jit(solution)/shard_map/ppermute | solution.py:232
  25.1 1.6 %collective-permute-start.7 = (f16[12,8,256]{2,1,0:T(8,128)(2,1)S(1)}, f16[12,8,256]{2,1,0:T(8,128)(2,1)S(1)}, u32[]{:S(2)}, u32[]{:S(2)}) collective-permute-start(f16[12,8,256]{2,1,0:T(8,128)(2,1)S(1)} %get-tuple-element.41), channel_id=1, source_target_pairs={{0,6},{1,7},{2,4},{3,5},{4,2},{5,3},{6,0},{7,1},{8,14},{9,15},{10,... | collective-permute-start | bytes 147464 | tf_op jit(solution)/shard_map/ppermute | solution.py:232
  26.8 1.8 %collective-permute-start.9 = (f16[12,8,256]{2,1,0:T(8,128)(2,1)S(1)}, f16[12,8,256]{2,1,0:T(8,128)(2,1)S(1)}, u32[]{:S(2)}, u32[]{:S(2)}) collective-permute-start(f16[12,8,256]{2,1,0:T(8,128)(2,1)S(1)} %get-tuple-element.41), channel_id=1, source_target_pairs={{0,2},{1,3},{2,0},{3,1},{4,6},{5,7},{6,4},{7,5},{8,10},{9,11},{10,... | collective-permute-start | bytes 147464 | tf_op jit(solution)/shard_map/ppermute | solution.py:232
  28.6 1.6 %collective-permute-done.7 = f16[12,8,256]{2,1,0:T(8,128)(2,1)S(1)} collective-permute-done((f16[12,8,256]{2,1,0:T(8,128)(2,1)S(1)}, f16[12,8,256]{2,1,0:T(8,128)(2,1)S(1)}, u32[]{:S(2)}, u32[]{:S(2)}) %collective-permute-start.7) | collective-permute-done | bytes 49184 | tf_op jit(solution)/shard_map/ppermute | solution.py:232
  30.2 0.5 collective-permute-done.8
  30.9 3.1 %collective-permute-start.10 = (f16[12,8,256]{2,1,0:T(8,128)(2,1)S(1)}, f16[12,8,256]{2,1,0:T(8,128)(2,1)S(1)}, u32[]{:S(2)}, u32[]{:S(2)}) collective-permute-start(f16[12,8,256]{2,1,0:T(8,128)(2,1)S(1)} %multiply_convert_fusion.1), channel_id=1, source_target_pairs={{0,8},{1,9},{2,10},{3,11},{4,12},{5,13},{6,14},{7,15},{8,0},{9,1},... | collective-permute-start | bytes 147464 | tf_op jit(solution)/shard_map/ppermute | solution.py:232
  34.0 2.3 %collective-permute-done.10 = f16[12,8,256]{2,1,0:T(8,128)(2,1)S(1)} collective-permute-done((f16[12,8,256]{2,1,0:T(8,128)(2,1)S(1)}, f16[12,8,256]{2,1,0:T(8,128)(2,1)S(1)}, u32[]{:S(2)}, u32[]{:S(2)}) %collective-permute-start.10) | collective-permute-done | bytes 49184 | tf_op jit(solution)/shard_map/ppermute | solution.py:232
  36.4 0.5 demand_step.4
  36.9 0.8 %collective-permute-done.11.other_ref = bf16[12,8,256]{2,1,0:T(8,128)(2,1)S(1)} collective-permute-done((bf16[12,8,256]{2,1,0:T(8,128)(2,1)S(1)}, bf16[12,8,256]{2,1,0:T(8,128)(2,1)S(1)}, u32[]{:S(2)}, u32[]{:S(2)}) %collective-permute-start.11) | collective-permute-done | bytes 49184 | tf_op jit(solution)/shard_map/ppermute | solution.py:232
  37.6 2.2 %adjoint_forward.3 = (f32[12,8,256]{2,1,0:T(8,128)S(1)}, f32[12,8,256]{2,1,0:T(8,128)S(1)}, f32[12,16,256]{2,1,0:T(8,128)S(1)}) custom-call(s32[48]{0:T(128)S(4)} %get-tuple-element.21.row_ref, s32[48]{0:T(128)S(4)} %get-tuple-element.22.col_ref, s32[1]{0:T(128)S(6)} %copy.15.count_ref, f32[12,1,256]{2,1,0:T(1,128)S(1)} %bitcast.29, ...), custom_call_target="tpu_custom_call" | custom-call | flops 201326592 | bytes 6291456 | tf_op jit(solution)/shard_map/adjoint_forward/pallas_call | solution.py:277
  40.0 1.1 %collective-permute-done.12 = f32[12,8,256]{2,1,0:T(8,128)S(1)} collective-permute-done((f32[12,8,256]{2,1,0:T(8,128)S(1)}, f32[12,8,256]{2,1,0:T(8,128)S(1)}, u32[]{:S(2)}, u32[]{:S(2)}) %collective-permute-start.12) | collective-permute-done | bytes 98336 | tf_op jit(solution)/shard_map/ppermute | solution.py:232
  41.3 2.7 %collective-permute-start.13 = (f16[12,2,256]{2,1,0:T(2,128)(2,1)S(1)}, f16[12,2,256]{2,1,0:T(2,128)(2,1)S(1)}, u32[]{:S(2)}, u32[]{:S(2)}) collective-permute-start(f16[12,2,256]{2,1,0:T(2,128)(2,1)S(1)} %get-tuple-element.49), channel_id=1, source_target_pairs={{0,6},{1,7},{2,4},{3,5},{4,2},{5,3},{6,0},{7,1},{8,14},{9,15},{10,... | collective-permute-start | bytes 36872 | tf_op jit(solution)/shard_map/ppermute | solution.py:232
  44.4 0.5 collective-permute-start.15
  44.9 1.1 %collective-permute-done.13 = f16[12,2,256]{2,1,0:T(2,128)(2,1)S(1)} collective-permute-done((f16[12,2,256]{2,1,0:T(2,128)(2,1)S(1)}, f16[12,2,256]{2,1,0:T(2,128)(2,1)S(1)}, u32[]{:S(2)}, u32[]{:S(2)}) %collective-permute-start.13) | collective-permute-done | bytes 12320 | tf_op jit(solution)/shard_map/ppermute | solution.py:232
  46.0 1.8 %collective-permute-done.14 = f16[12,2,256]{2,1,0:T(2,128)(2,1)S(1)} collective-permute-done((f16[12,2,256]{2,1,0:T(2,128)(2,1)S(1)}, f16[12,2,256]{2,1,0:T(2,128)(2,1)S(1)}, u32[]{:S(2)}, u32[]{:S(2)}) %collective-permute-start.14) | collective-permute-done | bytes 12320 | tf_op jit(solution)/shard_map/ppermute | solution.py:232
  48.2 2.7 %collective-permute-start.16 = (f16[12,1,256]{2,1,0:T(2,128)(2,1)S(1)}, f16[12,1,256]{2,1,0:T(2,128)(2,1)S(1)}, u32[]{:S(2)}, u32[]{:S(2)}) collective-permute-start(f16[12,1,256]{2,1,0:T(2,128)(2,1)S(1)} %fusion.3), channel_id=1, source_target_pairs={{0,8},{1,9},{2,10},{3,11},{4,12},{5,13},{6,14},{7,15},{8,0},{9,1},... | collective-permute-start | bytes 18440 | tf_op jit(solution)/shard_map/ppermute | solution.py:232
  50.9 0.7 %copy.14 = f32[16,12,256]{2,0,1:T(8,128)} copy(f32[16,12,256]{2,0,1:T(8,128)S(1)} %bitcast.19) | data formatting | bytes 393216
  51.6 0.8 %demand_step.5 = f32[12,16,32]{2,1,0:T(8,128)} custom-call(f32[12,16,256]{2,1,0:T(8,128)S(1)} %bitcast.23, f32[12,16,32]{2,1,0:T(8,128)S(1)} %bitcast.26, f32[12,16,32]{2,1,0:T(8,128)S(1)} %get-tuple-element.38.refs_2_, f32[12,16,256]{2,1,0:T(8,128)S(1)} %get-tuple-element.31.refs_4_.flows_ref.refs_3_, f32[12,16,256]{2,1,0:T(8,128)S(1)} %get-tuple-element.35.refs_4_), custom_call_target="tpu_custom_call" | custom-call | flops 1000000 | bytes 786432 | tf_op jit(solution)/shard_map/demand_step/pallas_call | solution.py:219
  52.4 0.5 collective-permute-done.16
  52.9 0.6 %maximum_bitcast_fusion = f32[1,12,256]{2,0,1:T(1,128)} fusion(f16[12,1,256]{2,1,0:T(2,128)(2,1)S(1)} %collective-permute-done.16, f32[12,2,256]{2,1,0:T(2,128)S(1)} %fusion.2, s32[]{:T(128)S(6)} %select_n.54, f32[12,8,256]{2,1,0:T(8,128)S(1)} %get-tuple-element.40, s32[]{:T(128)S(6)} %select_n.46), kind=kLoop, calls=%fused_computation.15 | loop fusion | flops 18432 | bytes 43016 | tf_op jit(solution)/shard_map/transpose | solution.py:283
  (29 shorter events, 2.7 us)
Async XLA Ops:
  1.3 19.0 %copy-start = (f32[16,12,256]{2,0,1:T(8,128)S(1)}, f32[16,12,256]{2,0,1:T(8,128)}, u32[]{:S(2)}) copy-start(f32[16,12,256]{2,0,1:T(8,128)} %param.7) | copy-start | bytes 589828
  1.3 19.0 %copy-start.1 = (f32[16,12,32]{2,0,1:T(8,128)S(1)}, f32[16,12,32]{2,0,1:T(8,128)}, u32[]{:S(2)}) copy-start(f32[16,12,32]{2,0,1:T(8,128)} %param.8) | copy-start | bytes 73732
  1.3 20.2 %copy-start.2 = (f32[1,12,256]{2,0,1:T(1,128)S(1)}, f32[1,12,256]{2,0,1:T(1,128)}, u32[]{:S(2)}) copy-start(f32[1,12,256]{2,0,1:T(1,128)} %param.9) | copy-start | bytes 36868
  5.1 1.5 %collective-permute-start = (f32[12,8,256]{2,1,0:T(8,128)S(1)}, f32[12,8,256]{2,1,0:T(8,128)S(1)}, u32[]{:S(2)}, u32[]{:S(2)}) collective-permute-start(f32[12,8,256]{2,1,0:T(8,128)S(1)} %get-tuple-element.28), channel_id=1, source_target_pairs={{0,1},{1,0},{2,3},{3,2},{4,5},{5,4},{6,7},{7,6},{8,9},{9,8},{10,11... | collective-permute-start | bytes 294920 | tf_op jit(solution)/shard_map/ppermute | solution.py:232
  6.6 6.3 %collective-permute-start.1 = (f16[12,8,256]{2,1,0:T(8,128)(2,1)S(1)}, f16[12,8,256]{2,1,0:T(8,128)(2,1)S(1)}, u32[]{:S(2)}, u32[]{:S(2)}) collective-permute-start(f16[12,8,256]{2,1,0:T(8,128)(2,1)S(1)} %get-tuple-element.45), channel_id=1, source_target_pairs={{0,6},{1,7},{2,4},{3,5},{4,2},{5,3},{6,0},{7,1},{8,14},{9,15},{10,... | collective-permute-start | bytes 147464 | tf_op jit(solution)/shard_map/ppermute | solution.py:232
  10.5 4.1 %collective-permute-start.2 = (f16[12,8,256]{2,1,0:T(8,128)(2,1)S(1)}, f16[12,8,256]{2,1,0:T(8,128)(2,1)S(1)}, u32[]{:S(2)}, u32[]{:S(2)}) collective-permute-start(f16[12,8,256]{2,1,0:T(8,128)(2,1)S(1)} %get-tuple-element.45), channel_id=1, source_target_pairs={{0,4},{1,5},{2,6},{3,7},{4,0},{5,1},{6,2},{7,3},{8,12},{9,13},{10,... | collective-permute-start | bytes 147464 | tf_op jit(solution)/shard_map/ppermute | solution.py:232
  11.0 4.1 %collective-permute-start.3 = (f16[12,8,256]{2,1,0:T(8,128)(2,1)S(1)}, f16[12,8,256]{2,1,0:T(8,128)(2,1)S(1)}, u32[]{:S(2)}, u32[]{:S(2)}) collective-permute-start(f16[12,8,256]{2,1,0:T(8,128)(2,1)S(1)} %get-tuple-element.45), channel_id=1, source_target_pairs={{0,2},{1,3},{2,0},{3,1},{4,6},{5,7},{6,4},{7,5},{8,10},{9,11},{10,... | collective-permute-start | bytes 147464 | tf_op jit(solution)/shard_map/ppermute | solution.py:232
  15.1 5.1 %collective-permute-start.4 = (f16[12,8,256]{2,1,0:T(8,128)(2,1)S(1)}, f16[12,8,256]{2,1,0:T(8,128)(2,1)S(1)}, u32[]{:S(2)}, u32[]{:S(2)}) collective-permute-start(f16[12,8,256]{2,1,0:T(8,128)(2,1)S(1)} %get-tuple-element.43), channel_id=1, source_target_pairs={{0,8},{1,9},{2,10},{3,11},{4,12},{5,13},{6,14},{7,15},{8,0},{9,1},... | collective-permute-start | bytes 147464 | tf_op jit(solution)/shard_map/ppermute | solution.py:232
  20.2 1.3 %collective-permute-start.5 = (bf16[12,8,256]{2,1,0:T(8,128)(2,1)S(1)}, bf16[12,8,256]{2,1,0:T(8,128)(2,1)S(1)}, u32[]{:S(2)}, u32[]{:S(2)}) collective-permute-start(bf16[12,8,256]{2,1,0:T(8,128)(2,1)S(1)} %fusion.own_ref), channel_id=1, source_target_pairs={{0,1},{1,0},{2,3},{3,2},{4,5},{5,4},{6,7},{7,6},{8,9},{9,8},{10,11... | collective-permute-start | bytes 147464 | tf_op jit(solution)/shard_map/ppermute | solution.py:232
  23.7 1.4 %collective-permute-start.6 = (f32[12,8,256]{2,1,0:T(8,128)S(1)}, f32[12,8,256]{2,1,0:T(8,128)S(1)}, u32[]{:S(2)}, u32[]{:S(2)}) collective-permute-start(f32[12,8,256]{2,1,0:T(8,128)S(1)} %get-tuple-element.34), channel_id=1, source_target_pairs={{0,1},{1,0},{2,3},{3,2},{4,5},{5,4},{6,7},{7,6},{8,9},{9,8},{10,11... | collective-permute-start | bytes 294920 | tf_op jit(solution)/shard_map/ppermute | solution.py:232
  25.1 5.2 %collective-permute-start.7 = (f16[12,8,256]{2,1,0:T(8,128)(2,1)S(1)}, f16[12,8,256]{2,1,0:T(8,128)(2,1)S(1)}, u32[]{:S(2)}, u32[]{:S(2)}) collective-permute-start(f16[12,8,256]{2,1,0:T(8,128)(2,1)S(1)} %get-tuple-element.41), channel_id=1, source_target_pairs={{0,6},{1,7},{2,4},{3,5},{4,2},{5,3},{6,0},{7,1},{8,14},{9,15},{10,... | collective-permute-start | bytes 147464 | tf_op jit(solution)/shard_map/ppermute | solution.py:232
  26.6 4.1 %collective-permute-start.8 = (f16[12,8,256]{2,1,0:T(8,128)(2,1)S(1)}, f16[12,8,256]{2,1,0:T(8,128)(2,1)S(1)}, u32[]{:S(2)}, u32[]{:S(2)}) collective-permute-start(f16[12,8,256]{2,1,0:T(8,128)(2,1)S(1)} %get-tuple-element.41), channel_id=1, source_target_pairs={{0,4},{1,5},{2,6},{3,7},{4,0},{5,1},{6,2},{7,3},{8,12},{9,13},{10,... | collective-permute-start | bytes 147464 | tf_op jit(solution)/shard_map/ppermute | solution.py:232
  26.8 4.1 %collective-permute-start.9 = (f16[12,8,256]{2,1,0:T(8,128)(2,1)S(1)}, f16[12,8,256]{2,1,0:T(8,128)(2,1)S(1)}, u32[]{:S(2)}, u32[]{:S(2)}) collective-permute-start(f16[12,8,256]{2,1,0:T(8,128)(2,1)S(1)} %get-tuple-element.41), channel_id=1, source_target_pairs={{0,2},{1,3},{2,0},{3,1},{4,6},{5,7},{6,4},{7,5},{8,10},{9,11},{10,... | collective-permute-start | bytes 147464 | tf_op jit(solution)/shard_map/ppermute | solution.py:232
  30.9 5.3 %collective-permute-start.10 = (f16[12,8,256]{2,1,0:T(8,128)(2,1)S(1)}, f16[12,8,256]{2,1,0:T(8,128)(2,1)S(1)}, u32[]{:S(2)}, u32[]{:S(2)}) collective-permute-start(f16[12,8,256]{2,1,0:T(8,128)(2,1)S(1)} %multiply_convert_fusion.1), channel_id=1, source_target_pairs={{0,8},{1,9},{2,10},{3,11},{4,12},{5,13},{6,14},{7,15},{8,0},{9,1},... | collective-permute-start | bytes 147464 | tf_op jit(solution)/shard_map/ppermute | solution.py:232
  36.3 1.3 %collective-permute-start.11 = (bf16[12,8,256]{2,1,0:T(8,128)(2,1)S(1)}, bf16[12,8,256]{2,1,0:T(8,128)(2,1)S(1)}, u32[]{:S(2)}, u32[]{:S(2)}) collective-permute-start(bf16[12,8,256]{2,1,0:T(8,128)(2,1)S(1)} %get-tuple-element.39.own_ref), channel_id=1, source_target_pairs={{0,1},{1,0},{2,3},{3,2},{4,5},{5,4},{6,7},{7,6},{8,9},{9,8},{10,11... | collective-permute-start | bytes 147464 | tf_op jit(solution)/shard_map/ppermute | solution.py:232
  39.8 1.4 %collective-permute-start.12 = (f32[12,8,256]{2,1,0:T(8,128)S(1)}, f32[12,8,256]{2,1,0:T(8,128)S(1)}, u32[]{:S(2)}, u32[]{:S(2)}) collective-permute-start(f32[12,8,256]{2,1,0:T(8,128)S(1)} %get-tuple-element.37), channel_id=1, source_target_pairs={{0,1},{1,0},{2,3},{3,2},{4,5},{5,4},{6,7},{7,6},{8,9},{9,8},{10,11... | collective-permute-start | bytes 294920 | tf_op jit(solution)/shard_map/ppermute | solution.py:232
  41.3 4.7 %collective-permute-start.13 = (f16[12,2,256]{2,1,0:T(2,128)(2,1)S(1)}, f16[12,2,256]{2,1,0:T(2,128)(2,1)S(1)}, u32[]{:S(2)}, u32[]{:S(2)}) collective-permute-start(f16[12,2,256]{2,1,0:T(2,128)(2,1)S(1)} %get-tuple-element.49), channel_id=1, source_target_pairs={{0,6},{1,7},{2,4},{3,5},{4,2},{5,3},{6,0},{7,1},{8,14},{9,15},{10,... | collective-permute-start | bytes 36872 | tf_op jit(solution)/shard_map/ppermute | solution.py:232
  44.1 3.7 %collective-permute-start.14 = (f16[12,2,256]{2,1,0:T(2,128)(2,1)S(1)}, f16[12,2,256]{2,1,0:T(2,128)(2,1)S(1)}, u32[]{:S(2)}, u32[]{:S(2)}) collective-permute-start(f16[12,2,256]{2,1,0:T(2,128)(2,1)S(1)} %get-tuple-element.51), channel_id=1, source_target_pairs={{0,4},{1,5},{2,6},{3,7},{4,0},{5,1},{6,2},{7,3},{8,12},{9,13},{10,... | collective-permute-start | bytes 36872 | tf_op jit(solution)/shard_map/ppermute | solution.py:232
  44.4 3.7 %collective-permute-start.15 = (f16[12,2,256]{2,1,0:T(2,128)(2,1)S(1)}, f16[12,2,256]{2,1,0:T(2,128)(2,1)S(1)}, u32[]{:S(2)}, u32[]{:S(2)}) collective-permute-start(f16[12,2,256]{2,1,0:T(2,128)(2,1)S(1)} %get-tuple-element.50), channel_id=1, source_target_pairs={{0,2},{1,3},{2,0},{3,1},{4,6},{5,7},{6,4},{7,5},{8,10},{9,11},{10,... | collective-permute-start | bytes 36872 | tf_op jit(solution)/shard_map/ppermute | solution.py:232
  48.2 4.7 %collective-permute-start.16 = (f16[12,1,256]{2,1,0:T(2,128)(2,1)S(1)}, f16[12,1,256]{2,1,0:T(2,128)(2,1)S(1)}, u32[]{:S(2)}, u32[]{:S(2)}) collective-permute-start(f16[12,1,256]{2,1,0:T(2,128)(2,1)S(1)} %fusion.3), channel_id=1, source_target_pairs={{0,8},{1,9},{2,10},{3,11},{4,12},{5,13},{6,14},{7,15},{8,0},{9,1},... | collective-permute-start | bytes 18440 | tf_op jit(solution)/shard_map/ppermute | solution.py:232

commit v6 on v5

--- a/solution.py
+++ b/solution.py
@@ -9,7 +9,7 @@
 
 PATHS_PER = 8
 ITERS = 3
-CHUNKS = 4
+CHUNKS = 3
 VMEM_LIMIT = 20 * 2**20
 F32 = jnp.float32
 BF16 = jnp.bfloat16

time: 53.7 us -> 53.4 us (level)
  no operation moved by 1% of the time
where the time goes in v6:
time: 53.4 us; the launch traced here: 53.3 us
  starting transfers between devices  21.2 us (40%)
  waiting for transfers between devices  17.5 us (33%)
  Pallas kernels  11.3 us (21%)
  between operations  1.46 us (3%)
  other arithmetic  1.03 us (2%)
  local copies, waits for them, and re-layouts  0.76 us (1%)
    ppermute x17, starting transfers between devices, swap(): return lax.ppermute(x, 'comm', [(i, i ^ bit) for i in range(n_dev)])  21.2 us
    ppermute x17, waiting for transfers between devices, swap(): return lax.ppermute(x, 'comm', [(i, i ^ bit) for i in range(n_dev)])  17.5 us
    pallas_call x2, Pallas kernels, per_device(): following(*index, tile_count, capacity, base, flows, rounded, swap(rounde...  4.31 us
    pallas_call x1, Pallas kernels, per_device(): pl.pallas_call(first_kernel, out_shape=(halves, halves, V(tiles.shape, BF...  3.55 us
    pallas_call x3, Pallas kernels, demand_step(): pl.pallas_call(functools.partial(demand_kernel, sweep), out_shape=outs, i...  1.74 us
    pallas_call x1, Pallas kernels, sum_all(): beside, total = turn(beside, total)  1.67 us
  transfers between devices with their start and end apart: 17, of which 16 were waited for; matrix products, arithmetic and copies ran while one was open for 1% of the time, Pallas kernels for 6%

profile of v6, /device:TPU:0, one launch (start us, length us, event | category | flops | bytes accessed | tf_op | source)
XLA Modules:
  0.0 53.3 jit_solution(13586129080129118835)
XLA Ops:
  1.3 3.5 %first_forward.1 = (f32[12,8,256]{2,1,0:T(8,128)S(1)}, f32[12,8,256]{2,1,0:T(8,128)S(1)}, bf16[48,256,256]{2,1,0:T(8,128)(2,1)S(1)}, s32[48]{0:T(128)S(4)}, s32[48]{0:T(128)S(4)}) custom-call(s32[1]{0:T(128)S(6)} %copy.15.count_ref, s32[48]{0:T(128)} %row_hbm.1, s32[48]{0:T(128)} %col_hbm.1, f32[12,1,256]{2,1,0:T(1,128)} %bitcast.27, ...), custom_call_target="tpu_custom_call" | custom-call | flops 100663296 | bytes 6291456 | tf_op jit(solution)/shard_map/first_forward/pallas_call | solution.py:173
  4.9 0.5 collective-permute-start
  5.4 0.9 %collective-permute-done = f32[12,8,256]{2,1,0:T(8,128)S(1)} collective-permute-done((f32[12,8,256]{2,1,0:T(8,128)S(1)}, f32[12,8,256]{2,1,0:T(8,128)S(1)}, u32[]{:S(2)}, u32[]{:S(2)}) %collective-permute-start) | collective-permute-done | bytes 98336 | tf_op jit(solution)/shard_map/ppermute | solution.py:232
  6.3 3.9 %collective-permute-start.1 = (f16[12,8,256]{2,1,0:T(8,128)(2,1)S(1)}, f16[12,8,256]{2,1,0:T(8,128)(2,1)S(1)}, u32[]{:S(2)}, u32[]{:S(2)}) collective-permute-start(f16[12,8,256]{2,1,0:T(8,128)(2,1)S(1)} %get-tuple-element.45), channel_id=1, source_target_pairs={{0,6},{1,7},{2,4},{3,5},{4,2},{5,3},{6,0},{7,1},{8,14},{9,15},{10,... | collective-permute-start | bytes 147464 | tf_op jit(solution)/shard_map/ppermute | solution.py:232
  10.3 0.5 collective-permute-start.2
  10.9 1.7 %transpose_tiles.1 = (bf16[48,256,256]{2,1,0:T(8,128)(2,1)S(1)}, f32[12,8,256]{2,1,0:T(8,128)S(1)}) custom-call(bf16[48,256,256]{2,1,0:T(8,128)(2,1)S(1)} %get-tuple-element.26.tiles_v, f32[12,8,256]{2,1,0:T(8,128)S(1)} %get-tuple-element.46.total_ref), custom_call_target="tpu_custom_call" | custom-call | bytes 12582912 | tf_op jit(solution)/shard_map/transpose_tiles/pallas_call | solution.py:245
  12.6 1.8 %collective-permute-done.2 = f16[12,8,256]{2,1,0:T(8,128)(2,1)S(1)} collective-permute-done((f16[12,8,256]{2,1,0:T(8,128)(2,1)S(1)}, f16[12,8,256]{2,1,0:T(8,128)(2,1)S(1)}, u32[]{:S(2)}, u32[]{:S(2)}) %collective-permute-start.2) | collective-permute-done | bytes 49184 | tf_op jit(solution)/shard_map/ppermute | solution.py:232
  14.9 2.7 %collective-permute-start.4 = (f16[12,8,256]{2,1,0:T(8,128)(2,1)S(1)}, f16[12,8,256]{2,1,0:T(8,128)(2,1)S(1)}, u32[]{:S(2)}, u32[]{:S(2)}) collective-permute-start(f16[12,8,256]{2,1,0:T(8,128)(2,1)S(1)} %get-tuple-element.43), channel_id=1, source_target_pairs={{0,8},{1,9},{2,10},{3,11},{4,12},{5,13},{6,14},{7,15},{8,0},{9,1},... | collective-permute-start | bytes 147464 | tf_op jit(solution)/shard_map/ppermute | solution.py:232
  17.5 2.4 %collective-permute-done.4 = f16[12,8,256]{2,1,0:T(8,128)(2,1)S(1)} collective-permute-done((f16[12,8,256]{2,1,0:T(8,128)(2,1)S(1)}, f16[12,8,256]{2,1,0:T(8,128)(2,1)S(1)}, u32[]{:S(2)}, u32[]{:S(2)}) %collective-permute-start.4) | collective-permute-done | bytes 49184 | tf_op jit(solution)/shard_map/ppermute | solution.py:232
  20.1 0.5 demand_step.3
  20.5 0.7 %collective-permute-done.5.other_ref = bf16[12,8,256]{2,1,0:T(8,128)(2,1)S(1)} collective-permute-done((bf16[12,8,256]{2,1,0:T(8,128)(2,1)S(1)}, bf16[12,8,256]{2,1,0:T(8,128)(2,1)S(1)}, u32[]{:S(2)}, u32[]{:S(2)}) %collective-permute-start.5) | collective-permute-done | bytes 49184 | tf_op jit(solution)/shard_map/ppermute | solution.py:232
  21.3 2.2 %adjoint_forward.2 = (f32[12,8,256]{2,1,0:T(8,128)S(1)}, f32[12,8,256]{2,1,0:T(8,128)S(1)}, f32[12,16,256]{2,1,0:T(8,128)S(1)}) custom-call(s32[48]{0:T(128)S(4)} %get-tuple-element.21.row_ref, s32[48]{0:T(128)S(4)} %get-tuple-element.22.col_ref, s32[1]{0:T(128)S(6)} %copy.15.count_ref, f32[12,1,256]{2,1,0:T(1,128)S(1)} %bitcast.28, ...), custom_call_target="tpu_custom_call" | custom-call | flops 201326592 | bytes 6291456 | tf_op jit(solution)/shard_map/adjoint_forward/pallas_call | solution.py:277
  23.7 1.1 %collective-permute-done.6 = f32[12,8,256]{2,1,0:T(8,128)S(1)} collective-permute-done((f32[12,8,256]{2,1,0:T(8,128)S(1)}, f32[12,8,256]{2,1,0:T(8,128)S(1)}, u32[]{:S(2)}, u32[]{:S(2)}) %collective-permute-start.6) | collective-permute-done | bytes 98336 | tf_op jit(solution)/shard_map/ppermute | solution.py:232
  24.8 1.6 %collective-permute-start.7 = (f16[12,8,256]{2,1,0:T(8,128)(2,1)S(1)}, f16[12,8,256]{2,1,0:T(8,128)(2,1)S(1)}, u32[]{:S(2)}, u32[]{:S(2)}) collective-permute-start(f16[12,8,256]{2,1,0:T(8,128)(2,1)S(1)} %get-tuple-element.41), channel_id=1, source_target_pairs={{0,6},{1,7},{2,4},{3,5},{4,2},{5,3},{6,0},{7,1},{8,14},{9,15},{10,... | collective-permute-start | bytes 147464 | tf_op jit(solution)/shard_map/ppermute | solution.py:232
  26.5 1.8 %collective-permute-start.9 = (f16[12,8,256]{2,1,0:T(8,128)(2,1)S(1)}, f16[12,8,256]{2,1,0:T(8,128)(2,1)S(1)}, u32[]{:S(2)}, u32[]{:S(2)}) collective-permute-start(f16[12,8,256]{2,1,0:T(8,128)(2,1)S(1)} %get-tuple-element.41), channel_id=1, source_target_pairs={{0,2},{1,3},{2,0},{3,1},{4,6},{5,7},{6,4},{7,5},{8,10},{9,11},{10,... | collective-permute-start | bytes 147464 | tf_op jit(solution)/shard_map/ppermute | solution.py:232
  28.4 1.6 %collective-permute-done.7 = f16[12,8,256]{2,1,0:T(8,128)(2,1)S(1)} collective-permute-done((f16[12,8,256]{2,1,0:T(8,128)(2,1)S(1)}, f16[12,8,256]{2,1,0:T(8,128)(2,1)S(1)}, u32[]{:S(2)}, u32[]{:S(2)}) %collective-permute-start.7) | collective-permute-done | bytes 49184 | tf_op jit(solution)/shard_map/ppermute | solution.py:232
  30.0 0.5 collective-permute-done.8
  30.7 3.1 %collective-permute-start.10 = (f16[12,8,256]{2,1,0:T(8,128)(2,1)S(1)}, f16[12,8,256]{2,1,0:T(8,128)(2,1)S(1)}, u32[]{:S(2)}, u32[]{:S(2)}) collective-permute-start(f16[12,8,256]{2,1,0:T(8,128)(2,1)S(1)} %multiply_convert_fusion.1), channel_id=1, source_target_pairs={{0,8},{1,9},{2,10},{3,11},{4,12},{5,13},{6,14},{7,15},{8,0},{9,1},... | collective-permute-start | bytes 147464 | tf_op jit(solution)/shard_map/ppermute | solution.py:232
  33.7 2.3 %collective-permute-done.10 = f16[12,8,256]{2,1,0:T(8,128)(2,1)S(1)} collective-permute-done((f16[12,8,256]{2,1,0:T(8,128)(2,1)S(1)}, f16[12,8,256]{2,1,0:T(8,128)(2,1)S(1)}, u32[]{:S(2)}, u32[]{:S(2)}) %collective-permute-start.10) | collective-permute-done | bytes 49184 | tf_op jit(solution)/shard_map/ppermute | solution.py:232
  36.2 0.5 demand_step.4
  36.6 0.7 %collective-permute-done.11.other_ref = bf16[12,8,256]{2,1,0:T(8,128)(2,1)S(1)} collective-permute-done((bf16[12,8,256]{2,1,0:T(8,128)(2,1)S(1)}, bf16[12,8,256]{2,1,0:T(8,128)(2,1)S(1)}, u32[]{:S(2)}, u32[]{:S(2)}) %collective-permute-start.11) | collective-permute-done | bytes 49184 | tf_op jit(solution)/shard_map/ppermute | solution.py:232
  37.4 2.2 %adjoint_forward.3 = (f32[12,8,256]{2,1,0:T(8,128)S(1)}, f32[12,8,256]{2,1,0:T(8,128)S(1)}, f32[12,16,256]{2,1,0:T(8,128)S(1)}) custom-call(s32[48]{0:T(128)S(4)} %get-tuple-element.21.row_ref, s32[48]{0:T(128)S(4)} %get-tuple-element.22.col_ref, s32[1]{0:T(128)S(6)} %copy.15.count_ref, f32[12,1,256]{2,1,0:T(1,128)S(1)} %bitcast.29, ...), custom_call_target="tpu_custom_call" | custom-call | flops 201326592 | bytes 6291456 | tf_op jit(solution)/shard_map/adjoint_forward/pallas_call | solution.py:277
  39.8 1.1 %collective-permute-done.12 = f32[12,8,256]{2,1,0:T(8,128)S(1)} collective-permute-done((f32[12,8,256]{2,1,0:T(8,128)S(1)}, f32[12,8,256]{2,1,0:T(8,128)S(1)}, u32[]{:S(2)}, u32[]{:S(2)}) %collective-permute-start.12) | collective-permute-done | bytes 98336 | tf_op jit(solution)/shard_map/ppermute | solution.py:232
  41.1 2.7 %collective-permute-start.13 = (f16[12,2,256]{2,1,0:T(2,128)(2,1)S(1)}, f16[12,2,256]{2,1,0:T(2,128)(2,1)S(1)}, u32[]{:S(2)}, u32[]{:S(2)}) collective-permute-start(f16[12,2,256]{2,1,0:T(2,128)(2,1)S(1)} %get-tuple-element.49), channel_id=1, source_target_pairs={{0,6},{1,7},{2,4},{3,5},{4,2},{5,3},{6,0},{7,1},{8,14},{9,15},{10,... | collective-permute-start | bytes 36872 | tf_op jit(solution)/shard_map/ppermute | solution.py:232
  44.2 0.5 collective-permute-start.15
  44.7 1.1 %collective-permute-done.13 = f16[12,2,256]{2,1,0:T(2,128)(2,1)S(1)} collective-permute-done((f16[12,2,256]{2,1,0:T(2,128)(2,1)S(1)}, f16[12,2,256]{2,1,0:T(2,128)(2,1)S(1)}, u32[]{:S(2)}, u32[]{:S(2)}) %collective-permute-start.13) | collective-permute-done | bytes 12320 | tf_op jit(solution)/shard_map/ppermute | solution.py:232
  45.8 1.8 %collective-permute-done.14 = f16[12,2,256]{2,1,0:T(2,128)(2,1)S(1)} collective-permute-done((f16[12,2,256]{2,1,0:T(2,128)(2,1)S(1)}, f16[12,2,256]{2,1,0:T(2,128)(2,1)S(1)}, u32[]{:S(2)}, u32[]{:S(2)}) %collective-permute-start.14) | collective-permute-done | bytes 12320 | tf_op jit(solution)/shard_map/ppermute | solution.py:232
  48.0 2.7 %collective-permute-start.16 = (f16[12,1,256]{2,1,0:T(2,128)(2,1)S(1)}, f16[12,1,256]{2,1,0:T(2,128)(2,1)S(1)}, u32[]{:S(2)}, u32[]{:S(2)}) collective-permute-start(f16[12,1,256]{2,1,0:T(2,128)(2,1)S(1)} %fusion.3), channel_id=1, source_target_pairs={{0,8},{1,9},{2,10},{3,11},{4,12},{5,13},{6,14},{7,15},{8,0},{9,1},... | collective-permute-start | bytes 18440 | tf_op jit(solution)/shard_map/ppermute | solution.py:232
  50.7 0.7 %copy.14 = f32[16,12,256]{2,0,1:T(8,128)} copy(f32[16,12,256]{2,0,1:T(8,128)S(1)} %bitcast.19) | data formatting | bytes 393216
  51.3 0.8 %demand_step.5 = f32[12,16,32]{2,1,0:T(8,128)} custom-call(f32[12,16,256]{2,1,0:T(8,128)S(1)} %bitcast.23, f32[12,16,32]{2,1,0:T(8,128)S(1)} %bitcast.26, f32[12,16,32]{2,1,0:T(8,128)S(1)} %get-tuple-element.38.refs_2_, f32[12,16,256]{2,1,0:T(8,128)S(1)} %get-tuple-element.31.refs_4_.flows_ref.refs_3_, f32[12,16,256]{2,1,0:T(8,128)S(1)} %get-tuple-element.35.refs_4_), custom_call_target="tpu_custom_call" | custom-call | flops 1000000 | bytes 786432 | tf_op jit(solution)/shard_map/demand_step/pallas_call | solution.py:219
  52.1 0.5 collective-permute-done.16
  52.6 0.6 %maximum_bitcast_fusion = f32[1,12,256]{2,0,1:T(1,128)} fusion(f16[12,1,256]{2,1,0:T(2,128)(2,1)S(1)} %collective-permute-done.16, f32[12,2,256]{2,1,0:T(2,128)S(1)} %fusion.2, s32[]{:T(128)S(6)} %select_n.54, f32[12,8,256]{2,1,0:T(8,128)S(1)} %get-tuple-element.40, s32[]{:T(128)S(6)} %select_n.46), kind=kLoop, calls=%fused_computation.15 | loop fusion | flops 18432 | bytes 43016 | tf_op jit(solution)/shard_map/transpose | solution.py:283
  (29 shorter events, 2.7 us)
Async XLA Ops:
  1.3 18.8 %copy-start = (f32[16,12,256]{2,0,1:T(8,128)S(1)}, f32[16,12,256]{2,0,1:T(8,128)}, u32[]{:S(2)}) copy-start(f32[16,12,256]{2,0,1:T(8,128)} %param.7) | copy-start | bytes 589828
  1.3 18.8 %copy-start.1 = (f32[16,12,32]{2,0,1:T(8,128)S(1)}, f32[16,12,32]{2,0,1:T(8,128)}, u32[]{:S(2)}) copy-start(f32[16,12,32]{2,0,1:T(8,128)} %param.8) | copy-start | bytes 73732
  1.3 20.0 %copy-start.2 = (f32[1,12,256]{2,0,1:T(1,128)S(1)}, f32[1,12,256]{2,0,1:T(1,128)}, u32[]{:S(2)}) copy-start(f32[1,12,256]{2,0,1:T(1,128)} %param.9) | copy-start | bytes 36868
  4.9 1.5 %collective-permute-start = (f32[12,8,256]{2,1,0:T(8,128)S(1)}, f32[12,8,256]{2,1,0:T(8,128)S(1)}, u32[]{:S(2)}, u32[]{:S(2)}) collective-permute-start(f32[12,8,256]{2,1,0:T(8,128)S(1)} %get-tuple-element.28), channel_id=1, source_target_pairs={{0,1},{1,0},{2,3},{3,2},{4,5},{5,4},{6,7},{7,6},{8,9},{9,8},{10,11... | collective-permute-start | bytes 294920 | tf_op jit(solution)/shard_map/ppermute | solution.py:232
  6.3 6.3 %collective-permute-start.1 = (f16[12,8,256]{2,1,0:T(8,128)(2,1)S(1)}, f16[12,8,256]{2,1,0:T(8,128)(2,1)S(1)}, u32[]{:S(2)}, u32[]{:S(2)}) collective-permute-start(f16[12,8,256]{2,1,0:T(8,128)(2,1)S(1)} %get-tuple-element.45), channel_id=1, source_target_pairs={{0,6},{1,7},{2,4},{3,5},{4,2},{5,3},{6,0},{7,1},{8,14},{9,15},{10,... | collective-permute-start | bytes 147464 | tf_op jit(solution)/shard_map/ppermute | solution.py:232
  10.3 4.1 %collective-permute-start.2 = (f16[12,8,256]{2,1,0:T(8,128)(2,1)S(1)}, f16[12,8,256]{2,1,0:T(8,128)(2,1)S(1)}, u32[]{:S(2)}, u32[]{:S(2)}) collective-permute-start(f16[12,8,256]{2,1,0:T(8,128)(2,1)S(1)} %get-tuple-element.45), channel_id=1, source_target_pairs={{0,4},{1,5},{2,6},{3,7},{4,0},{5,1},{6,2},{7,3},{8,12},{9,13},{10,... | collective-permute-start | bytes 147464 | tf_op jit(solution)/shard_map/ppermute | solution.py:232
  10.7 4.1 %collective-permute-start.3 = (f16[12,8,256]{2,1,0:T(8,128)(2,1)S(1)}, f16[12,8,256]{2,1,0:T(8,128)(2,1)S(1)}, u32[]{:S(2)}, u32[]{:S(2)}) collective-permute-start(f16[12,8,256]{2,1,0:T(8,128)(2,1)S(1)} %get-tuple-element.45), channel_id=1, source_target_pairs={{0,2},{1,3},{2,0},{3,1},{4,6},{5,7},{6,4},{7,5},{8,10},{9,11},{10,... | collective-permute-start | bytes 147464 | tf_op jit(solution)/shard_map/ppermute | solution.py:232
  14.9 5.1 %collective-permute-start.4 = (f16[12,8,256]{2,1,0:T(8,128)(2,1)S(1)}, f16[12,8,256]{2,1,0:T(8,128)(2,1)S(1)}, u32[]{:S(2)}, u32[]{:S(2)}) collective-permute-start(f16[12,8,256]{2,1,0:T(8,128)(2,1)S(1)} %get-tuple-element.43), channel_id=1, source_target_pairs={{0,8},{1,9},{2,10},{3,11},{4,12},{5,13},{6,14},{7,15},{8,0},{9,1},... | collective-permute-start | bytes 147464 | tf_op jit(solution)/shard_map/ppermute | solution.py:232
  20.0 1.3 %collective-permute-start.5 = (bf16[12,8,256]{2,1,0:T(8,128)(2,1)S(1)}, bf16[12,8,256]{2,1,0:T(8,128)(2,1)S(1)}, u32[]{:S(2)}, u32[]{:S(2)}) collective-permute-start(bf16[12,8,256]{2,1,0:T(8,128)(2,1)S(1)} %fusion.own_ref), channel_id=1, source_target_pairs={{0,1},{1,0},{2,3},{3,2},{4,5},{5,4},{6,7},{7,6},{8,9},{9,8},{10,11... | collective-permute-start | bytes 147464 | tf_op jit(solution)/shard_map/ppermute | solution.py:232
  23.4 1.4 %collective-permute-start.6 = (f32[12,8,256]{2,1,0:T(8,128)S(1)}, f32[12,8,256]{2,1,0:T(8,128)S(1)}, u32[]{:S(2)}, u32[]{:S(2)}) collective-permute-start(f32[12,8,256]{2,1,0:T(8,128)S(1)} %get-tuple-element.34), channel_id=1, source_target_pairs={{0,1},{1,0},{2,3},{3,2},{4,5},{5,4},{6,7},{7,6},{8,9},{9,8},{10,11... | collective-permute-start | bytes 294920 | tf_op jit(solution)/shard_map/ppermute | solution.py:232
  24.8 5.2 %collective-permute-start.7 = (f16[12,8,256]{2,1,0:T(8,128)(2,1)S(1)}, f16[12,8,256]{2,1,0:T(8,128)(2,1)S(1)}, u32[]{:S(2)}, u32[]{:S(2)}) collective-permute-start(f16[12,8,256]{2,1,0:T(8,128)(2,1)S(1)} %get-tuple-element.41), channel_id=1, source_target_pairs={{0,6},{1,7},{2,4},{3,5},{4,2},{5,3},{6,0},{7,1},{8,14},{9,15},{10,... | collective-permute-start | bytes 147464 | tf_op jit(solution)/shard_map/ppermute | solution.py:232
  26.4 4.1 %collective-permute-start.8 = (f16[12,8,256]{2,1,0:T(8,128)(2,1)S(1)}, f16[12,8,256]{2,1,0:T(8,128)(2,1)S(1)}, u32[]{:S(2)}, u32[]{:S(2)}) collective-permute-start(f16[12,8,256]{2,1,0:T(8,128)(2,1)S(1)} %get-tuple-element.41), channel_id=1, source_target_pairs={{0,4},{1,5},{2,6},{3,7},{4,0},{5,1},{6,2},{7,3},{8,12},{9,13},{10,... | collective-permute-start | bytes 147464 | tf_op jit(solution)/shard_map/ppermute | solution.py:232
  26.5 4.1 %collective-permute-start.9 = (f16[12,8,256]{2,1,0:T(8,128)(2,1)S(1)}, f16[12,8,256]{2,1,0:T(8,128)(2,1)S(1)}, u32[]{:S(2)}, u32[]{:S(2)}) collective-permute-start(f16[12,8,256]{2,1,0:T(8,128)(2,1)S(1)} %get-tuple-element.41), channel_id=1, source_target_pairs={{0,2},{1,3},{2,0},{3,1},{4,6},{5,7},{6,4},{7,5},{8,10},{9,11},{10,... | collective-permute-start | bytes 147464 | tf_op jit(solution)/shard_map/ppermute | solution.py:232
  30.7 5.3 %collective-permute-start.10 = (f16[12,8,256]{2,1,0:T(8,128)(2,1)S(1)}, f16[12,8,256]{2,1,0:T(8,128)(2,1)S(1)}, u32[]{:S(2)}, u32[]{:S(2)}) collective-permute-start(f16[12,8,256]{2,1,0:T(8,128)(2,1)S(1)} %multiply_convert_fusion.1), channel_id=1, source_target_pairs={{0,8},{1,9},{2,10},{3,11},{4,12},{5,13},{6,14},{7,15},{8,0},{9,1},... | collective-permute-start | bytes 147464 | tf_op jit(solution)/shard_map/ppermute | solution.py:232
  36.1 1.3 %collective-permute-start.11 = (bf16[12,8,256]{2,1,0:T(8,128)(2,1)S(1)}, bf16[12,8,256]{2,1,0:T(8,128)(2,1)S(1)}, u32[]{:S(2)}, u32[]{:S(2)}) collective-permute-start(bf16[12,8,256]{2,1,0:T(8,128)(2,1)S(1)} %get-tuple-element.39.own_ref), channel_id=1, source_target_pairs={{0,1},{1,0},{2,3},{3,2},{4,5},{5,4},{6,7},{7,6},{8,9},{9,8},{10,11... | collective-permute-start | bytes 147464 | tf_op jit(solution)/shard_map/ppermute | solution.py:232
  39.5 1.4 %collective-permute-start.12 = (f32[12,8,256]{2,1,0:T(8,128)S(1)}, f32[12,8,256]{2,1,0:T(8,128)S(1)}, u32[]{:S(2)}, u32[]{:S(2)}) collective-permute-start(f32[12,8,256]{2,1,0:T(8,128)S(1)} %get-tuple-element.37), channel_id=1, source_target_pairs={{0,1},{1,0},{2,3},{3,2},{4,5},{5,4},{6,7},{7,6},{8,9},{9,8},{10,11... | collective-permute-start | bytes 294920 | tf_op jit(solution)/shard_map/ppermute | solution.py:232
  41.1 4.7 %collective-permute-start.13 = (f16[12,2,256]{2,1,0:T(2,128)(2,1)S(1)}, f16[12,2,256]{2,1,0:T(2,128)(2,1)S(1)}, u32[]{:S(2)}, u32[]{:S(2)}) collective-permute-start(f16[12,2,256]{2,1,0:T(2,128)(2,1)S(1)} %get-tuple-element.49), channel_id=1, source_target_pairs={{0,6},{1,7},{2,4},{3,5},{4,2},{5,3},{6,0},{7,1},{8,14},{9,15},{10,... | collective-permute-start | bytes 36872 | tf_op jit(solution)/shard_map/ppermute | solution.py:232
  43.8 3.7 %collective-permute-start.14 = (f16[12,2,256]{2,1,0:T(2,128)(2,1)S(1)}, f16[12,2,256]{2,1,0:T(2,128)(2,1)S(1)}, u32[]{:S(2)}, u32[]{:S(2)}) collective-permute-start(f16[12,2,256]{2,1,0:T(2,128)(2,1)S(1)} %get-tuple-element.51), channel_id=1, source_target_pairs={{0,4},{1,5},{2,6},{3,7},{4,0},{5,1},{6,2},{7,3},{8,12},{9,13},{10,... | collective-permute-start | bytes 36872 | tf_op jit(solution)/shard_map/ppermute | solution.py:232
  44.2 3.7 %collective-permute-start.15 = (f16[12,2,256]{2,1,0:T(2,128)(2,1)S(1)}, f16[12,2,256]{2,1,0:T(2,128)(2,1)S(1)}, u32[]{:S(2)}, u32[]{:S(2)}) collective-permute-start(f16[12,2,256]{2,1,0:T(2,128)(2,1)S(1)} %get-tuple-element.50), channel_id=1, source_target_pairs={{0,2},{1,3},{2,0},{3,1},{4,6},{5,7},{6,4},{7,5},{8,10},{9,11},{10,... | collective-permute-start | bytes 36872 | tf_op jit(solution)/shard_map/ppermute | solution.py:232
  48.0 4.7 %collective-permute-start.16 = (f16[12,1,256]{2,1,0:T(2,128)(2,1)S(1)}, f16[12,1,256]{2,1,0:T(2,128)(2,1)S(1)}, u32[]{:S(2)}, u32[]{:S(2)}) collective-permute-start(f16[12,1,256]{2,1,0:T(2,128)(2,1)S(1)} %fusion.3), channel_id=1, source_target_pairs={{0,8},{1,9},{2,10},{3,11},{4,12},{5,13},{6,14},{7,15},{8,0},{9,1},... | collective-permute-start | bytes 18440 | tf_op jit(solution)/shard_map/ppermute | solution.py:232
